TPU v7x, 32 devices: a whole 2x2x4 slice. The times are simulated.
32 devices in a mesh: energy: 2 (over x), chain: 16 (over z, y, core).
Axes of the slice: x: 2, y: 2, z: 4, core: 2. Of those that a mesh axis runs over, the one named last changes fastest.
Arguments:
- lower: bfloat16 [32, 2, 256, 256], P(('energy', 'chain')), parts along dimension 0, may hold values from -0.125 to 0.125
- upper: bfloat16 [32, 2, 256, 256], P(('energy', 'chain')), parts along dimension 0, may hold values from -0.125 to 0.125
- right_side: bfloat16 [32, 2, 256, 256], P(('energy', 'chain')), parts along dimension 0, may hold values from -6 to 6
Outputs:
- reduced_rhs: bfloat16 [32, 2, 256, 256], P(('energy', 'chain')), parts along dimension 0
There are 2 independent parts, one for each index of `energy`. A program takes and returns all parts, laid end to end along the dimension named above; each array names one. Nothing has to cross between parts.
All inputs are finite; a program needn't handle non-finite values.
Results may differ from a plain program's by a relative error of at most 0.011.
Values may be sent and summed in bfloat16 or wider, within the bound.
No kernel may reach another device: no remote copies, remote signals or barrier semaphores. Data moves between devices by JAX's collectives and lax.ppermute only.
A program may use at most 64 MiB of HBM per device.

v0:
```python
import jax
import jax.numpy as jnp
from jax import lax
from jax.sharding import PartitionSpec as P

SECTIONS = 3
NS_STEPS = 2


def passed_along(shard, axis, by):
    length = lax.axis_size(axis)
    pairs = [(i, i + by) for i in range(length) if 0 <= i + by < length]
    return lax.ppermute(shard, axis, pairs)


def complex_product(left_block, right_block):
    real_part = jnp.dot(
        left_block[0], right_block[0], preferred_element_type=jnp.float32
    ) - jnp.dot(left_block[1], right_block[1], preferred_element_type=jnp.float32)
    imag_part = jnp.dot(
        left_block[0], right_block[1], preferred_element_type=jnp.float32
    ) + jnp.dot(left_block[1], right_block[0], preferred_element_type=jnp.float32)
    return jnp.stack([real_part, imag_part])


def approx_inverse(diagonal_new, identity_block):
    diagonal_low = diagonal_new.astype(jnp.bfloat16)
    approx = (2.0 * identity_block - diagonal_new).astype(jnp.bfloat16)
    for repeat in range(NS_STEPS):
        correction = (2.0 * identity_block - complex_product(diagonal_low, approx)).astype(
            jnp.bfloat16
        )
        approx = complex_product(approx, correction).astype(jnp.bfloat16)
    return approx


def exchange_rows(send_upward, send_downward, reach):
    below = passed_along(send_upward, "chain", reach)[0]
    above = passed_along(send_downward, "chain", -reach)[0]
    return (below, above)


def local(lower, upper, right_side):
    order = lower.shape[2]
    lower_block = lower[0]
    upper_block = upper[0]
    current = right_side[0]
    unit_matrix = jnp.eye(order, dtype=jnp.float32)
    identity_block = jnp.stack([unit_matrix, jnp.zeros_like(unit_matrix)])
    for number in range(SECTIONS):
        reach = 2**number
        final = number == SECTIONS - 1
        if final:
            send_upward = jnp.concatenate([upper_block, current], axis=-1)[None]
            send_downward = jnp.concatenate([lower_block, current], axis=-1)[None]
            below, above = exchange_rows(send_upward, send_downward, reach)
            below_upper = below[:, :, :order]
            below_rhs = below[:, :, order:]
            above_lower = above[:, :, :order]
            above_rhs = above[:, :, order:]
        else:
            packed = jnp.concatenate([lower_block, upper_block, current], axis=-1)[None]
            below, above = exchange_rows(packed, packed, reach)
            below_lower = below[:, :, :order]
            below_upper = below[:, :, order : 2 * order]
            below_rhs = below[:, :, 2 * order :]
            above_lower = above[:, :, :order]
            above_upper = above[:, :, order : 2 * order]
            above_rhs = above[:, :, 2 * order :]
        diagonal_new = (
            identity_block
            - complex_product(lower_block, below_upper)
            - complex_product(upper_block, above_lower)
        )
        inverse = approx_inverse(diagonal_new, identity_block)
        rhs_new = (
            current
            - complex_product(lower_block, below_rhs)
            - complex_product(upper_block, above_rhs)
        ).astype(jnp.bfloat16)
        if not final:
            lower_raw = (-complex_product(lower_block, below_lower)).astype(jnp.bfloat16)
            upper_raw = (-complex_product(upper_block, above_upper)).astype(jnp.bfloat16)
            lower_block = complex_product(inverse, lower_raw).astype(jnp.bfloat16)
            upper_block = complex_product(inverse, upper_raw).astype(jnp.bfloat16)
        current = complex_product(inverse, rhs_new).astype(jnp.bfloat16)
    return current[None]


def solution(mesh):
    placed = (
        P(("energy", "chain"), None, None, None),
        P(("energy", "chain"), None, None, None),
        P(("energy", "chain"), None, None, None),
    )
    return jax.shard_map(
        local,
        mesh=mesh,
        in_specs=placed,
        out_specs=P(("energy", "chain"), None, None, None),
        check_vma=False,
    )
```

profile of v0, /device:TPU:0, one launch (start us, length us, event | category | flops | bytes accessed | tf_op | source)
XLA Modules:
  0.0 114.5 jit_solution(17838638921217624509)
XLA Ops:
  0.0 1.1 copy.6
  1.1 1.1 copy.4
  2.4 1.3 %collective-permute-start.1 = (bf16[1,2,256,768]{2,3,1,0:T(8,128)(2,1)S(1)}, bf16[1,2,256,768]{2,3,1,0:T(8,128)(2,1)S(1)}, u32[]{:S(2)}, u32[]{:S(2)}) collective-permute-start(bf16[1,2,256,768]{2,3,1,0:T(8,128)(2,1)S(1)} %maximum_bitcast_fusion), channel_id=1, source_target_pairs={{1,0},{2,1},{3,2},{4,3},{5,4},{6,5},{7,6},{8,7},{9,8},{10,9},{11,1... | collective-permute-start | bytes 2359304 | tf_op jit(solution)/shard_map/ppermute | solution.py:13
  3.7 3.1 %collective-permute-start = (bf16[1,2,256,768]{2,3,1,0:T(8,128)(2,1)S(1)}, bf16[1,2,256,768]{2,3,1,0:T(8,128)(2,1)S(1)}, u32[]{:S(2)}, u32[]{:S(2)}) collective-permute-start(bf16[1,2,256,768]{2,3,1,0:T(8,128)(2,1)S(1)} %maximum_bitcast_fusion), channel_id=1, source_target_pairs={{0,1},{1,2},{2,3},{3,4},{4,5},{5,6},{6,7},{7,8},{8,9},{9,10},{10,1... | collective-permute-start | bytes 2359304 | tf_op jit(solution)/shard_map/ppermute | solution.py:13
  8.2 0.5 collective-permute-done
  10.2 0.2 fusion.41
  12.1 0.2 fusion.134
  12.3 0.2 fusion.45
  12.6 0.2 fusion.181
  12.8 0.2 fusion.44
  13.0 0.2 fusion.182
  13.2 0.2 fusion.38
  13.5 0.2 fusion.39
  14.2 0.2 fusion.30
  14.5 0.2 fusion.31
  14.9 0.2 fusion.33
  15.9 0.2 fusion.34
  16.2 0.2 fusion.35
  17.1 0.2 fusion.37
  17.8 0.2 fusion.47
  18.1 0.2 fusion.74
  18.5 0.2 fusion.51
  18.7 0.2 fusion.50
  19.0 0.2 fusion.49
  19.2 0.2 fusion.48
  19.5 1.3 %collective-permute-start.3 = (bf16[1,2,256,768]{2,3,1,0:T(8,128)(2,1)S(1)}, bf16[1,2,256,768]{2,3,1,0:T(8,128)(2,1)S(1)}, u32[]{:S(2)}, u32[]{:S(2)}) collective-permute-start(bf16[1,2,256,768]{2,3,1,0:T(8,128)(2,1)S(1)} %maximum_bitcast_fusion.1), channel_id=1, source_target_pairs={{2,0},{3,1},{4,2},{5,3},{6,4},{7,5},{8,6},{9,7},{10,8},{11,9},{12,... | collective-permute-start | bytes 2359304 | tf_op jit(solution)/shard_map/ppermute | solution.py:13
  20.8 22.0 %collective-permute-start.2 = (bf16[1,2,256,768]{2,3,1,0:T(8,128)(2,1)S(1)}, bf16[1,2,256,768]{2,3,1,0:T(8,128)(2,1)S(1)}, u32[]{:S(2)}, u32[]{:S(2)}) collective-permute-start(bf16[1,2,256,768]{2,3,1,0:T(8,128)(2,1)S(1)} %maximum_bitcast_fusion.1), channel_id=1, source_target_pairs={{0,2},{1,3},{2,4},{3,5},{4,6},{5,7},{6,8},{7,9},{8,10},{9,11},{10,... | collective-permute-start | bytes 2359304 | tf_op jit(solution)/shard_map/ppermute | solution.py:13
  42.8 15.1 %collective-permute-done.3 = bf16[1,2,256,768]{2,3,1,0:T(8,128)(2,1)S(1)} collective-permute-done((bf16[1,2,256,768]{2,3,1,0:T(8,128)(2,1)S(1)}, bf16[1,2,256,768]{2,3,1,0:T(8,128)(2,1)S(1)}, u32[]{:S(2)}, u32[]{:S(2)}) %collective-permute-start.3) | collective-permute-done | bytes 786464 | tf_op jit(solution)/shard_map/ppermute | solution.py:13
  59.1 15.9 %collective-permute-done.2 = bf16[1,2,256,768]{2,3,1,0:T(8,128)(2,1)S(1)} collective-permute-done((bf16[1,2,256,768]{2,3,1,0:T(8,128)(2,1)S(1)}, bf16[1,2,256,768]{2,3,1,0:T(8,128)(2,1)S(1)}, u32[]{:S(2)}, u32[]{:S(2)}) %collective-permute-start.2) | collective-permute-done | bytes 786464 | tf_op jit(solution)/shard_map/ppermute | solution.py:13
  78.1 0.2 fusion.148
  78.4 0.2 fusion.55
  78.6 0.2 fusion.185
  78.8 0.2 fusion.54
  79.1 0.2 fusion.186
  79.3 0.2 fusion.28
  79.5 0.2 fusion.29
  81.8 0.2 fusion.24
  82.1 0.2 fusion.25
  82.3 0.2 fusion.155
  82.6 0.2 fusion.154
  82.8 0.2 fusion.26
  83.0 0.2 fusion.27
  83.3 0.2 fusion.166
  83.5 0.2 fusion.165
  83.8 0.2 fusion.57
  84.0 0.2 fusion.63
  84.2 0.2 fusion.72
  84.7 0.2 fusion.60
  84.9 0.2 fusion.59
  85.2 0.2 fusion.58
  85.5 5.7 %collective-permute-start.4 = (bf16[1,2,256,512]{2,3,1,0:T(8,128)(2,1)S(1)}, bf16[1,2,256,512]{2,3,1,0:T(8,128)(2,1)S(1)}, u32[]{:S(2)}, u32[]{:S(2)}) collective-permute-start(bf16[1,2,256,512]{2,3,1,0:T(8,128)(2,1)S(1)} %get-tuple-element.11), channel_id=1, source_target_pairs={{0,4},{1,5},{2,6},{3,7},{4,8},{5,9},{6,10},{7,11},{8,12},{9,13},{1... | collective-permute-start | bytes 1572872 | tf_op jit(solution)/shard_map/ppermute | solution.py:13
  91.1 1.5 %collective-permute-start.5 = (bf16[1,2,256,512]{2,3,1,0:T(8,128)(2,1)S(1)}, bf16[1,2,256,512]{2,3,1,0:T(8,128)(2,1)S(1)}, u32[]{:S(2)}, u32[]{:S(2)}) collective-permute-start(bf16[1,2,256,512]{2,3,1,0:T(8,128)(2,1)S(1)} %get-tuple-element.12), channel_id=1, source_target_pairs={{4,0},{5,1},{6,2},{7,3},{8,4},{9,5},{10,6},{11,7},{12,8},{13,9},{1... | collective-permute-start | bytes 1572872 | tf_op jit(solution)/shard_map/ppermute | solution.py:13
  92.6 9.9 %collective-permute-done.4 = bf16[1,2,256,512]{2,3,1,0:T(8,128)(2,1)S(1)} collective-permute-done((bf16[1,2,256,512]{2,3,1,0:T(8,128)(2,1)S(1)}, bf16[1,2,256,512]{2,3,1,0:T(8,128)(2,1)S(1)}, u32[]{:S(2)}, u32[]{:S(2)}) %collective-permute-start.4) | collective-permute-done | bytes 524320 | tf_op jit(solution)/shard_map/ppermute | solution.py:13
  103.3 3.4 %collective-permute-done.5 = bf16[1,2,256,512]{2,3,1,0:T(8,128)(2,1)S(1)} collective-permute-done((bf16[1,2,256,512]{2,3,1,0:T(8,128)(2,1)S(1)}, bf16[1,2,256,512]{2,3,1,0:T(8,128)(2,1)S(1)}, u32[]{:S(2)}, u32[]{:S(2)}) %collective-permute-start.5) | collective-permute-done | bytes 524320 | tf_op jit(solution)/shard_map/ppermute | solution.py:13
  109.6 0.2 fusion.65
  109.9 0.2 fusion.189
  110.1 0.2 fusion.64
  110.3 0.2 fusion.190
  110.6 0.2 fusion.22
  110.8 0.2 fusion.23
  113.1 0.2 fusion.67
  113.3 0.2 fusion.70
  113.6 0.2 fusion.71
  113.8 0.7 pad_maximum_fusion.1
  (116 shorter events, 19.6 us)
Async XLA Ops:
  0.0 2.2 %copy-start = (bf16[1,2,256,256]{3,2,1,0:T(8,128)(2,1)S(1)}, bf16[1,2,256,256]{3,2,1,0:T(8,128)(2,1)}, u32[]{:S(2)}) copy-start(bf16[1,2,256,256]{3,2,1,0:T(8,128)(2,1)} %param.4) | copy-start | bytes 786436
  2.4 4.4 %collective-permute-start.1 = (bf16[1,2,256,768]{2,3,1,0:T(8,128)(2,1)S(1)}, bf16[1,2,256,768]{2,3,1,0:T(8,128)(2,1)S(1)}, u32[]{:S(2)}, u32[]{:S(2)}) collective-permute-start(bf16[1,2,256,768]{2,3,1,0:T(8,128)(2,1)S(1)} %maximum_bitcast_fusion), channel_id=1, source_target_pairs={{1,0},{2,1},{3,2},{4,3},{5,4},{6,5},{7,6},{8,7},{9,8},{10,9},{11,1... | collective-permute-start | bytes 2359304 | tf_op jit(solution)/shard_map/ppermute | solution.py:13
  3.7 4.9 %collective-permute-start = (bf16[1,2,256,768]{2,3,1,0:T(8,128)(2,1)S(1)}, bf16[1,2,256,768]{2,3,1,0:T(8,128)(2,1)S(1)}, u32[]{:S(2)}, u32[]{:S(2)}) collective-permute-start(bf16[1,2,256,768]{2,3,1,0:T(8,128)(2,1)S(1)} %maximum_bitcast_fusion), channel_id=1, source_target_pairs={{0,1},{1,2},{2,3},{3,4},{4,5},{5,6},{6,7},{7,8},{8,9},{9,10},{10,1... | collective-permute-start | bytes 2359304 | tf_op jit(solution)/shard_map/ppermute | solution.py:13
  7.5 1.1 copy-start.1
  19.5 38.4 %collective-permute-start.3 = (bf16[1,2,256,768]{2,3,1,0:T(8,128)(2,1)S(1)}, bf16[1,2,256,768]{2,3,1,0:T(8,128)(2,1)S(1)}, u32[]{:S(2)}, u32[]{:S(2)}) collective-permute-start(bf16[1,2,256,768]{2,3,1,0:T(8,128)(2,1)S(1)} %maximum_bitcast_fusion.1), channel_id=1, source_target_pairs={{2,0},{3,1},{4,2},{5,3},{6,4},{7,5},{8,6},{9,7},{10,8},{11,9},{12,... | collective-permute-start | bytes 2359304 | tf_op jit(solution)/shard_map/ppermute | solution.py:13
  20.8 54.2 %collective-permute-start.2 = (bf16[1,2,256,768]{2,3,1,0:T(8,128)(2,1)S(1)}, bf16[1,2,256,768]{2,3,1,0:T(8,128)(2,1)S(1)}, u32[]{:S(2)}, u32[]{:S(2)}) collective-permute-start(bf16[1,2,256,768]{2,3,1,0:T(8,128)(2,1)S(1)} %maximum_bitcast_fusion.1), channel_id=1, source_target_pairs={{0,2},{1,3},{2,4},{3,5},{4,6},{5,7},{6,8},{7,9},{8,10},{9,11},{10,... | collective-permute-start | bytes 2359304 | tf_op jit(solution)/shard_map/ppermute | solution.py:13
  85.5 17.1 %collective-permute-start.4 = (bf16[1,2,256,512]{2,3,1,0:T(8,128)(2,1)S(1)}, bf16[1,2,256,512]{2,3,1,0:T(8,128)(2,1)S(1)}, u32[]{:S(2)}, u32[]{:S(2)}) collective-permute-start(bf16[1,2,256,512]{2,3,1,0:T(8,128)(2,1)S(1)} %get-tuple-element.11), channel_id=1, source_target_pairs={{0,4},{1,5},{2,6},{3,7},{4,8},{5,9},{6,10},{7,11},{8,12},{9,13},{1... | collective-permute-start | bytes 1572872 | tf_op jit(solution)/shard_map/ppermute | solution.py:13
  91.1 15.6 %collective-permute-start.5 = (bf16[1,2,256,512]{2,3,1,0:T(8,128)(2,1)S(1)}, bf16[1,2,256,512]{2,3,1,0:T(8,128)(2,1)S(1)}, u32[]{:S(2)}, u32[]{:S(2)}) collective-permute-start(bf16[1,2,256,512]{2,3,1,0:T(8,128)(2,1)S(1)} %get-tuple-element.12), channel_id=1, source_target_pairs={{4,0},{5,1},{6,2},{7,3},{8,4},{9,5},{10,6},{11,7},{12,8},{13,9},{1... | collective-permute-start | bytes 1572872 | tf_op jit(solution)/shard_map/ppermute | solution.py:13
where the time goes:
time: 115 us
  waiting for transfers between devices  44.8 us (39%)
  starting transfers between devices  34.8 us (30%)
  matrix products  29.3 us (25%)
  local copies, waits for them, and re-layouts  2.35 us (2%)
  other arithmetic  2.09 us (2%)
  between operations  1.22 us (1%)
    ppermute x6, waiting for transfers between devices, passed_along(): return lax.ppermute(shard, axis, pairs)  44.8 us
    ppermute x6, starting transfers between devices, passed_along(): return lax.ppermute(shard, axis, pairs)  34.8 us
    dot_general x35, matrix products, complex_product(): jnp.dot(left_block[1], right_block[0], preferred_element_type=jnp.float32)  7.33 us
    dot_general x35, matrix products, complex_product(): jnp.dot(left_block[0], right_block[0], preferred_element_type=jnp.float32)  7.33 us
    dot_general x35, matrix products, complex_product(): jnp.dot(left_block[1], right_block[1], preferred_element_type=jnp.float32)  7.33 us
    dot_general x35, matrix products, complex_product(): jnp.dot(left_block[0], right_block[1], preferred_element_type=jnp.float32)  7.32 us
    unnamed x7, local copies, waits for them, and re-layouts  2.35 us
  transfers between devices with their start and end apart: 6, of which 5 were waited for; matrix products, arithmetic and copies ran while one was open for 3% of the time, Pallas kernels for 0%

commit v1 on v0

v1 whole, which is shorter than its diff:
```python
import functools

import jax
import jax.numpy as jnp
from jax import lax
from jax.experimental import pallas as pl
from jax.experimental.pallas import tpu as pltpu
from jax.sharding import PartitionSpec as P

SECTIONS = 3
GROUP = 4
LOW, UPP = 0, 1


def wide(block):
    real, imag = block[0], block[1]
    return jnp.concatenate(
        [jnp.concatenate([real, -imag], axis=1), jnp.concatenate([imag, real], axis=1)], axis=0
    )


def tall(block):
    return block.reshape(block.shape[0] * block.shape[1], block.shape[2])


def product(left, right):
    return jnp.dot(left, right, preferred_element_type=jnp.float32)


def low(value):
    return value.astype(jnp.bfloat16)


def parts(stacked, order):
    return stacked.reshape(2, order, stacked.shape[-1])


def inverse_less_one(coupling, order):
    first = low(coupling)
    first_wide = wide(parts(first, order))
    second = product(first_wide, first)
    second_low = low(second)
    pair = product(wide(parts(second_low, order)), jnp.concatenate([second_low, first], axis=1))
    fourth = low(pair[:, :order])
    short = coupling + second + pair[:, order:]
    whole = short + fourth.astype(jnp.float32) + product(
        wide(parts(low(short), order)), fourth
    )
    return low(whole)


def couplings_kernel(flags, own_a, own_b, near, far_a, far_b, new, spread, own_out):
    order = near.shape[2]
    side = flags[0]
    middle = flags[1]

    @pl.when(middle == 1)
    def _():
        own_out[...] = own_b[...]

    @pl.when(middle == 0)
    def _():
        own_out[...] = own_a[...]

    near_lead = wide(own_out[side])
    far_lead = wide(own_out[1 - side])
    far_cross = jnp.where(middle == 1, far_a[side], far_b[side])
    far_same = jnp.where(middle == 1, far_a[1 - side], far_b[1 - side])
    coupling = product(near_lead, tall(near[1 - side])) + product(far_lead, tall(far_cross))
    spread_low = inverse_less_one(coupling, order)
    spread[...] = parts(spread_low, order)
    spread_wide = wide(parts(spread_low, order))
    for place, lead, same in ((side, near_lead, near[side]), (1 - side, far_lead, far_same)):
        raw = -product(lead, tall(same))
        new[place] = parts(low(raw + product(spread_wide, low(raw))), order)


def injections_kernel(flags, own_lu, spread, own_a, own_b, near, far_a, far_b, new):
    order = near.shape[1]
    side = flags[0]
    middle = flags[1]
    own = tall(jnp.where(middle == 1, own_b[...], own_a[...]))
    far = tall(jnp.where(middle == 1, far_a[...], far_b[...]))
    raw = (
        own.astype(jnp.float32)
        - product(wide(own_lu[side]), tall(near[...]))
        - product(wide(own_lu[1 - side]), far)
    )
    new[...] = parts(low(raw + product(wide(spread[...]), low(raw))), order)


def later_couplings_kernel(own, below, above, new, spread):
    order = own.shape[2]
    lower_wide = wide(own[LOW])
    upper_wide = wide(own[UPP])
    coupling = product(lower_wide, tall(below[UPP])) + product(upper_wide, tall(above[LOW]))
    spread_low = inverse_less_one(coupling, order)
    spread[...] = parts(spread_low, order)
    spread_wide = wide(parts(spread_low, order))
    for place, lead, same in ((LOW, lower_wide, below), (UPP, upper_wide, above)):
        raw = -product(lead, tall(same[place]))
        new[place] = parts(low(raw + product(spread_wide, low(raw))), order)


def last_couplings_kernel(own, below_upper, above_lower, spread):
    order = own.shape[2]
    coupling = product(wide(own[LOW]), tall(below_upper[...])) + product(
        wide(own[UPP]), tall(above_lower[...])
    )
    spread[...] = parts(inverse_less_one(coupling, order), order)


def later_injections_kernel(own_lu, spread, own, below, above, new):
    order = own.shape[1]
    raw = (
        tall(own[...]).astype(jnp.float32)
        - product(wide(own_lu[LOW]), tall(below[...]))
        - product(wide(own_lu[UPP]), tall(above[...]))
    )
    new[...] = parts(low(raw + product(wide(spread[...]), low(raw))), order)


def run(kernel, products, outs, *operands, scalars=0):
    order = operands[-1].shape[-1]
    count = len(operands)
    bytes_in = sum(o.size * o.dtype.itemsize for o in operands)
    return pl.pallas_call(
        kernel,
        out_shape=[jax.ShapeDtypeStruct(s, jnp.bfloat16) for s in outs],
        in_specs=[pl.BlockSpec(memory_space=pltpu.SMEM)] * scalars
        + [pl.BlockSpec(memory_space=pltpu.VMEM)] * (count - scalars),
        out_specs=[pl.BlockSpec(memory_space=pltpu.VMEM)] * len(outs),
        compiler_params=pltpu.CompilerParams(vmem_limit_bytes=24 * 1024 * 1024),
        cost_estimate=pl.CostEstimate(
            flops=products * 8 * order**3, bytes_accessed=bytes_in, transcendentals=0
        ),
    )(*operands)


def local(length, lower, upper, right_side):
    order = lower.shape[2]
    block = (2, order, order)
    pair = (2,) + block
    place = lax.axis_index("chain")
    spot = place % GROUP
    side = jnp.where(spot < GROUP // 2, UPP, LOW)
    middle = jnp.where((spot == 1) | (spot == 2), 1, 0)
    flags = jnp.stack([side, middle]).astype(jnp.int32)

    groups = [g for g in range(0, length, GROUP)]

    def move(value, pairs):
        kept = [(a, b) for a, b in pairs if 0 <= a < length and 0 <= b < length]
        return lax.ppermute(value, "chain", kept)

    around = [(g + a, g + b) for g in groups for a, b in ((0, 2), (1, 0), (2, 3), (3, 1))]
    swapped = [(g + a, g + b) for g in groups for a, b in ((1, 2), (2, 1))]
    onward = [(g + a, g + b) for g in groups for a, b in ((1, GROUP), (2, 3 - GROUP))]
    two_up = [
        (g + a, g + b) for g in groups for a, b in ((0, 1), (1, GROUP), (2, 3), (3, GROUP + 2))
    ]
    two_down = [(b, a) for a, b in two_up]
    four_up = [(i, i + GROUP) for i in range(length)]
    four_down = [(b, a) for a, b in four_up]

    couplings = jnp.concatenate([lower, upper], axis=0)
    rhs = right_side[0]

    near = move(couplings, around)
    mine = move(couplings, swapped)
    near_rhs = move(rhs, around)
    mine_rhs = move(rhs, swapped)
    far = move(near, onward)
    far_rhs = move(near_rhs, onward)
    held, spread, own = run(
        couplings_kernel, 10, (pair, block, pair), flags, couplings, mine, near, couplings, far,
        scalars=1,
    )
    (current,) = run(
        injections_kernel, 3, (block,), flags, own, spread, rhs, mine_rhs, near_rhs, rhs, far_rhs,
        scalars=1,
    )

    below, above = move(held, two_up), move(held, two_down)
    below_rhs, above_rhs = move(current, two_up), move(current, two_down)
    next_held, spread = run(later_couplings_kernel, 10, (pair, block), held, below, above)
    (current,) = run(
        later_injections_kernel, 3, (block,), held, spread, current, below_rhs, above_rhs
    )
    held = next_held

    below_upper, above_lower = move(held[UPP], four_up), move(held[LOW], four_down)
    below_rhs, above_rhs = move(current, four_up), move(current, four_down)
    (spread,) = run(last_couplings_kernel, 6, (block,), held, below_upper, above_lower)
    (current,) = run(
        later_injections_kernel, 3, (block,), held, spread, current, below_rhs, above_rhs
    )
    returned = move(current, swapped)
    return jnp.where(middle == 1, returned, current)[None]


def solution(mesh):
    placed = P(("energy", "chain"), None, None, None)
    return jax.shard_map(
        functools.partial(local, mesh.shape["chain"]),
        mesh=mesh,
        in_specs=(placed,) * 3,
        out_specs=placed,
        check_vma=False,
    )
```

time: 115 us -> 80.5 us (0.70)
  the two profiles are of different devices: /device:TPU:0 before, /device:TPU:1 now
where the time goes in v1:
time: 80.5 us; the launch traced here: 80.1 us
  starting transfers between devices  42.8 us (53%)
  waiting for transfers between devices  25.2 us (31%)
  Pallas kernels  9.89 us (12%)
  local copies, waits for them, and re-layouts  1.08 us (1%)
  other arithmetic  0.81 us (1%)
    ppermute x15, starting transfers between devices, move(): return lax.ppermute(value, 'chain', kept)  42.8 us
    ppermute x15, waiting for transfers between devices, move(): return lax.ppermute(value, 'chain', kept)  25.2 us
    pallas_call x6, Pallas kernels, run(): pl.pallas_call(kernel, out_shape=[jax.ShapeDtypeStruct(s, jnp.bfloat16) f...  9.89 us
  transfers between devices with their start and end apart: 15, of which 7 were waited for; matrix products, arithmetic and copies ran while one was open for 0% of the time, Pallas kernels for 11%

profile of v1, /device:TPU:1, one launch (start us, length us, event | category | flops | bytes accessed | tf_op | source)
XLA Modules:
  0.0 80.1 jit_solution(12688596674412095072)
XLA Ops:
  0.0 0.0 copy-start.1
  0.0 1.0 %constant_dynamic-update-slice_fusion.1 = bf16[2,2,256,256]{3,2,1,0:T(8,128)(2,1)S(1)} fusion(bf16[1,2,256,256]{3,2,1,0:T(8,128)(2,1)} %param.3), kind=kLoop, calls=%fused_computation.4 | loop fusion | bytes 524288
  1.0 0.0 copy-done.1
  1.0 0.0 copy-start
  1.1 0.1 collective-permute-start.1
  1.1 4.6 %collective-permute-start = (bf16[2,2,256,256]{3,2,1,0:T(8,128)(2,1)S(1)}, bf16[2,2,256,256]{3,2,1,0:T(8,128)(2,1)S(1)}, u32[]{:S(2)}, u32[]{:S(2)}) collective-permute-start(bf16[2,2,256,256]{3,2,1,0:T(8,128)(2,1)S(1)} %constant_dynamic-update-slice_fusion.own_a.far_a), channel_id=1, source_target_pairs={{1,2},{2,1},{5,6},{6,5},{9,10},{10,9},{13,14},{14,13},{17,18},{18,... | collective-permute-start | bytes 1572872 | tf_op jit(solution)/shard_map/ppermute | solution.py:154
  5.8 6.6 %collective-permute-done.1.near = bf16[2,2,256,256]{3,2,1,0:T(8,128)(2,1)S(1)} collective-permute-done((bf16[2,2,256,256]{3,2,1,0:T(8,128)(2,1)S(1)}, bf16[2,2,256,256]{3,2,1,0:T(8,128)(2,1)S(1)}, u32[]{:S(2)}, u32[]{:S(2)}) %collective-permute-start.1) | collective-permute-done | bytes 524320 | tf_op jit(solution)/shard_map/ppermute | solution.py:154
  12.4 5.6 %collective-permute-start.2 = (bf16[2,2,256,256]{3,2,1,0:T(8,128)(2,1)S(1)}, bf16[2,2,256,256]{3,2,1,0:T(8,128)(2,1)S(1)}, u32[]{:S(2)}, u32[]{:S(2)}) collective-permute-start(bf16[2,2,256,256]{3,2,1,0:T(8,128)(2,1)S(1)} %collective-permute-done.1.near), channel_id=1, source_target_pairs={{1,4},{5,8},{6,3},{9,12},{10,7},{14,11},{17,20},{21,24},{22,19},{2... | collective-permute-start | bytes 1572872 | tf_op jit(solution)/shard_map/ppermute | solution.py:154
  18.0 0.0 copy-done
  18.0 0.0 collective-permute-start.8
  18.1 0.1 pad_add_fusion.flags
  18.2 0.0 collective-permute-done.own_b
  18.2 5.9 %collective-permute-done.2.far_b = bf16[2,2,256,256]{3,2,1,0:T(8,128)(2,1)S(1)} collective-permute-done((bf16[2,2,256,256]{3,2,1,0:T(8,128)(2,1)S(1)}, bf16[2,2,256,256]{3,2,1,0:T(8,128)(2,1)S(1)}, u32[]{:S(2)}, u32[]{:S(2)}) %collective-permute-start.2) | collective-permute-done | bytes 524320 | tf_op jit(solution)/shard_map/ppermute | solution.py:154
  24.1 2.8 %shard_map.37 = (bf16[2,2,256,256]{3,2,1,0:T(8,128)(2,1)S(1)}, bf16[2,256,256]{2,1,0:T(8,128)(2,1)S(1)}, bf16[2,2,256,256]{3,2,1,0:T(8,128)(2,1)S(1)}) custom-call(s32[2]{0:T(128)S(1)} %pad_add_fusion.flags, bf16[2,2,256,256]{3,2,1,0:T(8,128)(2,1)S(1)} %constant_dynamic-update-slice_fusion.own_a.far_a, ...), custom_call_target="tpu_custom_call" | custom-call | flops 1342177280 | bytes 2621448 | tf_op jit(solution)/shard_map/pallas_call | solution.py:127
  26.9 4.4 %collective-permute-start.3 = (bf16[2,2,256,256]{3,2,1,0:T(8,128)(2,1)S(1)}, bf16[2,2,256,256]{3,2,1,0:T(8,128)(2,1)S(1)}, u32[]{:S(2)}, u32[]{:S(2)}) collective-permute-start(bf16[2,2,256,256]{3,2,1,0:T(8,128)(2,1)S(1)} %get-tuple-element.10.own.own_lu), channel_id=1, source_target_pairs={{0,1},{1,4},{2,3},{3,6},{4,5},{5,8},{6,7},{7,10},{8,9},{9,12},{10,... | collective-permute-start | bytes 1572872 | tf_op jit(solution)/shard_map/ppermute | solution.py:154
  31.3 1.9 %collective-permute-start.4 = (bf16[2,2,256,256]{3,2,1,0:T(8,128)(2,1)S(1)}, bf16[2,2,256,256]{3,2,1,0:T(8,128)(2,1)S(1)}, u32[]{:S(2)}, u32[]{:S(2)}) collective-permute-start(bf16[2,2,256,256]{3,2,1,0:T(8,128)(2,1)S(1)} %get-tuple-element.10.own.own_lu), channel_id=1, source_target_pairs={{1,0},{4,1},{3,2},{6,3},{5,4},{8,5},{7,6},{10,7},{9,8},{12,9},{11,... | collective-permute-start | bytes 1572872 | tf_op jit(solution)/shard_map/ppermute | solution.py:154
  33.2 1.9 %collective-permute-start.7 = (bf16[2,256,256]{2,1,0:T(8,128)(2,1)S(1)}, bf16[2,256,256]{2,1,0:T(8,128)(2,1)S(1)}, u32[]{:S(2)}, u32[]{:S(2)}) collective-permute-start(bf16[2,256,256]{2,1,0:T(8,128)(2,1)S(1)} %bitcast.10), channel_id=1, source_target_pairs={{1,2},{2,1},{5,6},{6,5},{9,10},{10,9},{13,14},{14,13},{17,18},{18,... | collective-permute-start | bytes 786440 | tf_op jit(solution)/shard_map/ppermute | solution.py:154
  35.1 0.0 collective-permute-done.8.near
  35.2 2.4 %collective-permute-start.9 = (bf16[2,256,256]{2,1,0:T(8,128)(2,1)S(1)}, bf16[2,256,256]{2,1,0:T(8,128)(2,1)S(1)}, u32[]{:S(2)}, u32[]{:S(2)}) collective-permute-start(bf16[2,256,256]{2,1,0:T(8,128)(2,1)S(1)} %collective-permute-done.8.near), channel_id=1, source_target_pairs={{1,4},{5,8},{6,3},{9,12},{10,7},{14,11},{17,20},{21,24},{22,19},{2... | collective-permute-start | bytes 786440 | tf_op jit(solution)/shard_map/ppermute | solution.py:154
  37.6 3.3 %collective-permute-done.7.own_b = bf16[2,256,256]{2,1,0:T(8,128)(2,1)S(1)} collective-permute-done((bf16[2,256,256]{2,1,0:T(8,128)(2,1)S(1)}, bf16[2,256,256]{2,1,0:T(8,128)(2,1)S(1)}, u32[]{:S(2)}, u32[]{:S(2)}) %collective-permute-start.7) | collective-permute-done | bytes 262176 | tf_op jit(solution)/shard_map/ppermute | solution.py:154
  40.9 0.0 collective-permute-done.9.far_b
  40.9 1.4 %shard_map.40.own = bf16[2,256,256]{2,1,0:T(8,128)(2,1)S(1)} custom-call(s32[2]{0:T(128)S(1)} %pad_add_fusion.flags, bf16[2,2,256,256]{3,2,1,0:T(8,128)(2,1)S(1)} %get-tuple-element.13.own_lu, bf16[2,256,256]{2,1,0:T(8,128)(2,1)S(1)} %get-tuple-element.14.spread, bf16[2,256,256]{2,1,0:T(8,128)(2,1)S(1)} %bitcast.11, ...), custom_call_target="tpu_custom_call" | custom-call | flops 402653184 | bytes 2097160 | tf_op jit(solution)/shard_map/pallas_call | solution.py:127
  42.4 4.3 %collective-permute-start.10 = (bf16[2,256,256]{2,1,0:T(8,128)(2,1)S(1)}, bf16[2,256,256]{2,1,0:T(8,128)(2,1)S(1)}, u32[]{:S(2)}, u32[]{:S(2)}) collective-permute-start(bf16[2,256,256]{2,1,0:T(8,128)(2,1)S(1)} %shard_map.40.own), channel_id=1, source_target_pairs={{0,1},{1,4},{2,3},{3,6},{4,5},{5,8},{6,7},{7,10},{8,9},{9,12},{10,... | collective-permute-start | bytes 786440 | tf_op jit(solution)/shard_map/ppermute | solution.py:154
  46.7 1.9 %collective-permute-start.11 = (bf16[2,256,256]{2,1,0:T(8,128)(2,1)S(1)}, bf16[2,256,256]{2,1,0:T(8,128)(2,1)S(1)}, u32[]{:S(2)}, u32[]{:S(2)}) collective-permute-start(bf16[2,256,256]{2,1,0:T(8,128)(2,1)S(1)} %shard_map.40.own), channel_id=1, source_target_pairs={{1,0},{4,1},{3,2},{6,3},{5,4},{8,5},{7,6},{10,7},{9,8},{12,9},{11,... | collective-permute-start | bytes 786440 | tf_op jit(solution)/shard_map/ppermute | solution.py:154
  48.6 0.0 collective-permute-done.3.below
  48.6 0.0 collective-permute-done.4.above
  48.7 2.2 %shard_map.38 = (bf16[2,2,256,256]{3,2,1,0:T(8,128)(2,1)S(1)}, bf16[2,256,256]{2,1,0:T(8,128)(2,1)S(1)}) custom-call(bf16[2,2,256,256]{3,2,1,0:T(8,128)(2,1)S(1)} %get-tuple-element.10.own.own_lu, bf16[2,2,256,256]{3,2,1,0:T(8,128)(2,1)S(1)} %collective-permute-done.3.below, bf16[2,2,256,256]{3,2,1,0:T(8,128)(2,1)S(1)} %collective-permute-done.4.above), custom_call_target="tpu_custom_call" | custom-call | flops 1342177280 | bytes 1572864 | tf_op jit(solution)/shard_map/pallas_call | solution.py:127
  50.9 3.2 %collective-permute-start.5 = (bf16[2,256,256]{2,1,0:T(8,128)(2,1)S(1)}, bf16[2,256,256]{2,1,0:T(8,128)(2,1)S(1)}, u32[]{:S(2)}, u32[]{:S(2)}) collective-permute-start(bf16[2,256,256]{2,1,0:T(8,128)(2,1)S(1)} %get-tuple-element.16), channel_id=1, source_target_pairs={{0,4},{1,5},{2,6},{3,7},{4,8},{5,9},{6,10},{7,11},{8,12},{9,13},{1... | collective-permute-start | bytes 786440 | tf_op jit(solution)/shard_map/ppermute | solution.py:154
  54.1 1.3 %collective-permute-start.6 = (bf16[2,256,256]{2,1,0:T(8,128)(2,1)S(1)}, bf16[2,256,256]{2,1,0:T(8,128)(2,1)S(1)}, u32[]{:S(2)}, u32[]{:S(2)}) collective-permute-start(bf16[2,256,256]{2,1,0:T(8,128)(2,1)S(1)} %get-tuple-element.15), channel_id=1, source_target_pairs={{4,0},{5,1},{6,2},{7,3},{8,4},{9,5},{10,6},{11,7},{12,8},{13,9},{1... | collective-permute-start | bytes 786440 | tf_op jit(solution)/shard_map/ppermute | solution.py:154
  55.4 0.0 collective-permute-done.10.below
  55.4 0.0 collective-permute-done.11.above
  55.5 0.9 %shard_map.41.own = bf16[2,256,256]{2,1,0:T(8,128)(2,1)S(1)} custom-call(bf16[2,2,256,256]{3,2,1,0:T(8,128)(2,1)S(1)} %get-tuple-element.10.own.own_lu, bf16[2,256,256]{2,1,0:T(8,128)(2,1)S(1)} %get-tuple-element.12.spread, bf16[2,256,256]{2,1,0:T(8,128)(2,1)S(1)} %shard_map.40.own, bf16[2,256,256]{2,1,0:T(8,128)(2,1)S(1)} %collective-permute-done.10.below, ...), custom_call_target="tpu_custom_call" | custom-call | flops 402653184 | bytes 1572864 | tf_op jit(solution)/shard_map/pallas_call | solution.py:127
  56.4 4.0 %collective-permute-start.12 = (bf16[2,256,256]{2,1,0:T(8,128)(2,1)S(1)}, bf16[2,256,256]{2,1,0:T(8,128)(2,1)S(1)}, u32[]{:S(2)}, u32[]{:S(2)}) collective-permute-start(bf16[2,256,256]{2,1,0:T(8,128)(2,1)S(1)} %shard_map.41.own), channel_id=1, source_target_pairs={{0,4},{1,5},{2,6},{3,7},{4,8},{5,9},{6,10},{7,11},{8,12},{9,13},{1... | collective-permute-start | bytes 786440 | tf_op jit(solution)/shard_map/ppermute | solution.py:154
  60.4 1.3 %collective-permute-start.13 = (bf16[2,256,256]{2,1,0:T(8,128)(2,1)S(1)}, bf16[2,256,256]{2,1,0:T(8,128)(2,1)S(1)}, u32[]{:S(2)}, u32[]{:S(2)}) collective-permute-start(bf16[2,256,256]{2,1,0:T(8,128)(2,1)S(1)} %shard_map.41.own), channel_id=1, source_target_pairs={{4,0},{5,1},{6,2},{7,3},{8,4},{9,5},{10,6},{11,7},{12,8},{13,9},{1... | collective-permute-start | bytes 786440 | tf_op jit(solution)/shard_map/ppermute | solution.py:154
  61.7 0.0 collective-permute-done.5.below_upper
  61.7 1.3 %collective-permute-done.6.above_lower = bf16[2,256,256]{2,1,0:T(8,128)(2,1)S(1)} collective-permute-done((bf16[2,256,256]{2,1,0:T(8,128)(2,1)S(1)}, bf16[2,256,256]{2,1,0:T(8,128)(2,1)S(1)}, u32[]{:S(2)}, u32[]{:S(2)}) %collective-permute-start.6) | collective-permute-done | bytes 262176 | tf_op jit(solution)/shard_map/ppermute | solution.py:154
  63.0 1.7 %shard_map.39.spread = bf16[2,256,256]{2,1,0:T(8,128)(2,1)S(1)} custom-call(bf16[2,2,256,256]{3,2,1,0:T(8,128)(2,1)S(1)} %get-tuple-element.11.own.own_lu, bf16[2,256,256]{2,1,0:T(8,128)(2,1)S(1)} %collective-permute-done.5.below_upper, bf16[2,256,256]{2,1,0:T(8,128)(2,1)S(1)} %collective-permute-done.6.above_lower), custom_call_target="tpu_custom_call" | custom-call | flops 805306368 | bytes 1048576 | tf_op jit(solution)/shard_map/pallas_call | solution.py:127
  64.7 0.1 collective-permute-done.12.below
  64.8 3.8 %collective-permute-done.13.above = bf16[2,256,256]{2,1,0:T(8,128)(2,1)S(1)} collective-permute-done((bf16[2,256,256]{2,1,0:T(8,128)(2,1)S(1)}, bf16[2,256,256]{2,1,0:T(8,128)(2,1)S(1)}, u32[]{:S(2)}, u32[]{:S(2)}) %collective-permute-start.13) | collective-permute-done | bytes 262176 | tf_op jit(solution)/shard_map/ppermute | solution.py:154
  68.7 0.9 %shard_map.42 = bf16[2,256,256]{2,1,0:T(8,128)(2,1)S(1)} custom-call(bf16[2,2,256,256]{3,2,1,0:T(8,128)(2,1)S(1)} %get-tuple-element.11.own.own_lu, bf16[2,256,256]{2,1,0:T(8,128)(2,1)S(1)} %shard_map.39.spread, bf16[2,256,256]{2,1,0:T(8,128)(2,1)S(1)} %shard_map.41.own, bf16[2,256,256]{2,1,0:T(8,128)(2,1)S(1)} %collective-permute-done.12.below, ...), custom_call_target="tpu_custom_call" | custom-call | flops 402653184 | bytes 1572864 | tf_op jit(solution)/shard_map/pallas_call | solution.py:127
  69.6 5.7 %collective-permute-start.14 = (bf16[2,256,256]{2,1,0:T(8,128)(2,1)S(1)}, bf16[2,256,256]{2,1,0:T(8,128)(2,1)S(1)}, u32[]{:S(2)}, u32[]{:S(2)}) collective-permute-start(bf16[2,256,256]{2,1,0:T(8,128)(2,1)S(1)} %shard_map.42), channel_id=1, source_target_pairs={{1,2},{2,1},{5,6},{6,5},{9,10},{10,9},{13,14},{14,13},{17,18},{18,... | collective-permute-start | bytes 786440 | tf_op jit(solution)/shard_map/ppermute | solution.py:154
  75.3 4.0 %collective-permute-done.14 = bf16[2,256,256]{2,1,0:T(8,128)(2,1)S(1)} collective-permute-done((bf16[2,256,256]{2,1,0:T(8,128)(2,1)S(1)}, bf16[2,256,256]{2,1,0:T(8,128)(2,1)S(1)}, u32[]{:S(2)}, u32[]{:S(2)}) %collective-permute-start.14) | collective-permute-done | bytes 262176 | tf_op jit(solution)/shard_map/ppermute | solution.py:154
  79.3 0.7 select_bitcast_fusion
  (2 shorter events, 0.1 us)
Async XLA Ops:
  0.0 1.0 %copy-start.1 = (bf16[1,2,256,256]{3,2,1,0:T(8,128)(2,1)S(1)}, bf16[1,2,256,256]{3,2,1,0:T(8,128)(2,1)}, u32[]{:S(2)}) copy-start(bf16[1,2,256,256]{3,2,1,0:T(8,128)(2,1)} %param.4) | copy-start | bytes 786436
  1.0 17.0 %copy-start = (bf16[1,2,256,256]{3,2,1,0:T(8,128)(2,1)S(1)}, bf16[1,2,256,256]{3,2,1,0:T(8,128)(2,1)}, u32[]{:S(2)}) copy-start(bf16[1,2,256,256]{3,2,1,0:T(8,128)(2,1)} %param.5) | copy-start | bytes 786436
  1.1 11.3 %collective-permute-start.1 = (bf16[2,2,256,256]{3,2,1,0:T(8,128)(2,1)S(1)}, bf16[2,2,256,256]{3,2,1,0:T(8,128)(2,1)S(1)}, u32[]{:S(2)}, u32[]{:S(2)}) collective-permute-start(bf16[2,2,256,256]{3,2,1,0:T(8,128)(2,1)S(1)} %constant_dynamic-update-slice_fusion.own_a.far_a), channel_id=1, source_target_pairs={{0,2},{1,0},{2,3},{3,1},{4,6},{5,4},{6,7},{7,5},{8,10},{9,8},{10,1... | collective-permute-start | bytes 1572872 | tf_op jit(solution)/shard_map/ppermute | solution.py:154
  1.1 17.0 %collective-permute-start = (bf16[2,2,256,256]{3,2,1,0:T(8,128)(2,1)S(1)}, bf16[2,2,256,256]{3,2,1,0:T(8,128)(2,1)S(1)}, u32[]{:S(2)}, u32[]{:S(2)}) collective-permute-start(bf16[2,2,256,256]{3,2,1,0:T(8,128)(2,1)S(1)} %constant_dynamic-update-slice_fusion.own_a.far_a), channel_id=1, source_target_pairs={{1,2},{2,1},{5,6},{6,5},{9,10},{10,9},{13,14},{14,13},{17,18},{18,... | collective-permute-start | bytes 1572872 | tf_op jit(solution)/shard_map/ppermute | solution.py:154
  12.4 11.7 %collective-permute-start.2 = (bf16[2,2,256,256]{3,2,1,0:T(8,128)(2,1)S(1)}, bf16[2,2,256,256]{3,2,1,0:T(8,128)(2,1)S(1)}, u32[]{:S(2)}, u32[]{:S(2)}) collective-permute-start(bf16[2,2,256,256]{3,2,1,0:T(8,128)(2,1)S(1)} %collective-permute-done.1.near), channel_id=1, source_target_pairs={{1,4},{5,8},{6,3},{9,12},{10,7},{14,11},{17,20},{21,24},{22,19},{2... | collective-permute-start | bytes 1572872 | tf_op jit(solution)/shard_map/ppermute | solution.py:154
  18.0 17.1 %collective-permute-start.8 = (bf16[2,256,256]{2,1,0:T(8,128)(2,1)S(1)}, bf16[2,256,256]{2,1,0:T(8,128)(2,1)S(1)}, u32[]{:S(2)}, u32[]{:S(2)}) collective-permute-start(bf16[2,256,256]{2,1,0:T(8,128)(2,1)S(1)} %bitcast.9), channel_id=1, source_target_pairs={{0,2},{1,0},{2,3},{3,1},{4,6},{5,4},{6,7},{7,5},{8,10},{9,8},{10,1... | collective-permute-start | bytes 786440 | tf_op jit(solution)/shard_map/ppermute | solution.py:154
  26.9 21.7 %collective-permute-start.3 = (bf16[2,2,256,256]{3,2,1,0:T(8,128)(2,1)S(1)}, bf16[2,2,256,256]{3,2,1,0:T(8,128)(2,1)S(1)}, u32[]{:S(2)}, u32[]{:S(2)}) collective-permute-start(bf16[2,2,256,256]{3,2,1,0:T(8,128)(2,1)S(1)} %get-tuple-element.10.own.own_lu), channel_id=1, source_target_pairs={{0,1},{1,4},{2,3},{3,6},{4,5},{5,8},{6,7},{7,10},{8,9},{9,12},{10,... | collective-permute-start | bytes 1572872 | tf_op jit(solution)/shard_map/ppermute | solution.py:154
  31.3 17.4 %collective-permute-start.4 = (bf16[2,2,256,256]{3,2,1,0:T(8,128)(2,1)S(1)}, bf16[2,2,256,256]{3,2,1,0:T(8,128)(2,1)S(1)}, u32[]{:S(2)}, u32[]{:S(2)}) collective-permute-start(bf16[2,2,256,256]{3,2,1,0:T(8,128)(2,1)S(1)} %get-tuple-element.10.own.own_lu), channel_id=1, source_target_pairs={{1,0},{4,1},{3,2},{6,3},{5,4},{8,5},{7,6},{10,7},{9,8},{12,9},{11,... | collective-permute-start | bytes 1572872 | tf_op jit(solution)/shard_map/ppermute | solution.py:154
  33.2 7.7 %collective-permute-start.7 = (bf16[2,256,256]{2,1,0:T(8,128)(2,1)S(1)}, bf16[2,256,256]{2,1,0:T(8,128)(2,1)S(1)}, u32[]{:S(2)}, u32[]{:S(2)}) collective-permute-start(bf16[2,256,256]{2,1,0:T(8,128)(2,1)S(1)} %bitcast.10), channel_id=1, source_target_pairs={{1,2},{2,1},{5,6},{6,5},{9,10},{10,9},{13,14},{14,13},{17,18},{18,... | collective-permute-start | bytes 786440 | tf_op jit(solution)/shard_map/ppermute | solution.py:154
  35.2 5.8 %collective-permute-start.9 = (bf16[2,256,256]{2,1,0:T(8,128)(2,1)S(1)}, bf16[2,256,256]{2,1,0:T(8,128)(2,1)S(1)}, u32[]{:S(2)}, u32[]{:S(2)}) collective-permute-start(bf16[2,256,256]{2,1,0:T(8,128)(2,1)S(1)} %collective-permute-done.8.near), channel_id=1, source_target_pairs={{1,4},{5,8},{6,3},{9,12},{10,7},{14,11},{17,20},{21,24},{22,19},{2... | collective-permute-start | bytes 786440 | tf_op jit(solution)/shard_map/ppermute | solution.py:154
  42.4 13.1 %collective-permute-start.10 = (bf16[2,256,256]{2,1,0:T(8,128)(2,1)S(1)}, bf16[2,256,256]{2,1,0:T(8,128)(2,1)S(1)}, u32[]{:S(2)}, u32[]{:S(2)}) collective-permute-start(bf16[2,256,256]{2,1,0:T(8,128)(2,1)S(1)} %shard_map.40.own), channel_id=1, source_target_pairs={{0,1},{1,4},{2,3},{3,6},{4,5},{5,8},{6,7},{7,10},{8,9},{9,12},{10,... | collective-permute-start | bytes 786440 | tf_op jit(solution)/shard_map/ppermute | solution.py:154
  46.7 8.7 %collective-permute-start.11 = (bf16[2,256,256]{2,1,0:T(8,128)(2,1)S(1)}, bf16[2,256,256]{2,1,0:T(8,128)(2,1)S(1)}, u32[]{:S(2)}, u32[]{:S(2)}) collective-permute-start(bf16[2,256,256]{2,1,0:T(8,128)(2,1)S(1)} %shard_map.40.own), channel_id=1, source_target_pairs={{1,0},{4,1},{3,2},{6,3},{5,4},{8,5},{7,6},{10,7},{9,8},{12,9},{11,... | collective-permute-start | bytes 786440 | tf_op jit(solution)/shard_map/ppermute | solution.py:154
  50.9 10.8 %collective-permute-start.5 = (bf16[2,256,256]{2,1,0:T(8,128)(2,1)S(1)}, bf16[2,256,256]{2,1,0:T(8,128)(2,1)S(1)}, u32[]{:S(2)}, u32[]{:S(2)}) collective-permute-start(bf16[2,256,256]{2,1,0:T(8,128)(2,1)S(1)} %get-tuple-element.16), channel_id=1, source_target_pairs={{0,4},{1,5},{2,6},{3,7},{4,8},{5,9},{6,10},{7,11},{8,12},{9,13},{1... | collective-permute-start | bytes 786440 | tf_op jit(solution)/shard_map/ppermute | solution.py:154
  54.1 8.9 %collective-permute-start.6 = (bf16[2,256,256]{2,1,0:T(8,128)(2,1)S(1)}, bf16[2,256,256]{2,1,0:T(8,128)(2,1)S(1)}, u32[]{:S(2)}, u32[]{:S(2)}) collective-permute-start(bf16[2,256,256]{2,1,0:T(8,128)(2,1)S(1)} %get-tuple-element.15), channel_id=1, source_target_pairs={{4,0},{5,1},{6,2},{7,3},{8,4},{9,5},{10,6},{11,7},{12,8},{13,9},{1... | collective-permute-start | bytes 786440 | tf_op jit(solution)/shard_map/ppermute | solution.py:154
  56.4 8.5 %collective-permute-start.12 = (bf16[2,256,256]{2,1,0:T(8,128)(2,1)S(1)}, bf16[2,256,256]{2,1,0:T(8,128)(2,1)S(1)}, u32[]{:S(2)}, u32[]{:S(2)}) collective-permute-start(bf16[2,256,256]{2,1,0:T(8,128)(2,1)S(1)} %shard_map.41.own), channel_id=1, source_target_pairs={{0,4},{1,5},{2,6},{3,7},{4,8},{5,9},{6,10},{7,11},{8,12},{9,13},{1... | collective-permute-start | bytes 786440 | tf_op jit(solution)/shard_map/ppermute | solution.py:154
  60.4 8.3 %collective-permute-start.13 = (bf16[2,256,256]{2,1,0:T(8,128)(2,1)S(1)}, bf16[2,256,256]{2,1,0:T(8,128)(2,1)S(1)}, u32[]{:S(2)}, u32[]{:S(2)}) collective-permute-start(bf16[2,256,256]{2,1,0:T(8,128)(2,1)S(1)} %shard_map.41.own), channel_id=1, source_target_pairs={{4,0},{5,1},{6,2},{7,3},{8,4},{9,5},{10,6},{11,7},{12,8},{13,9},{1... | collective-permute-start | bytes 786440 | tf_op jit(solution)/shard_map/ppermute | solution.py:154
  69.6 9.8 %collective-permute-start.14 = (bf16[2,256,256]{2,1,0:T(8,128)(2,1)S(1)}, bf16[2,256,256]{2,1,0:T(8,128)(2,1)S(1)}, u32[]{:S(2)}, u32[]{:S(2)}) collective-permute-start(bf16[2,256,256]{2,1,0:T(8,128)(2,1)S(1)} %shard_map.42), channel_id=1, source_target_pairs={{1,2},{2,1},{5,6},{6,5},{9,10},{10,9},{13,14},{14,13},{17,18},{18,... | collective-permute-start | bytes 786440 | tf_op jit(solution)/shard_map/ppermute | solution.py:154

commit v2 on v0

v2 whole, which is shorter than its diff:
```python
import functools

import jax
import jax.numpy as jnp
from jax import lax
from jax.experimental import pallas as pl
from jax.experimental.pallas import tpu as pltpu
from jax.sharding import PartitionSpec as P

GROUP = 4
LOW, UPP = 0, 1


def wide(block):
    real, imag = block[0], block[1]
    return jnp.concatenate(
        [jnp.concatenate([real, -imag], axis=1), jnp.concatenate([imag, real], axis=1)], axis=0
    )


def tall(block):
    return block.reshape(block.shape[0] * block.shape[1], block.shape[2])


def product(left, right):
    return jnp.dot(left, right, preferred_element_type=jnp.float32)


def low(value):
    return value.astype(jnp.bfloat16)


def parts(stacked):
    return stacked.reshape(2, stacked.shape[0] // 2, stacked.shape[1])


def beside(*blocks):
    return jnp.concatenate(blocks, axis=1)


def inverse_less_one(coupling):
    order = coupling.shape[1]
    first = low(coupling)
    second = product(wide(parts(first)), first)
    second_low = low(second)
    pair = product(wide(parts(second_low)), beside(second_low, first))
    fourth = low(pair[:, :order])
    short = coupling + second + pair[:, order:]
    whole = short + pair[:, :order] + product(wide(parts(low(short))), fourth)
    return low(whole)


def solved(spread, raw):
    return low(raw.astype(jnp.float32) + product(wide(spread), low(raw)))


def row_couplings(letter, own, near, far, new, spread):
    order = spread.shape[1]
    other = 1 - letter
    by_near = product(wide(own(letter)), beside(tall(near(other)), tall(near(letter))))
    by_far = product(wide(own(other)), beside(tall(far(letter)), tall(far(other))))
    spread[...] = parts(inverse_less_one(by_near[:, :order] + by_far[:, :order]))
    solution_of = spread[...]
    new[letter] = parts(solved(solution_of, -by_near[:, order:]))
    new[other] = parts(solved(solution_of, -by_far[:, order:]))


def row_injections(letter, own, spread, rhs, near, far):
    raw = tall(rhs).astype(jnp.float32) - product(wide(own(letter)), tall(near))
    return parts(solved(spread[...], raw - product(wide(own(1 - letter)), tall(far))))


def picked(edge, at_edge, inside):
    return lambda place: jnp.where(edge, at_edge[place], inside[place])


def first_couplings_kernel(flags, held, crossed, core, onward, level, new, spread):
    edge = flags[1] == 1
    own = picked(edge, crossed, held)
    near = picked(edge, onward, core)
    far = picked(edge, level, crossed)
    row_couplings(flags[0], own, near, far, new, spread)


def first_injections_kernel(
    flags, held, crossed, spread, held_rhs, crossed_rhs, core_rhs, onward_rhs, level_rhs, new
):
    edge = flags[1] == 1
    own = picked(edge, crossed, held)
    rhs = jnp.where(edge, crossed_rhs[...], held_rhs[...])
    near = jnp.where(edge, onward_rhs[...], core_rhs[...])
    far = jnp.where(edge, level_rhs[...], crossed_rhs[...])
    new[...] = row_injections(flags[0], own, spread, rhs, near, far)


def later_couplings_kernel(flags, held, core, level, new, spread):
    def at(ref):
        return lambda place: ref[place]

    row_couplings(flags[2], at(held), at(core), at(level), new, spread)


def later_injections_kernel(flags, held, spread, rhs, core, level, new):
    new[...] = row_injections(
        flags[2], lambda place: held[place], spread, rhs[...], core[...], level[...]
    )


def last_couplings_kernel(held, below_upper, above_lower, spread):
    coupling = product(wide(held[LOW]), tall(below_upper[...]))
    coupling = coupling + product(wide(held[UPP]), tall(above_lower[...]))
    spread[...] = parts(inverse_less_one(coupling))


def last_injections_kernel(held, spread, rhs, below, above, new):
    new[...] = row_injections(
        LOW, lambda place: held[place], spread, rhs[...], below[...], above[...]
    )


def run(kernel, outs, *operands, scalars=0):
    return pl.pallas_call(
        kernel,
        out_shape=[jax.ShapeDtypeStruct(s, jnp.bfloat16) for s in outs],
        in_specs=[pl.BlockSpec(memory_space=pltpu.SMEM)] * scalars
        + [pl.BlockSpec(memory_space=pltpu.VMEM)] * (len(operands) - scalars),
        out_specs=[pl.BlockSpec(memory_space=pltpu.VMEM)] * len(outs),
        compiler_params=pltpu.CompilerParams(vmem_limit_bytes=24 * 1024 * 1024),
    )(*operands)


def local(length, lower, upper, right_side):
    block = lower.shape[1:]
    pair = (2,) + block
    spot = lax.axis_index("chain") % GROUP
    first_letter = jnp.where(spot < GROUP // 2, LOW, UPP)
    edge = jnp.where((spot == 0) | (spot == GROUP - 1), 1, 0)
    second_letter = jnp.where(spot % 2 == 0, LOW, UPP)
    flags = jnp.stack([first_letter, edge, second_letter]).astype(jnp.int32)

    groups = range(0, length, GROUP)

    def move(value, *pairs):
        moves = [(g + a, g + b) for g in groups for a, b in pairs]
        return lax.ppermute(
            value, "chain", [(a, b) for a, b in moves if 0 <= a < length and 0 <= b < length]
        )

    mirrored = ((0, 3), (1, 2), (2, 1), (3, 0))
    inward = ((0, 1), (3, 2))
    outward = ((1, 0), (2, 3))
    levels = ((0, -GROUP), (3, 3 + GROUP))
    in_core = ((0, 1), (1, 0), (2, 3), (3, 2))
    between = ((0, 1 + GROUP), (1, -GROUP), (2, 3 + GROUP), (3, 2 - GROUP))
    upward = tuple((i, i + GROUP) for i in range(GROUP))
    downward = tuple((i, i - GROUP) for i in range(GROUP))
    home = ((0, 3), (1, 1), (2, 2), (3, 0))

    held = jnp.concatenate([lower, upper], axis=0)
    rhs = right_side[0]

    crossed = move(held, *mirrored)
    level = move(held, *levels)
    core = move(held, *inward)
    crossed_rhs = move(rhs, *mirrored)
    level_rhs = move(rhs, *levels)
    core_rhs = move(rhs, *inward)
    onward = move(crossed, *outward)
    onward_rhs = move(crossed_rhs, *outward)
    new_held, spread = run(
        first_couplings_kernel, (pair, block), flags, held, crossed, core, onward, level, scalars=1
    )
    (rhs,) = run(
        first_injections_kernel, (block,),
        flags, held, crossed, spread, rhs, crossed_rhs, core_rhs, onward_rhs, level_rhs,
        scalars=1,
    )
    held = new_held

    core, level = move(held, *in_core), move(held, *between)
    core_rhs, level_rhs = move(rhs, *in_core), move(rhs, *between)
    new_held, spread = run(
        later_couplings_kernel, (pair, block), flags, held, core, level, scalars=1
    )
    (rhs,) = run(
        later_injections_kernel, (block,),
        flags, held, spread, rhs, core_rhs, level_rhs,
        scalars=1,
    )
    held = new_held

    below, above = move(held[UPP], *upward), move(held[LOW], *downward)
    below_rhs, above_rhs = move(rhs, *upward), move(rhs, *downward)
    (spread,) = run(last_couplings_kernel, (block,), held, below, above)
    (result,) = run(last_injections_kernel, (block,), held, spread, rhs, below_rhs, above_rhs)
    return move(result, *home)[None]


def solution(mesh):
    placed = P(("energy", "chain"), None, None, None)
    return jax.shard_map(
        functools.partial(local, mesh.shape["chain"]),
        mesh=mesh,
        in_specs=(placed,) * 3,
        out_specs=placed,
        check_vma=False,
    )
```

time: 115 us -> 73 us (0.63)
  matrix products: 29.3 us -> 0 us
  waiting for transfers between devices: 44.8 us -> 25.6 us
  Pallas kernels: 0 us -> 10.4 us
  other arithmetic: 2.09 us -> 0.08 us
    dot_general x140 -> x0, matrix products: 29.3 us -> none  [the longest x35 7.33 us: complex_product(): jnp.dot(left_block[1], right_block[0], preferred_element_type=jnp.float32)]
    ppermute x6 -> x17, waiting for transfers between devices: 44.8 us -> 25.6 us  [move(): lax.ppermute(value, 'chain', [(a, b) for a, b in moves if 0 <= a < length...]
    pallas_call x0 -> x6, Pallas kernels: none -> 10.4 us  [run(): pl.pallas_call(kernel, out_shape=[jax.ShapeDtypeStruct(s, jnp.bfloat16) f...]
    convert_element_type x16 -> x0, other arithmetic: 1.16 us -> none  [the longest x6 0.37 us: approx_inverse(): (2.0 * identity_block - complex_product(diagonal_low, approx)).astype(jnp...]
    unnamed x7 -> x6, local copies, waits for them, and re-layouts: 2.35 us -> 1.73 us
    ppermute x6 -> x17, starting transfers between devices: 34.8 us -> 34.5 us  [move(): lax.ppermute(value, 'chain', [(a, b) for a, b in moves if 0 <= a < length...]
  transfers between devices with their start and end apart: 6 -> 17, of which waited for: 5 -> 7; matrix products, arithmetic and copies ran while one was open for 3% -> 0% of each run, Pallas kernels for 0% -> 13%
where the time goes in v2:
time: 73 us; the launch traced here: 72.6 us
  starting transfers between devices  34.5 us (47%)
  waiting for transfers between devices  25.6 us (35%)
  Pallas kernels  10.4 us (14%)
  local copies, waits for them, and re-layouts  1.79 us (2%)
    ppermute x17, starting transfers between devices, move(): lax.ppermute(value, 'chain', [(a, b) for a, b in moves if 0 <= a < length...  34.5 us
    ppermute x17, waiting for transfers between devices, move(): lax.ppermute(value, 'chain', [(a, b) for a, b in moves if 0 <= a < length...  25.6 us
    pallas_call x6, Pallas kernels, run(): pl.pallas_call(kernel, out_shape=[jax.ShapeDtypeStruct(s, jnp.bfloat16) f...  10.4 us
    unnamed x6, local copies, waits for them, and re-layouts  1.73 us
  transfers between devices with their start and end apart: 17, of which 7 were waited for; matrix products, arithmetic and copies ran while one was open for 0% of the time, Pallas kernels for 13%

profile of v2, /device:TPU:0, one launch (start us, length us, event | category | flops | bytes accessed | tf_op | source)
XLA Modules:
  0.0 72.6 jit_solution(14345910053116490655)
XLA Ops:
  0.0 0.0 copy-start.1
  0.0 1.0 %constant_dynamic-update-slice_fusion.1 = bf16[2,2,256,256]{3,2,1,0:T(8,128)(2,1)S(1)} fusion(bf16[1,2,256,256]{3,2,1,0:T(8,128)(2,1)} %param.3), kind=kLoop, calls=%fused_computation.3 | loop fusion | bytes 524288
  1.0 0.0 copy-done.1
  1.0 0.0 copy-start
  1.1 2.5 %collective-permute-start = (bf16[2,2,256,256]{3,2,1,0:T(8,128)(2,1)S(1)}, bf16[2,2,256,256]{3,2,1,0:T(8,128)(2,1)S(1)}, u32[]{:S(2)}, u32[]{:S(2)}) collective-permute-start(bf16[2,2,256,256]{3,2,1,0:T(8,128)(2,1)S(1)} %constant_dynamic-update-slice_fusion.held), channel_id=1, source_target_pairs={{0,3},{1,2},{2,1},{3,0},{4,7},{5,6},{6,5},{7,4},{8,11},{9,10},{10,... | collective-permute-start | bytes 1572872 | tf_op jit(solution)/shard_map/ppermute | solution.py:145
  3.5 2.6 %collective-permute-start.1 = (bf16[2,2,256,256]{3,2,1,0:T(8,128)(2,1)S(1)}, bf16[2,2,256,256]{3,2,1,0:T(8,128)(2,1)S(1)}, u32[]{:S(2)}, u32[]{:S(2)}) collective-permute-start(bf16[2,2,256,256]{3,2,1,0:T(8,128)(2,1)S(1)} %constant_dynamic-update-slice_fusion.held), channel_id=1, source_target_pairs={{0,1},{3,2},{4,5},{7,6},{8,9},{11,10},{12,13},{15,14},{16,17},{19,... | collective-permute-start | bytes 1572872 | tf_op jit(solution)/shard_map/ppermute | solution.py:145
  6.1 1.3 %collective-permute-start.3 = (bf16[2,2,256,256]{3,2,1,0:T(8,128)(2,1)S(1)}, bf16[2,2,256,256]{3,2,1,0:T(8,128)(2,1)S(1)}, u32[]{:S(2)}, u32[]{:S(2)}) collective-permute-start(bf16[2,2,256,256]{3,2,1,0:T(8,128)(2,1)S(1)} %constant_dynamic-update-slice_fusion.held), channel_id=1, source_target_pairs={{3,7},{4,0},{7,11},{8,4},{11,15},{12,8},{19,23},{20,16},{23,27},{2... | collective-permute-start | bytes 1572872 | tf_op jit(solution)/shard_map/ppermute | solution.py:145
  7.4 8.4 %collective-permute-done.crossed = bf16[2,2,256,256]{3,2,1,0:T(8,128)(2,1)S(1)} collective-permute-done((bf16[2,2,256,256]{3,2,1,0:T(8,128)(2,1)S(1)}, bf16[2,2,256,256]{3,2,1,0:T(8,128)(2,1)S(1)}, u32[]{:S(2)}, u32[]{:S(2)}) %collective-permute-start) | collective-permute-done | bytes 524320 | tf_op jit(solution)/shard_map/ppermute | solution.py:145
  15.9 1.3 %collective-permute-start.2 = (bf16[2,2,256,256]{3,2,1,0:T(8,128)(2,1)S(1)}, bf16[2,2,256,256]{3,2,1,0:T(8,128)(2,1)S(1)}, u32[]{:S(2)}, u32[]{:S(2)}) collective-permute-start(bf16[2,2,256,256]{3,2,1,0:T(8,128)(2,1)S(1)} %collective-permute-done.crossed), channel_id=1, source_target_pairs={{1,0},{2,3},{5,4},{6,7},{9,8},{10,11},{13,12},{14,15},{17,16},{18,... | collective-permute-start | bytes 1572872 | tf_op jit(solution)/shard_map/ppermute | solution.py:145
  17.1 0.0 copy-done
  17.2 2.2 %collective-permute-start.8 = (bf16[2,256,256]{2,1,0:T(8,128)(2,1)S(1)}, bf16[2,256,256]{2,1,0:T(8,128)(2,1)S(1)}, u32[]{:S(2)}, u32[]{:S(2)}) collective-permute-start(bf16[2,256,256]{2,1,0:T(8,128)(2,1)S(1)} %bitcast.9), channel_id=1, source_target_pairs={{0,3},{1,2},{2,1},{3,0},{4,7},{5,6},{6,5},{7,4},{8,11},{9,10},{10,... | collective-permute-start | bytes 786440 | tf_op jit(solution)/shard_map/ppermute | solution.py:145
  19.4 0.1 pad_add_fusion.flags
  19.5 0.0 collective-permute-done.1.core
  19.5 0.0 collective-permute-done.3.level
  19.5 0.2 collective-permute-done.2.onward
  19.6 2.5 %shard_map.37 = (bf16[2,2,256,256]{3,2,1,0:T(8,128)(2,1)S(1)}, bf16[2,256,256]{2,1,0:T(8,128)(2,1)S(1)}) custom-call(s32[3]{0:T(128)S(1)} %pad_add_fusion.flags, bf16[2,2,256,256]{3,2,1,0:T(8,128)(2,1)S(1)} %constant_dynamic-update-slice_fusion.held, bf16[2,2,256,256]{3,2,1,0:T(8,128)(2,1)S(1)} %collective-permute-done.crossed, ...), custom_call_target="tpu_custom_call" | custom-call | tf_op jit(solution)/shard_map/pallas_call | solution.py:122
  22.1 1.1 %collective-permute-start.4 = (bf16[2,2,256,256]{3,2,1,0:T(8,128)(2,1)S(1)}, bf16[2,2,256,256]{3,2,1,0:T(8,128)(2,1)S(1)}, u32[]{:S(2)}, u32[]{:S(2)}) collective-permute-start(bf16[2,2,256,256]{3,2,1,0:T(8,128)(2,1)S(1)} %get-tuple-element.9.held), channel_id=1, source_target_pairs={{0,1},{1,0},{2,3},{3,2},{4,5},{5,4},{6,7},{7,6},{8,9},{9,8},{10,11... | collective-permute-start | bytes 1572872 | tf_op jit(solution)/shard_map/ppermute | solution.py:145
  23.2 3.5 %collective-permute-start.5 = (bf16[2,2,256,256]{3,2,1,0:T(8,128)(2,1)S(1)}, bf16[2,2,256,256]{3,2,1,0:T(8,128)(2,1)S(1)}, u32[]{:S(2)}, u32[]{:S(2)}) collective-permute-start(bf16[2,2,256,256]{3,2,1,0:T(8,128)(2,1)S(1)} %get-tuple-element.9.held), channel_id=1, source_target_pairs={{0,5},{2,7},{4,9},{5,0},{6,11},{7,2},{8,13},{9,4},{10,15},{11,6},{... | collective-permute-start | bytes 1572872 | tf_op jit(solution)/shard_map/ppermute | solution.py:145
  26.7 1.3 %collective-permute-start.11 = (bf16[2,256,256]{2,1,0:T(8,128)(2,1)S(1)}, bf16[2,256,256]{2,1,0:T(8,128)(2,1)S(1)}, u32[]{:S(2)}, u32[]{:S(2)}) collective-permute-start(bf16[2,256,256]{2,1,0:T(8,128)(2,1)S(1)} %bitcast.10), channel_id=1, source_target_pairs={{3,7},{4,0},{7,11},{8,4},{11,15},{12,8},{19,23},{20,16},{23,27},{2... | collective-permute-start | bytes 786440 | tf_op jit(solution)/shard_map/ppermute | solution.py:145
  28.0 1.3 %collective-permute-start.9 = (bf16[2,256,256]{2,1,0:T(8,128)(2,1)S(1)}, bf16[2,256,256]{2,1,0:T(8,128)(2,1)S(1)}, u32[]{:S(2)}, u32[]{:S(2)}) collective-permute-start(bf16[2,256,256]{2,1,0:T(8,128)(2,1)S(1)} %bitcast.11), channel_id=1, source_target_pairs={{0,1},{3,2},{4,5},{7,6},{8,9},{11,10},{12,13},{15,14},{16,17},{19,... | collective-permute-start | bytes 786440 | tf_op jit(solution)/shard_map/ppermute | solution.py:145
  29.3 0.0 collective-permute-done.8.crossed_rhs
  29.3 1.3 %collective-permute-start.10 = (bf16[2,256,256]{2,1,0:T(8,128)(2,1)S(1)}, bf16[2,256,256]{2,1,0:T(8,128)(2,1)S(1)}, u32[]{:S(2)}, u32[]{:S(2)}) collective-permute-start(bf16[2,256,256]{2,1,0:T(8,128)(2,1)S(1)} %collective-permute-done.8.crossed_rhs), channel_id=1, source_target_pairs={{1,0},{2,3},{5,4},{6,7},{9,8},{10,11},{13,12},{14,15},{17,16},{18,... | collective-permute-start | bytes 786440 | tf_op jit(solution)/shard_map/ppermute | solution.py:145
  30.6 5.9 %collective-permute-done.11.level_rhs = bf16[2,256,256]{2,1,0:T(8,128)(2,1)S(1)} collective-permute-done((bf16[2,256,256]{2,1,0:T(8,128)(2,1)S(1)}, bf16[2,256,256]{2,1,0:T(8,128)(2,1)S(1)}, u32[]{:S(2)}, u32[]{:S(2)}) %collective-permute-start.11) | collective-permute-done | bytes 262176 | tf_op jit(solution)/shard_map/ppermute | solution.py:145
  36.5 0.0 collective-permute-done.9.core_rhs
  36.5 0.0 collective-permute-done.10.onward_rhs
  36.5 1.5 %shard_map.40.rhs = bf16[2,256,256]{2,1,0:T(8,128)(2,1)S(1)} custom-call(s32[3]{0:T(128)S(1)} %pad_add_fusion.flags, bf16[2,2,256,256]{3,2,1,0:T(8,128)(2,1)S(1)} %constant_dynamic-update-slice_fusion.held, bf16[2,2,256,256]{3,2,1,0:T(8,128)(2,1)S(1)} %collective-permute-done.crossed, bf16[2,256,256]{2,1,0:T(8,128)(2,1)S(1)} %get-tuple-element.12.spread, ...), custom_call_target="tpu_custom_call" | custom-call | tf_op jit(solution)/shard_map/pallas_call | solution.py:122
  38.0 0.1 collective-permute-start.12
  38.0 3.6 %collective-permute-start.13 = (bf16[2,256,256]{2,1,0:T(8,128)(2,1)S(1)}, bf16[2,256,256]{2,1,0:T(8,128)(2,1)S(1)}, u32[]{:S(2)}, u32[]{:S(2)}) collective-permute-start(bf16[2,256,256]{2,1,0:T(8,128)(2,1)S(1)} %shard_map.40.rhs), channel_id=1, source_target_pairs={{0,5},{2,7},{4,9},{5,0},{6,11},{7,2},{8,13},{9,4},{10,15},{11,6},{... | collective-permute-start | bytes 786440 | tf_op jit(solution)/shard_map/ppermute | solution.py:145
  41.6 0.0 collective-permute-done.4.core
  41.6 0.0 collective-permute-done.5.level
  41.7 2.5 %shard_map.38 = (bf16[2,2,256,256]{3,2,1,0:T(8,128)(2,1)S(1)}, bf16[2,256,256]{2,1,0:T(8,128)(2,1)S(1)}) custom-call(s32[3]{0:T(128)S(1)} %pad_add_fusion.flags, bf16[2,2,256,256]{3,2,1,0:T(8,128)(2,1)S(1)} %get-tuple-element.9.held, bf16[2,2,256,256]{3,2,1,0:T(8,128)(2,1)S(1)} %collective-permute-done.4.core, ...), custom_call_target="tpu_custom_call" | custom-call | tf_op jit(solution)/shard_map/pallas_call | solution.py:122
  44.2 3.5 %collective-permute-start.6 = (bf16[2,256,256]{2,1,0:T(8,128)(2,1)S(1)}, bf16[2,256,256]{2,1,0:T(8,128)(2,1)S(1)}, u32[]{:S(2)}, u32[]{:S(2)}) collective-permute-start(bf16[2,256,256]{2,1,0:T(8,128)(2,1)S(1)} %get-tuple-element.14), channel_id=1, source_target_pairs={{0,4},{1,5},{2,6},{3,7},{4,8},{5,9},{6,10},{7,11},{8,12},{9,13},{1... | collective-permute-start | bytes 786440 | tf_op jit(solution)/shard_map/ppermute | solution.py:145
  47.7 1.3 %collective-permute-start.7 = (bf16[2,256,256]{2,1,0:T(8,128)(2,1)S(1)}, bf16[2,256,256]{2,1,0:T(8,128)(2,1)S(1)}, u32[]{:S(2)}, u32[]{:S(2)}) collective-permute-start(bf16[2,256,256]{2,1,0:T(8,128)(2,1)S(1)} %get-tuple-element.13), channel_id=1, source_target_pairs={{4,0},{5,1},{6,2},{7,3},{8,4},{9,5},{10,6},{11,7},{12,8},{13,9},{1... | collective-permute-start | bytes 786440 | tf_op jit(solution)/shard_map/ppermute | solution.py:145
  49.0 0.0 collective-permute-done.12.core
  49.0 0.0 collective-permute-done.13.level
  49.0 1.4 %shard_map.41.rhs = bf16[2,256,256]{2,1,0:T(8,128)(2,1)S(1)} custom-call(s32[3]{0:T(128)S(1)} %pad_add_fusion.flags, bf16[2,2,256,256]{3,2,1,0:T(8,128)(2,1)S(1)} %get-tuple-element.9.held, bf16[2,256,256]{2,1,0:T(8,128)(2,1)S(1)} %get-tuple-element.11.spread, bf16[2,256,256]{2,1,0:T(8,128)(2,1)S(1)} %shard_map.40.rhs, ...), custom_call_target="tpu_custom_call" | custom-call | tf_op jit(solution)/shard_map/pallas_call | solution.py:122
  50.5 4.6 %collective-permute-start.14 = (bf16[2,256,256]{2,1,0:T(8,128)(2,1)S(1)}, bf16[2,256,256]{2,1,0:T(8,128)(2,1)S(1)}, u32[]{:S(2)}, u32[]{:S(2)}) collective-permute-start(bf16[2,256,256]{2,1,0:T(8,128)(2,1)S(1)} %shard_map.41.rhs), channel_id=1, source_target_pairs={{0,4},{1,5},{2,6},{3,7},{4,8},{5,9},{6,10},{7,11},{8,12},{9,13},{1... | collective-permute-start | bytes 786440 | tf_op jit(solution)/shard_map/ppermute | solution.py:145
  55.0 1.3 %collective-permute-start.15 = (bf16[2,256,256]{2,1,0:T(8,128)(2,1)S(1)}, bf16[2,256,256]{2,1,0:T(8,128)(2,1)S(1)}, u32[]{:S(2)}, u32[]{:S(2)}) collective-permute-start(bf16[2,256,256]{2,1,0:T(8,128)(2,1)S(1)} %shard_map.41.rhs), channel_id=1, source_target_pairs={{4,0},{5,1},{6,2},{7,3},{8,4},{9,5},{10,6},{11,7},{12,8},{13,9},{1... | collective-permute-start | bytes 786440 | tf_op jit(solution)/shard_map/ppermute | solution.py:145
  56.3 0.0 collective-permute-done.6.below_upper
  56.3 0.1 collective-permute-done.7.above_lower
  56.4 1.7 %shard_map.39.spread = bf16[2,256,256]{2,1,0:T(8,128)(2,1)S(1)} custom-call(bf16[2,2,256,256]{3,2,1,0:T(8,128)(2,1)S(1)} %get-tuple-element.10.held, bf16[2,256,256]{2,1,0:T(8,128)(2,1)S(1)} %collective-permute-done.6.below_upper, bf16[2,256,256]{2,1,0:T(8,128)(2,1)S(1)} %collective-permute-done.7.above_lower), custom_call_target="tpu_custom_call" | custom-call | tf_op jit(solution)/shard_map/pallas_call | solution.py:122
  58.1 1.0 %collective-permute-done.14.below = bf16[2,256,256]{2,1,0:T(8,128)(2,1)S(1)} collective-permute-done((bf16[2,256,256]{2,1,0:T(8,128)(2,1)S(1)}, bf16[2,256,256]{2,1,0:T(8,128)(2,1)S(1)}, u32[]{:S(2)}, u32[]{:S(2)}) %collective-permute-start.14) | collective-permute-done | bytes 262176 | tf_op jit(solution)/shard_map/ppermute | solution.py:145
  59.0 4.2 %collective-permute-done.15.above = bf16[2,256,256]{2,1,0:T(8,128)(2,1)S(1)} collective-permute-done((bf16[2,256,256]{2,1,0:T(8,128)(2,1)S(1)}, bf16[2,256,256]{2,1,0:T(8,128)(2,1)S(1)}, u32[]{:S(2)}, u32[]{:S(2)}) %collective-permute-start.15) | collective-permute-done | bytes 262176 | tf_op jit(solution)/shard_map/ppermute | solution.py:145
  63.3 0.9 %shard_map.42 = bf16[2,256,256]{2,1,0:T(8,128)(2,1)S(1)} custom-call(bf16[2,2,256,256]{3,2,1,0:T(8,128)(2,1)S(1)} %get-tuple-element.10.held, bf16[2,256,256]{2,1,0:T(8,128)(2,1)S(1)} %shard_map.39.spread, bf16[2,256,256]{2,1,0:T(8,128)(2,1)S(1)} %shard_map.41.rhs, bf16[2,256,256]{2,1,0:T(8,128)(2,1)S(1)} %collective-permute-done.14.below, ...), custom_call_target="tpu_custom_call" | custom-call | tf_op jit(solution)/shard_map/pallas_call | solution.py:122
  64.2 1.9 %collective-permute-start.16 = (bf16[2,256,256]{2,1,0:T(8,128)(2,1)S(1)}, bf16[2,256,256]{2,1,0:T(8,128)(2,1)S(1)}, u32[]{:S(2)}, u32[]{:S(2)}) collective-permute-start(bf16[2,256,256]{2,1,0:T(8,128)(2,1)S(1)} %shard_map.42), channel_id=1, source_target_pairs={{0,3},{1,1},{2,2},{3,0},{4,7},{5,5},{6,6},{7,4},{8,11},{9,9},{10,1... | collective-permute-start | bytes 786440 | tf_op jit(solution)/shard_map/ppermute | solution.py:145
  66.1 5.8 %collective-permute-done.16 = bf16[2,256,256]{2,1,0:T(8,128)(2,1)S(1)} collective-permute-done((bf16[2,256,256]{2,1,0:T(8,128)(2,1)S(1)}, bf16[2,256,256]{2,1,0:T(8,128)(2,1)S(1)}, u32[]{:S(2)}, u32[]{:S(2)}) %collective-permute-start.16) | collective-permute-done | bytes 262176 | tf_op jit(solution)/shard_map/ppermute | solution.py:145
  71.9 0.7 copy.6
  (2 shorter events, 0.1 us)
Async XLA Ops:
  0.0 1.0 %copy-start.1 = (bf16[1,2,256,256]{3,2,1,0:T(8,128)(2,1)S(1)}, bf16[1,2,256,256]{3,2,1,0:T(8,128)(2,1)}, u32[]{:S(2)}) copy-start(bf16[1,2,256,256]{3,2,1,0:T(8,128)(2,1)} %param.4) | copy-start | bytes 786436
  1.0 16.1 %copy-start = (bf16[1,2,256,256]{3,2,1,0:T(8,128)(2,1)S(1)}, bf16[1,2,256,256]{3,2,1,0:T(8,128)(2,1)}, u32[]{:S(2)}) copy-start(bf16[1,2,256,256]{3,2,1,0:T(8,128)(2,1)} %param.5) | copy-start | bytes 786436
  1.1 14.8 %collective-permute-start = (bf16[2,2,256,256]{3,2,1,0:T(8,128)(2,1)S(1)}, bf16[2,2,256,256]{3,2,1,0:T(8,128)(2,1)S(1)}, u32[]{:S(2)}, u32[]{:S(2)}) collective-permute-start(bf16[2,2,256,256]{3,2,1,0:T(8,128)(2,1)S(1)} %constant_dynamic-update-slice_fusion.held), channel_id=1, source_target_pairs={{0,3},{1,2},{2,1},{3,0},{4,7},{5,6},{6,5},{7,4},{8,11},{9,10},{10,... | collective-permute-start | bytes 1572872 | tf_op jit(solution)/shard_map/ppermute | solution.py:145
  3.5 15.9 %collective-permute-start.1 = (bf16[2,2,256,256]{3,2,1,0:T(8,128)(2,1)S(1)}, bf16[2,2,256,256]{3,2,1,0:T(8,128)(2,1)S(1)}, u32[]{:S(2)}, u32[]{:S(2)}) collective-permute-start(bf16[2,2,256,256]{3,2,1,0:T(8,128)(2,1)S(1)} %constant_dynamic-update-slice_fusion.held), channel_id=1, source_target_pairs={{0,1},{3,2},{4,5},{7,6},{8,9},{11,10},{12,13},{15,14},{16,17},{19,... | collective-permute-start | bytes 1572872 | tf_op jit(solution)/shard_map/ppermute | solution.py:145
  6.1 13.3 %collective-permute-start.3 = (bf16[2,2,256,256]{3,2,1,0:T(8,128)(2,1)S(1)}, bf16[2,2,256,256]{3,2,1,0:T(8,128)(2,1)S(1)}, u32[]{:S(2)}, u32[]{:S(2)}) collective-permute-start(bf16[2,2,256,256]{3,2,1,0:T(8,128)(2,1)S(1)} %constant_dynamic-update-slice_fusion.held), channel_id=1, source_target_pairs={{3,7},{4,0},{7,11},{8,4},{11,15},{12,8},{19,23},{20,16},{23,27},{2... | collective-permute-start | bytes 1572872 | tf_op jit(solution)/shard_map/ppermute | solution.py:145
  15.9 3.8 %collective-permute-start.2 = (bf16[2,2,256,256]{3,2,1,0:T(8,128)(2,1)S(1)}, bf16[2,2,256,256]{3,2,1,0:T(8,128)(2,1)S(1)}, u32[]{:S(2)}, u32[]{:S(2)}) collective-permute-start(bf16[2,2,256,256]{3,2,1,0:T(8,128)(2,1)S(1)} %collective-permute-done.crossed), channel_id=1, source_target_pairs={{1,0},{2,3},{5,4},{6,7},{9,8},{10,11},{13,12},{14,15},{17,16},{18,... | collective-permute-start | bytes 1572872 | tf_op jit(solution)/shard_map/ppermute | solution.py:145
  17.2 12.1 %collective-permute-start.8 = (bf16[2,256,256]{2,1,0:T(8,128)(2,1)S(1)}, bf16[2,256,256]{2,1,0:T(8,128)(2,1)S(1)}, u32[]{:S(2)}, u32[]{:S(2)}) collective-permute-start(bf16[2,256,256]{2,1,0:T(8,128)(2,1)S(1)} %bitcast.9), channel_id=1, source_target_pairs={{0,3},{1,2},{2,1},{3,0},{4,7},{5,6},{6,5},{7,4},{8,11},{9,10},{10,... | collective-permute-start | bytes 786440 | tf_op jit(solution)/shard_map/ppermute | solution.py:145
  22.1 19.5 %collective-permute-start.4 = (bf16[2,2,256,256]{3,2,1,0:T(8,128)(2,1)S(1)}, bf16[2,2,256,256]{3,2,1,0:T(8,128)(2,1)S(1)}, u32[]{:S(2)}, u32[]{:S(2)}) collective-permute-start(bf16[2,2,256,256]{3,2,1,0:T(8,128)(2,1)S(1)} %get-tuple-element.9.held), channel_id=1, source_target_pairs={{0,1},{1,0},{2,3},{3,2},{4,5},{5,4},{6,7},{7,6},{8,9},{9,8},{10,11... | collective-permute-start | bytes 1572872 | tf_op jit(solution)/shard_map/ppermute | solution.py:145
  23.2 18.5 %collective-permute-start.5 = (bf16[2,2,256,256]{3,2,1,0:T(8,128)(2,1)S(1)}, bf16[2,2,256,256]{3,2,1,0:T(8,128)(2,1)S(1)}, u32[]{:S(2)}, u32[]{:S(2)}) collective-permute-start(bf16[2,2,256,256]{3,2,1,0:T(8,128)(2,1)S(1)} %get-tuple-element.9.held), channel_id=1, source_target_pairs={{0,5},{2,7},{4,9},{5,0},{6,11},{7,2},{8,13},{9,4},{10,15},{11,6},{... | collective-permute-start | bytes 1572872 | tf_op jit(solution)/shard_map/ppermute | solution.py:145
  26.7 9.8 %collective-permute-start.11 = (bf16[2,256,256]{2,1,0:T(8,128)(2,1)S(1)}, bf16[2,256,256]{2,1,0:T(8,128)(2,1)S(1)}, u32[]{:S(2)}, u32[]{:S(2)}) collective-permute-start(bf16[2,256,256]{2,1,0:T(8,128)(2,1)S(1)} %bitcast.10), channel_id=1, source_target_pairs={{3,7},{4,0},{7,11},{8,4},{11,15},{12,8},{19,23},{20,16},{23,27},{2... | collective-permute-start | bytes 786440 | tf_op jit(solution)/shard_map/ppermute | solution.py:145
  28.0 8.5 %collective-permute-start.9 = (bf16[2,256,256]{2,1,0:T(8,128)(2,1)S(1)}, bf16[2,256,256]{2,1,0:T(8,128)(2,1)S(1)}, u32[]{:S(2)}, u32[]{:S(2)}) collective-permute-start(bf16[2,256,256]{2,1,0:T(8,128)(2,1)S(1)} %bitcast.11), channel_id=1, source_target_pairs={{0,1},{3,2},{4,5},{7,6},{8,9},{11,10},{12,13},{15,14},{16,17},{19,... | collective-permute-start | bytes 786440 | tf_op jit(solution)/shard_map/ppermute | solution.py:145
  29.3 7.2 %collective-permute-start.10 = (bf16[2,256,256]{2,1,0:T(8,128)(2,1)S(1)}, bf16[2,256,256]{2,1,0:T(8,128)(2,1)S(1)}, u32[]{:S(2)}, u32[]{:S(2)}) collective-permute-start(bf16[2,256,256]{2,1,0:T(8,128)(2,1)S(1)} %collective-permute-done.8.crossed_rhs), channel_id=1, source_target_pairs={{1,0},{2,3},{5,4},{6,7},{9,8},{10,11},{13,12},{14,15},{17,16},{18,... | collective-permute-start | bytes 786440 | tf_op jit(solution)/shard_map/ppermute | solution.py:145
  38.0 11.0 %collective-permute-start.12 = (bf16[2,256,256]{2,1,0:T(8,128)(2,1)S(1)}, bf16[2,256,256]{2,1,0:T(8,128)(2,1)S(1)}, u32[]{:S(2)}, u32[]{:S(2)}) collective-permute-start(bf16[2,256,256]{2,1,0:T(8,128)(2,1)S(1)} %shard_map.40.rhs), channel_id=1, source_target_pairs={{0,1},{1,0},{2,3},{3,2},{4,5},{5,4},{6,7},{7,6},{8,9},{9,8},{10,11... | collective-permute-start | bytes 786440 | tf_op jit(solution)/shard_map/ppermute | solution.py:145
  38.0 11.0 %collective-permute-start.13 = (bf16[2,256,256]{2,1,0:T(8,128)(2,1)S(1)}, bf16[2,256,256]{2,1,0:T(8,128)(2,1)S(1)}, u32[]{:S(2)}, u32[]{:S(2)}) collective-permute-start(bf16[2,256,256]{2,1,0:T(8,128)(2,1)S(1)} %shard_map.40.rhs), channel_id=1, source_target_pairs={{0,5},{2,7},{4,9},{5,0},{6,11},{7,2},{8,13},{9,4},{10,15},{11,6},{... | collective-permute-start | bytes 786440 | tf_op jit(solution)/shard_map/ppermute | solution.py:145
  44.2 12.1 %collective-permute-start.6 = (bf16[2,256,256]{2,1,0:T(8,128)(2,1)S(1)}, bf16[2,256,256]{2,1,0:T(8,128)(2,1)S(1)}, u32[]{:S(2)}, u32[]{:S(2)}) collective-permute-start(bf16[2,256,256]{2,1,0:T(8,128)(2,1)S(1)} %get-tuple-element.14), channel_id=1, source_target_pairs={{0,4},{1,5},{2,6},{3,7},{4,8},{5,9},{6,10},{7,11},{8,12},{9,13},{1... | collective-permute-start | bytes 786440 | tf_op jit(solution)/shard_map/ppermute | solution.py:145
  47.7 8.7 %collective-permute-start.7 = (bf16[2,256,256]{2,1,0:T(8,128)(2,1)S(1)}, bf16[2,256,256]{2,1,0:T(8,128)(2,1)S(1)}, u32[]{:S(2)}, u32[]{:S(2)}) collective-permute-start(bf16[2,256,256]{2,1,0:T(8,128)(2,1)S(1)} %get-tuple-element.13), channel_id=1, source_target_pairs={{4,0},{5,1},{6,2},{7,3},{8,4},{9,5},{10,6},{11,7},{12,8},{13,9},{1... | collective-permute-start | bytes 786440 | tf_op jit(solution)/shard_map/ppermute | solution.py:145
  50.5 8.6 %collective-permute-start.14 = (bf16[2,256,256]{2,1,0:T(8,128)(2,1)S(1)}, bf16[2,256,256]{2,1,0:T(8,128)(2,1)S(1)}, u32[]{:S(2)}, u32[]{:S(2)}) collective-permute-start(bf16[2,256,256]{2,1,0:T(8,128)(2,1)S(1)} %shard_map.41.rhs), channel_id=1, source_target_pairs={{0,4},{1,5},{2,6},{3,7},{4,8},{5,9},{6,10},{7,11},{8,12},{9,13},{1... | collective-permute-start | bytes 786440 | tf_op jit(solution)/shard_map/ppermute | solution.py:145
  55.0 8.3 %collective-permute-start.15 = (bf16[2,256,256]{2,1,0:T(8,128)(2,1)S(1)}, bf16[2,256,256]{2,1,0:T(8,128)(2,1)S(1)}, u32[]{:S(2)}, u32[]{:S(2)}) collective-permute-start(bf16[2,256,256]{2,1,0:T(8,128)(2,1)S(1)} %shard_map.41.rhs), channel_id=1, source_target_pairs={{4,0},{5,1},{6,2},{7,3},{8,4},{9,5},{10,6},{11,7},{12,8},{13,9},{1... | collective-permute-start | bytes 786440 | tf_op jit(solution)/shard_map/ppermute | solution.py:145
  64.2 7.7 %collective-permute-start.16 = (bf16[2,256,256]{2,1,0:T(8,128)(2,1)S(1)}, bf16[2,256,256]{2,1,0:T(8,128)(2,1)S(1)}, u32[]{:S(2)}, u32[]{:S(2)}) collective-permute-start(bf16[2,256,256]{2,1,0:T(8,128)(2,1)S(1)} %shard_map.42), channel_id=1, source_target_pairs={{0,3},{1,1},{2,2},{3,0},{4,7},{5,5},{6,6},{7,4},{8,11},{9,9},{10,1... | collective-permute-start | bytes 786440 | tf_op jit(solution)/shard_map/ppermute | solution.py:145

commit v3 on v2

v3 whole, which is shorter than its diff:
```python
import functools

import jax
import jax.numpy as jnp
from jax import lax
from jax.experimental import pallas as pl
from jax.experimental.pallas import tpu as pltpu
from jax.sharding import PartitionSpec as P

GROUP = 4
LOW, UPP, RHS = 0, 1, 2


def wide(block):
    real, imag = block[0], block[1]
    return jnp.concatenate(
        [jnp.concatenate([real, -imag], axis=1), jnp.concatenate([imag, real], axis=1)], axis=0
    )


def tall(block):
    return block.reshape(block.shape[0] * block.shape[1], block.shape[2])


def product(left, right):
    return jnp.dot(left, right, preferred_element_type=jnp.float32)


def low(value):
    return value.astype(jnp.bfloat16)


def parts(stacked):
    return stacked.reshape(2, stacked.shape[0] // 2, stacked.shape[1])


def beside(*blocks):
    return jnp.concatenate(blocks, axis=1)


def inverse_less_one(coupling):
    order = coupling.shape[1]
    first = low(coupling)
    second = product(wide(parts(first)), first)
    second_low = low(second)
    pair = product(wide(parts(second_low)), beside(second_low, first))
    fourth = low(pair[:, :order])
    short = coupling + second + pair[:, order:]
    whole = short + pair[:, :order] + product(wide(parts(low(short))), fourth)
    return low(whole)


def solved(spread, raw):
    return low(raw.astype(jnp.float32) + product(wide(spread), low(raw)))


def row_couplings(letter, own, near, far, new, spread):
    order = spread.shape[1]
    other = 1 - letter
    by_near = product(wide(own(letter)), beside(tall(near(other)), tall(near(letter))))
    by_far = product(wide(own(other)), beside(tall(far(letter)), tall(far(other))))
    spread[...] = parts(inverse_less_one(by_near[:, :order] + by_far[:, :order]))
    solution_of = spread[...]
    new[letter] = parts(solved(solution_of, -by_near[:, order:]))
    new[other] = parts(solved(solution_of, -by_far[:, order:]))


def row_injections(letter, own, spread, rhs, near, far):
    raw = tall(rhs).astype(jnp.float32) - product(wide(own(letter)), tall(near))
    return parts(solved(spread[...], raw - product(wide(own(1 - letter)), tall(far))))


def spot_of(length):
    return lax.axis_index("chain") % length


def near_kernel(own, near, half, half_rhs):
    order = near.shape[2]
    spot = spot_of(GROUP)
    kept = jnp.where(spot % 2 == 0, LOW, UPP)
    half[0] = own[kept]
    lead = wide(own[1 - kept])
    terms = product(lead, beside(tall(near[kept]), tall(near[1 - kept]), tall(near[RHS])))
    half[1] = parts(low(terms[:, :order]))
    half[2] = parts(low(-terms[:, order : 2 * order]))
    half_rhs[...] = parts(low(tall(own[RHS]).astype(jnp.float32) - terms[:, 2 * order :]))


def on_edge(there, here):
    spot = spot_of(GROUP)
    edge = (spot == 0) | (spot == GROUP - 1)
    return lambda place: jnp.where(edge, there[place], here[place])


def first_couplings_kernel(half_in, half_out, level, inner, new, spread):
    order = spread.shape[1]
    side = jnp.where(spot_of(GROUP) < GROUP // 2, UPP, LOW)
    half = on_edge(half_out, half_in)
    far = on_edge(level, inner)
    terms = product(wide(half(0)), beside(tall(far(1 - side)), tall(far(side))))
    spread[...] = parts(
        inverse_less_one(tall(half(1)).astype(jnp.float32) + terms[:, :order])
    )
    new[side] = parts(solved(spread[...], -terms[:, order:]))
    new[1 - side] = parts(solved(spread[...], tall(half(2))))


def first_injections_kernel(half_in, half_out, spread, rhs_in, rhs_out, level, inner, new):
    raw = tall(on_edge(rhs_out, rhs_in)(...)).astype(jnp.float32)
    lead = wide(on_edge(half_out, half_in)(0))
    raw = raw - product(lead, tall(on_edge(level, inner)(RHS)))
    new[...] = parts(solved(spread[...], raw))


def at(ref):
    return lambda place: ref[place]


def second_letter():
    return jnp.where(spot_of(GROUP) % 2 == 0, LOW, UPP)


def later_couplings_kernel(held, core, level, new, spread):
    row_couplings(second_letter(), at(held), at(core), at(level), new, spread)


def later_injections_kernel(held, spread, rhs, core, level, new):
    new[...] = row_injections(
        second_letter(), at(held), spread, rhs[...], core[...], level[...]
    )


def last_couplings_kernel(held, below_upper, above_lower, spread):
    coupling = product(wide(held[LOW]), tall(below_upper[...]))
    coupling = coupling + product(wide(held[UPP]), tall(above_lower[...]))
    spread[...] = parts(inverse_less_one(coupling))


def last_injections_kernel(held, spread, rhs, below, above, new):
    new[...] = row_injections(
        LOW, at(held), spread, rhs[...], below[...], above[...]
    )


def run(kernel, outs, *operands, weight=1):
    return pl.pallas_call(
        kernel,
        out_shape=[jax.ShapeDtypeStruct(s, jnp.bfloat16) for s in outs],
        in_specs=[pl.BlockSpec(memory_space=pltpu.VMEM)] * len(operands),
        out_specs=[pl.BlockSpec(memory_space=pltpu.VMEM)] * len(outs),
        compiler_params=pltpu.CompilerParams(vmem_limit_bytes=24 * 1024 * 1024),
        cost_estimate=pl.CostEstimate(flops=weight, bytes_accessed=1, transcendentals=0),
    )(*operands)


def local(length, lower, upper, right_side):
    block = lower.shape[1:]
    pair = (2,) + block
    groups = range(0, length, GROUP)

    def move(value, *pairs):
        moves = [(g + a, g + b) for g in groups for a, b in pairs]
        return lax.ppermute(
            value, "chain", [(a, b) for a, b in moves if 0 <= a < length and 0 <= b < length]
        )

    crossed = ((0, 3), (3, 0))
    inside = ((1, 2), (2, 1))
    levels = ((0, -GROUP), (3, 3 + GROUP))
    in_core = ((0, 1), (1, 0), (2, 3), (3, 2))
    between = ((0, 1 + GROUP), (1, -GROUP), (2, 3 + GROUP), (3, 2 - GROUP))
    upward = tuple((i, i + GROUP) for i in range(GROUP))
    downward = tuple((i, i - GROUP) for i in range(GROUP))
    home = ((0, 3), (1, 1), (2, 2), (3, 0))

    own = jnp.concatenate([lower, upper, right_side], axis=0)
    inner = move(own, *inside)
    near = move(own, *in_core)
    level = move(own, *levels)
    half, half_rhs = run(near_kernel, ((3,) + block, block), own, near)
    outer, outer_rhs = move(half, *crossed), move(half_rhs, *crossed)
    held, spread = run(first_couplings_kernel, (pair, block), half, outer, level, inner)
    (rhs,) = run(
        first_injections_kernel, (block,),
        half, outer, spread, half_rhs, outer_rhs, level, inner,
        weight=10**11,
    )

    core, level = move(held, *in_core), move(held, *between)
    core_rhs, level_rhs = move(rhs, *in_core), move(rhs, *between)
    new_held, spread = run(
        later_couplings_kernel, (pair, block), held, core, level
    )
    (rhs,) = run(
        later_injections_kernel, (block,),
        held, spread, rhs, core_rhs, level_rhs,
    )
    held = new_held

    below, above = move(held[UPP], *upward), move(held[LOW], *downward)
    below_rhs, above_rhs = move(rhs, *upward), move(rhs, *downward)
    (spread,) = run(last_couplings_kernel, (block,), held, below, above)
    (result,) = run(last_injections_kernel, (block,), held, spread, rhs, below_rhs, above_rhs)
    return move(result, *home)[None]


def solution(mesh):
    placed = P(("energy", "chain"), None, None, None)
    return jax.shard_map(
        functools.partial(local, mesh.shape["chain"]),
        mesh=mesh,
        in_specs=(placed,) * 3,
        out_specs=placed,
        check_vma=False,
    )
```

time: 73 us -> 66.1 us (0.905)
  starting transfers between devices: 34.5 us -> 31.5 us
  waiting for transfers between devices: 25.6 us -> 22.8 us
  Pallas kernels: 10.4 us -> 8.4 us
  local copies, waits for them, and re-layouts: 1.79 us -> 2.72 us
    ppermute x17 -> x14, starting transfers between devices: 34.5 us -> 31.5 us  [move(): lax.ppermute(value, 'chain', [(a, b) for a, b in moves if 0 <= a < length...]
    ppermute x17 -> x14, waiting for transfers between devices: 25.6 us -> 22.8 us  [move(): lax.ppermute(value, 'chain', [(a, b) for a, b in moves if 0 <= a < length...]
    pallas_call x6 -> x7, Pallas kernels: 10.4 us -> 8.4 us  [run(): pl.pallas_call(kernel, out_shape=[jax.ShapeDtypeStruct(s, jnp.bfloat16) f...]
    unnamed x6 -> x7, local copies, waits for them, and re-layouts: 1.73 us -> 2.66 us
  transfers between devices with their start and end apart: 17 -> 14, of which waited for: 7 -> 6; matrix products, arithmetic and copies ran while one was open for 0% -> 0% of each run, Pallas kernels for 13% -> 11%
where the time goes in v3:
time: 66.1 us; the launch traced here: 65.7 us
  starting transfers between devices  31.5 us (48%)
  waiting for transfers between devices  22.8 us (34%)
  Pallas kernels  8.4 us (13%)
  local copies, waits for them, and re-layouts  2.72 us (4%)
    ppermute x14, starting transfers between devices, move(): lax.ppermute(value, 'chain', [(a, b) for a, b in moves if 0 <= a < length...  31.5 us
    ppermute x14, waiting for transfers between devices, move(): lax.ppermute(value, 'chain', [(a, b) for a, b in moves if 0 <= a < length...  22.8 us
    pallas_call x7, Pallas kernels, run(): pl.pallas_call(kernel, out_shape=[jax.ShapeDtypeStruct(s, jnp.bfloat16) f...  8.4 us
    unnamed x7, local copies, waits for them, and re-layouts  2.66 us
  transfers between devices with their start and end apart: 14, of which 6 were waited for; matrix products, arithmetic and copies ran while one was open for 0% of the time, Pallas kernels for 11%

profile of v3, /device:TPU:0, one launch (start us, length us, event | category | flops | bytes accessed | tf_op | source)
XLA Modules:
  0.0 65.7 jit_solution(9771105643549349171)
XLA Ops:
  0.0 0.0 copy-start
  0.0 1.0 %constant_dynamic-update-slice_fusion.2 = bf16[3,2,256,256]{3,2,1,0:T(8,128)(2,1)S(1)} fusion(bf16[1,2,256,256]{3,2,1,0:T(8,128)(2,1)} %param.3), kind=kLoop, calls=%fused_computation.4 | loop fusion | bytes 524288
  1.0 0.0 copy-done
  1.0 0.0 copy-start.1
  1.1 0.9 %copy-done.1 = bf16[1,2,256,256]{3,2,1,0:T(8,128)(2,1)S(1)} copy-done((bf16[1,2,256,256]{3,2,1,0:T(8,128)(2,1)S(1)}, bf16[1,2,256,256]{3,2,1,0:T(8,128)(2,1)}, u32[]{:S(2)}) %copy-start.1) | copy-done | bytes 262168
  2.0 0.5 collective-permute-start
  2.5 0.7 %collective-permute-start.3 = (bf16[3,2,256,256]{3,2,1,0:T(8,128)(2,1)S(1)}, bf16[3,2,256,256]{3,2,1,0:T(8,128)(2,1)S(1)}, u32[]{:S(2)}, u32[]{:S(2)}) collective-permute-start(bf16[3,2,256,256]{3,2,1,0:T(8,128)(2,1)S(1)} %constant_dynamic-update-slice_fusion.own), channel_id=1, source_target_pairs={{1,2},{2,1},{5,6},{6,5},{9,10},{10,9},{13,14},{14,13},{17,18},{18,... | collective-permute-start | bytes 2359304 | tf_op jit(solution)/shard_map/ppermute | solution.py:163
  3.2 1.3 %collective-permute-start.2 = (bf16[3,2,256,256]{3,2,1,0:T(8,128)(2,1)S(1)}, bf16[3,2,256,256]{3,2,1,0:T(8,128)(2,1)S(1)}, u32[]{:S(2)}, u32[]{:S(2)}) collective-permute-start(bf16[3,2,256,256]{3,2,1,0:T(8,128)(2,1)S(1)} %constant_dynamic-update-slice_fusion.own), channel_id=1, source_target_pairs={{3,7},{4,0},{7,11},{8,4},{11,15},{12,8},{19,23},{20,16},{23,27},{2... | collective-permute-start | bytes 2359304 | tf_op jit(solution)/shard_map/ppermute | solution.py:163
  4.5 0.0 collective-permute-done.near
  4.5 0.6 shard_map.37
  5.2 6.5 %collective-permute-start.1 = (bf16[3,2,256,256]{3,2,1,0:T(8,128)(2,1)S(1)}, bf16[3,2,256,256]{3,2,1,0:T(8,128)(2,1)S(1)}, u32[]{:S(2)}, u32[]{:S(2)}) collective-permute-start(bf16[3,2,256,256]{3,2,1,0:T(8,128)(2,1)S(1)} %get-tuple-element.11.half_in), channel_id=1, source_target_pairs={{0,3},{3,0},{4,7},{7,4},{8,11},{11,8},{12,15},{15,12},{16,19},{19,... | collective-permute-start | bytes 2359304 | tf_op jit(solution)/shard_map/ppermute | solution.py:163
  11.7 1.9 %collective-permute-start.8 = (bf16[2,256,256]{2,1,0:T(8,128)(2,1)S(1)}, bf16[2,256,256]{2,1,0:T(8,128)(2,1)S(1)}, u32[]{:S(2)}, u32[]{:S(2)}) collective-permute-start(bf16[2,256,256]{2,1,0:T(8,128)(2,1)S(1)} %get-tuple-element.16.rhs_in), channel_id=1, source_target_pairs={{0,3},{3,0},{4,7},{7,4},{8,11},{11,8},{12,15},{15,12},{16,19},{19,... | collective-permute-start | bytes 786440 | tf_op jit(solution)/shard_map/ppermute | solution.py:163
  13.6 0.0 collective-permute-done.3.inner
  13.6 4.1 %collective-permute-done.2.level = bf16[3,2,256,256]{3,2,1,0:T(8,128)(2,1)S(1)} collective-permute-done((bf16[3,2,256,256]{3,2,1,0:T(8,128)(2,1)S(1)}, bf16[3,2,256,256]{3,2,1,0:T(8,128)(2,1)S(1)}, u32[]{:S(2)}, u32[]{:S(2)}) %collective-permute-start.2) | collective-permute-done | bytes 786464 | tf_op jit(solution)/shard_map/ppermute | solution.py:163
  17.7 7.7 %collective-permute-done.1.half_out = bf16[3,2,256,256]{3,2,1,0:T(8,128)(2,1)S(1)} collective-permute-done((bf16[3,2,256,256]{3,2,1,0:T(8,128)(2,1)S(1)}, bf16[3,2,256,256]{3,2,1,0:T(8,128)(2,1)S(1)}, u32[]{:S(2)}, u32[]{:S(2)}) %collective-permute-start.1) | collective-permute-done | bytes 786464 | tf_op jit(solution)/shard_map/ppermute | solution.py:163
  25.3 1.7 %shard_map.38 = (bf16[2,2,256,256]{3,2,1,0:T(8,128)(2,1)S(1)}, bf16[2,256,256]{2,1,0:T(8,128)(2,1)S(1)}) custom-call(bf16[3,2,256,256]{3,2,1,0:T(8,128)(2,1)S(1)} %get-tuple-element.11.half_in, bf16[3,2,256,256]{3,2,1,0:T(8,128)(2,1)S(1)} %collective-permute-done.1.half_out, bf16[3,2,256,256]{3,2,1,0:T(8,128)(2,1)S(1)} %collective-permute-done.2.level, ...), custom_call_target="tpu_custom_call" | custom-call | flops 1 | bytes 1 | tf_op jit(solution)/shard_map/pallas_call | solution.py:146
  27.0 1.9 %collective-permute-start.5 = (bf16[2,2,256,256]{3,2,1,0:T(8,128)(2,1)S(1)}, bf16[2,2,256,256]{3,2,1,0:T(8,128)(2,1)S(1)}, u32[]{:S(2)}, u32[]{:S(2)}) collective-permute-start(bf16[2,2,256,256]{3,2,1,0:T(8,128)(2,1)S(1)} %get-tuple-element.12.held), channel_id=1, source_target_pairs={{0,5},{2,7},{4,9},{5,0},{6,11},{7,2},{8,13},{9,4},{10,15},{11,6},{... | collective-permute-start | bytes 1572872 | tf_op jit(solution)/shard_map/ppermute | solution.py:163
  28.9 0.1 collective-permute-start.4
  29.0 0.0 collective-permute-done.8.rhs_out
  29.0 0.8 %shard_map.41.rhs = bf16[2,256,256]{2,1,0:T(8,128)(2,1)S(1)} custom-call(bf16[3,2,256,256]{3,2,1,0:T(8,128)(2,1)S(1)} %get-tuple-element.11.half_in, bf16[3,2,256,256]{3,2,1,0:T(8,128)(2,1)S(1)} %collective-permute-done.1.half_out, bf16[2,256,256]{2,1,0:T(8,128)(2,1)S(1)} %get-tuple-element.15.spread, bf16[2,256,256]{2,1,0:T(8,128)(2,1)S(1)} %get-tuple-element.16.rhs_in, ...), custom_call_target="tpu_custom_call" | custom-call | flops 99999997952 | bytes 1 | tf_op jit(solution)/shard_map/pallas_call | solution.py:146
  29.8 4.2 %collective-permute-start.10 = (bf16[2,256,256]{2,1,0:T(8,128)(2,1)S(1)}, bf16[2,256,256]{2,1,0:T(8,128)(2,1)S(1)}, u32[]{:S(2)}, u32[]{:S(2)}) collective-permute-start(bf16[2,256,256]{2,1,0:T(8,128)(2,1)S(1)} %shard_map.41.rhs), channel_id=1, source_target_pairs={{0,5},{2,7},{4,9},{5,0},{6,11},{7,2},{8,13},{9,4},{10,15},{11,6},{... | collective-permute-start | bytes 786440 | tf_op jit(solution)/shard_map/ppermute | solution.py:163
  34.0 0.1 collective-permute-start.9
  34.0 3.5 %collective-permute-done.5.level = bf16[2,2,256,256]{3,2,1,0:T(8,128)(2,1)S(1)} collective-permute-done((bf16[2,2,256,256]{3,2,1,0:T(8,128)(2,1)S(1)}, bf16[2,2,256,256]{3,2,1,0:T(8,128)(2,1)S(1)}, u32[]{:S(2)}, u32[]{:S(2)}) %collective-permute-start.5) | collective-permute-done | bytes 524320 | tf_op jit(solution)/shard_map/ppermute | solution.py:163
  37.5 0.0 collective-permute-done.4.core
  37.5 1.9 %shard_map.39 = (bf16[2,2,256,256]{3,2,1,0:T(8,128)(2,1)S(1)}, bf16[2,256,256]{2,1,0:T(8,128)(2,1)S(1)}) custom-call(bf16[2,2,256,256]{3,2,1,0:T(8,128)(2,1)S(1)} %get-tuple-element.12.held, bf16[2,2,256,256]{3,2,1,0:T(8,128)(2,1)S(1)} %collective-permute-done.4.core, bf16[2,2,256,256]{3,2,1,0:T(8,128)(2,1)S(1)} %collective-permute-done.5.level), custom_call_target="tpu_custom_call" | custom-call | flops 1 | bytes 1 | tf_op jit(solution)/shard_map/pallas_call | solution.py:146
  39.5 1.3 %collective-permute-start.7 = (bf16[2,256,256]{2,1,0:T(8,128)(2,1)S(1)}, bf16[2,256,256]{2,1,0:T(8,128)(2,1)S(1)}, u32[]{:S(2)}, u32[]{:S(2)}) collective-permute-start(bf16[2,256,256]{2,1,0:T(8,128)(2,1)S(1)} %get-tuple-element.17), channel_id=1, source_target_pairs={{4,0},{5,1},{6,2},{7,3},{8,4},{9,5},{10,6},{11,7},{12,8},{13,9},{1... | collective-permute-start | bytes 786440 | tf_op jit(solution)/shard_map/ppermute | solution.py:163
  40.8 4.7 %collective-permute-start.6 = (bf16[2,256,256]{2,1,0:T(8,128)(2,1)S(1)}, bf16[2,256,256]{2,1,0:T(8,128)(2,1)S(1)}, u32[]{:S(2)}, u32[]{:S(2)}) collective-permute-start(bf16[2,256,256]{2,1,0:T(8,128)(2,1)S(1)} %get-tuple-element.18), channel_id=1, source_target_pairs={{0,4},{1,5},{2,6},{3,7},{4,8},{5,9},{6,10},{7,11},{8,12},{9,13},{1... | collective-permute-start | bytes 786440 | tf_op jit(solution)/shard_map/ppermute | solution.py:163
  45.5 0.0 collective-permute-done.10.level
  45.5 0.0 collective-permute-done.9.core
  45.5 0.9 %shard_map.42.rhs = bf16[2,256,256]{2,1,0:T(8,128)(2,1)S(1)} custom-call(bf16[2,2,256,256]{3,2,1,0:T(8,128)(2,1)S(1)} %get-tuple-element.12.held, bf16[2,256,256]{2,1,0:T(8,128)(2,1)S(1)} %get-tuple-element.14.spread, bf16[2,256,256]{2,1,0:T(8,128)(2,1)S(1)} %shard_map.41.rhs, bf16[2,256,256]{2,1,0:T(8,128)(2,1)S(1)} %collective-permute-done.9.core, ...), custom_call_target="tpu_custom_call" | custom-call | flops 1 | bytes 1 | tf_op jit(solution)/shard_map/pallas_call | solution.py:146
  46.4 1.3 %collective-permute-start.12 = (bf16[2,256,256]{2,1,0:T(8,128)(2,1)S(1)}, bf16[2,256,256]{2,1,0:T(8,128)(2,1)S(1)}, u32[]{:S(2)}, u32[]{:S(2)}) collective-permute-start(bf16[2,256,256]{2,1,0:T(8,128)(2,1)S(1)} %shard_map.42.rhs), channel_id=1, source_target_pairs={{4,0},{5,1},{6,2},{7,3},{8,4},{9,5},{10,6},{11,7},{12,8},{13,9},{1... | collective-permute-start | bytes 786440 | tf_op jit(solution)/shard_map/ppermute | solution.py:163
  47.7 4.6 %collective-permute-start.11 = (bf16[2,256,256]{2,1,0:T(8,128)(2,1)S(1)}, bf16[2,256,256]{2,1,0:T(8,128)(2,1)S(1)}, u32[]{:S(2)}, u32[]{:S(2)}) collective-permute-start(bf16[2,256,256]{2,1,0:T(8,128)(2,1)S(1)} %shard_map.42.rhs), channel_id=1, source_target_pairs={{0,4},{1,5},{2,6},{3,7},{4,8},{5,9},{6,10},{7,11},{8,12},{9,13},{1... | collective-permute-start | bytes 786440 | tf_op jit(solution)/shard_map/ppermute | solution.py:163
  52.3 0.0 collective-permute-done.7.above_lower
  52.3 0.0 collective-permute-done.6.below_upper
  52.3 1.7 %shard_map.40.spread = bf16[2,256,256]{2,1,0:T(8,128)(2,1)S(1)} custom-call(bf16[2,2,256,256]{3,2,1,0:T(8,128)(2,1)S(1)} %get-tuple-element.13.held, bf16[2,256,256]{2,1,0:T(8,128)(2,1)S(1)} %collective-permute-done.6.below_upper, bf16[2,256,256]{2,1,0:T(8,128)(2,1)S(1)} %collective-permute-done.7.above_lower), custom_call_target="tpu_custom_call" | custom-call | flops 1 | bytes 1 | tf_op jit(solution)/shard_map/pallas_call | solution.py:146
  54.0 1.2 %collective-permute-done.12.above = bf16[2,256,256]{2,1,0:T(8,128)(2,1)S(1)} collective-permute-done((bf16[2,256,256]{2,1,0:T(8,128)(2,1)S(1)}, bf16[2,256,256]{2,1,0:T(8,128)(2,1)S(1)}, u32[]{:S(2)}, u32[]{:S(2)}) %collective-permute-start.12) | collective-permute-done | bytes 262176 | tf_op jit(solution)/shard_map/ppermute | solution.py:163
  55.2 1.2 %collective-permute-done.11.below = bf16[2,256,256]{2,1,0:T(8,128)(2,1)S(1)} collective-permute-done((bf16[2,256,256]{2,1,0:T(8,128)(2,1)S(1)}, bf16[2,256,256]{2,1,0:T(8,128)(2,1)S(1)}, u32[]{:S(2)}, u32[]{:S(2)}) %collective-permute-start.11) | collective-permute-done | bytes 262176 | tf_op jit(solution)/shard_map/ppermute | solution.py:163
  56.4 0.9 %shard_map.43 = bf16[2,256,256]{2,1,0:T(8,128)(2,1)S(1)} custom-call(bf16[2,2,256,256]{3,2,1,0:T(8,128)(2,1)S(1)} %get-tuple-element.13.held, bf16[2,256,256]{2,1,0:T(8,128)(2,1)S(1)} %shard_map.40.spread, bf16[2,256,256]{2,1,0:T(8,128)(2,1)S(1)} %shard_map.42.rhs, bf16[2,256,256]{2,1,0:T(8,128)(2,1)S(1)} %collective-permute-done.11.below, ...), custom_call_target="tpu_custom_call" | custom-call | flops 1 | bytes 1 | tf_op jit(solution)/shard_map/pallas_call | solution.py:146
  57.3 2.5 %collective-permute-start.13 = (bf16[2,256,256]{2,1,0:T(8,128)(2,1)S(1)}, bf16[2,256,256]{2,1,0:T(8,128)(2,1)S(1)}, u32[]{:S(2)}, u32[]{:S(2)}) collective-permute-start(bf16[2,256,256]{2,1,0:T(8,128)(2,1)S(1)} %shard_map.43), channel_id=1, source_target_pairs={{0,3},{1,1},{2,2},{3,0},{4,7},{5,5},{6,6},{7,4},{8,11},{9,9},{10,1... | collective-permute-start | bytes 786440 | tf_op jit(solution)/shard_map/ppermute | solution.py:163
  59.8 5.1 %collective-permute-done.13 = bf16[2,256,256]{2,1,0:T(8,128)(2,1)S(1)} collective-permute-done((bf16[2,256,256]{2,1,0:T(8,128)(2,1)S(1)}, bf16[2,256,256]{2,1,0:T(8,128)(2,1)S(1)}, u32[]{:S(2)}, u32[]{:S(2)}) %collective-permute-start.13) | collective-permute-done | bytes 262176 | tf_op jit(solution)/shard_map/ppermute | solution.py:163
  65.0 0.7 %copy.7 = bf16[1,2,256,256]{3,2,1,0:T(8,128)(2,1)} copy(bf16[1,2,256,256]{3,2,1,0:T(8,128)(2,1)S(1)} %bitcast.5) | data formatting | bytes 524288
  (3 shorter events, 0.1 us)
Async XLA Ops:
  0.0 1.0 %copy-start = (bf16[1,2,256,256]{3,2,1,0:T(8,128)(2,1)S(1)}, bf16[1,2,256,256]{3,2,1,0:T(8,128)(2,1)}, u32[]{:S(2)}) copy-start(bf16[1,2,256,256]{3,2,1,0:T(8,128)(2,1)} %param.4) | copy-start | bytes 786436
  1.0 0.9 %copy-start.1 = (bf16[1,2,256,256]{3,2,1,0:T(8,128)(2,1)S(1)}, bf16[1,2,256,256]{3,2,1,0:T(8,128)(2,1)}, u32[]{:S(2)}) copy-start(bf16[1,2,256,256]{3,2,1,0:T(8,128)(2,1)} %param.5) | copy-start | bytes 786436
  2.0 2.5 %collective-permute-start = (bf16[3,2,256,256]{3,2,1,0:T(8,128)(2,1)S(1)}, bf16[3,2,256,256]{3,2,1,0:T(8,128)(2,1)S(1)}, u32[]{:S(2)}, u32[]{:S(2)}) collective-permute-start(bf16[3,2,256,256]{3,2,1,0:T(8,128)(2,1)S(1)} %constant_dynamic-update-slice_fusion.own), channel_id=1, source_target_pairs={{0,1},{1,0},{2,3},{3,2},{4,5},{5,4},{6,7},{7,6},{8,9},{9,8},{10,11... | collective-permute-start | bytes 2359304 | tf_op jit(solution)/shard_map/ppermute | solution.py:163
  2.5 11.1 %collective-permute-start.3 = (bf16[3,2,256,256]{3,2,1,0:T(8,128)(2,1)S(1)}, bf16[3,2,256,256]{3,2,1,0:T(8,128)(2,1)S(1)}, u32[]{:S(2)}, u32[]{:S(2)}) collective-permute-start(bf16[3,2,256,256]{3,2,1,0:T(8,128)(2,1)S(1)} %constant_dynamic-update-slice_fusion.own), channel_id=1, source_target_pairs={{1,2},{2,1},{5,6},{6,5},{9,10},{10,9},{13,14},{14,13},{17,18},{18,... | collective-permute-start | bytes 2359304 | tf_op jit(solution)/shard_map/ppermute | solution.py:163
  3.2 14.5 %collective-permute-start.2 = (bf16[3,2,256,256]{3,2,1,0:T(8,128)(2,1)S(1)}, bf16[3,2,256,256]{3,2,1,0:T(8,128)(2,1)S(1)}, u32[]{:S(2)}, u32[]{:S(2)}) collective-permute-start(bf16[3,2,256,256]{3,2,1,0:T(8,128)(2,1)S(1)} %constant_dynamic-update-slice_fusion.own), channel_id=1, source_target_pairs={{3,7},{4,0},{7,11},{8,4},{11,15},{12,8},{19,23},{20,16},{23,27},{2... | collective-permute-start | bytes 2359304 | tf_op jit(solution)/shard_map/ppermute | solution.py:163
  5.2 20.2 %collective-permute-start.1 = (bf16[3,2,256,256]{3,2,1,0:T(8,128)(2,1)S(1)}, bf16[3,2,256,256]{3,2,1,0:T(8,128)(2,1)S(1)}, u32[]{:S(2)}, u32[]{:S(2)}) collective-permute-start(bf16[3,2,256,256]{3,2,1,0:T(8,128)(2,1)S(1)} %get-tuple-element.11.half_in), channel_id=1, source_target_pairs={{0,3},{3,0},{4,7},{7,4},{8,11},{11,8},{12,15},{15,12},{16,19},{19,... | collective-permute-start | bytes 2359304 | tf_op jit(solution)/shard_map/ppermute | solution.py:163
  11.7 17.4 %collective-permute-start.8 = (bf16[2,256,256]{2,1,0:T(8,128)(2,1)S(1)}, bf16[2,256,256]{2,1,0:T(8,128)(2,1)S(1)}, u32[]{:S(2)}, u32[]{:S(2)}) collective-permute-start(bf16[2,256,256]{2,1,0:T(8,128)(2,1)S(1)} %get-tuple-element.16.rhs_in), channel_id=1, source_target_pairs={{0,3},{3,0},{4,7},{7,4},{8,11},{11,8},{12,15},{15,12},{16,19},{19,... | collective-permute-start | bytes 786440 | tf_op jit(solution)/shard_map/ppermute | solution.py:163
  27.0 10.5 %collective-permute-start.5 = (bf16[2,2,256,256]{3,2,1,0:T(8,128)(2,1)S(1)}, bf16[2,2,256,256]{3,2,1,0:T(8,128)(2,1)S(1)}, u32[]{:S(2)}, u32[]{:S(2)}) collective-permute-start(bf16[2,2,256,256]{3,2,1,0:T(8,128)(2,1)S(1)} %get-tuple-element.12.held), channel_id=1, source_target_pairs={{0,5},{2,7},{4,9},{5,0},{6,11},{7,2},{8,13},{9,4},{10,15},{11,6},{... | collective-permute-start | bytes 1572872 | tf_op jit(solution)/shard_map/ppermute | solution.py:163
  28.9 8.6 %collective-permute-start.4 = (bf16[2,2,256,256]{3,2,1,0:T(8,128)(2,1)S(1)}, bf16[2,2,256,256]{3,2,1,0:T(8,128)(2,1)S(1)}, u32[]{:S(2)}, u32[]{:S(2)}) collective-permute-start(bf16[2,2,256,256]{3,2,1,0:T(8,128)(2,1)S(1)} %get-tuple-element.12.held), channel_id=1, source_target_pairs={{0,1},{1,0},{2,3},{3,2},{4,5},{5,4},{6,7},{7,6},{8,9},{9,8},{10,11... | collective-permute-start | bytes 1572872 | tf_op jit(solution)/shard_map/ppermute | solution.py:163
  29.8 15.7 %collective-permute-start.10 = (bf16[2,256,256]{2,1,0:T(8,128)(2,1)S(1)}, bf16[2,256,256]{2,1,0:T(8,128)(2,1)S(1)}, u32[]{:S(2)}, u32[]{:S(2)}) collective-permute-start(bf16[2,256,256]{2,1,0:T(8,128)(2,1)S(1)} %shard_map.41.rhs), channel_id=1, source_target_pairs={{0,5},{2,7},{4,9},{5,0},{6,11},{7,2},{8,13},{9,4},{10,15},{11,6},{... | collective-permute-start | bytes 786440 | tf_op jit(solution)/shard_map/ppermute | solution.py:163
  34.0 11.6 %collective-permute-start.9 = (bf16[2,256,256]{2,1,0:T(8,128)(2,1)S(1)}, bf16[2,256,256]{2,1,0:T(8,128)(2,1)S(1)}, u32[]{:S(2)}, u32[]{:S(2)}) collective-permute-start(bf16[2,256,256]{2,1,0:T(8,128)(2,1)S(1)} %shard_map.41.rhs), channel_id=1, source_target_pairs={{0,1},{1,0},{2,3},{3,2},{4,5},{5,4},{6,7},{7,6},{8,9},{9,8},{10,11... | collective-permute-start | bytes 786440 | tf_op jit(solution)/shard_map/ppermute | solution.py:163
  39.5 12.8 %collective-permute-start.7 = (bf16[2,256,256]{2,1,0:T(8,128)(2,1)S(1)}, bf16[2,256,256]{2,1,0:T(8,128)(2,1)S(1)}, u32[]{:S(2)}, u32[]{:S(2)}) collective-permute-start(bf16[2,256,256]{2,1,0:T(8,128)(2,1)S(1)} %get-tuple-element.17), channel_id=1, source_target_pairs={{4,0},{5,1},{6,2},{7,3},{8,4},{9,5},{10,6},{11,7},{12,8},{13,9},{1... | collective-permute-start | bytes 786440 | tf_op jit(solution)/shard_map/ppermute | solution.py:163
  40.8 11.5 %collective-permute-start.6 = (bf16[2,256,256]{2,1,0:T(8,128)(2,1)S(1)}, bf16[2,256,256]{2,1,0:T(8,128)(2,1)S(1)}, u32[]{:S(2)}, u32[]{:S(2)}) collective-permute-start(bf16[2,256,256]{2,1,0:T(8,128)(2,1)S(1)} %get-tuple-element.18), channel_id=1, source_target_pairs={{0,4},{1,5},{2,6},{3,7},{4,8},{5,9},{6,10},{7,11},{8,12},{9,13},{1... | collective-permute-start | bytes 786440 | tf_op jit(solution)/shard_map/ppermute | solution.py:163
  46.4 8.8 %collective-permute-start.12 = (bf16[2,256,256]{2,1,0:T(8,128)(2,1)S(1)}, bf16[2,256,256]{2,1,0:T(8,128)(2,1)S(1)}, u32[]{:S(2)}, u32[]{:S(2)}) collective-permute-start(bf16[2,256,256]{2,1,0:T(8,128)(2,1)S(1)} %shard_map.42.rhs), channel_id=1, source_target_pairs={{4,0},{5,1},{6,2},{7,3},{8,4},{9,5},{10,6},{11,7},{12,8},{13,9},{1... | collective-permute-start | bytes 786440 | tf_op jit(solution)/shard_map/ppermute | solution.py:163
  47.7 8.7 %collective-permute-start.11 = (bf16[2,256,256]{2,1,0:T(8,128)(2,1)S(1)}, bf16[2,256,256]{2,1,0:T(8,128)(2,1)S(1)}, u32[]{:S(2)}, u32[]{:S(2)}) collective-permute-start(bf16[2,256,256]{2,1,0:T(8,128)(2,1)S(1)} %shard_map.42.rhs), channel_id=1, source_target_pairs={{0,4},{1,5},{2,6},{3,7},{4,8},{5,9},{6,10},{7,11},{8,12},{9,13},{1... | collective-permute-start | bytes 786440 | tf_op jit(solution)/shard_map/ppermute | solution.py:163
  57.3 7.7 %collective-permute-start.13 = (bf16[2,256,256]{2,1,0:T(8,128)(2,1)S(1)}, bf16[2,256,256]{2,1,0:T(8,128)(2,1)S(1)}, u32[]{:S(2)}, u32[]{:S(2)}) collective-permute-start(bf16[2,256,256]{2,1,0:T(8,128)(2,1)S(1)} %shard_map.43), channel_id=1, source_target_pairs={{0,3},{1,1},{2,2},{3,0},{4,7},{5,5},{6,6},{7,4},{8,11},{9,9},{10,1... | collective-permute-start | bytes 786440 | tf_op jit(solution)/shard_map/ppermute | solution.py:163

commit v4 on v3

--- a/solution.py
+++ b/solution.py
@@ -74,42 +74,40 @@
     return lax.axis_index("chain") % length
 
 
-def near_kernel(own, near, half, half_rhs):
-    order = near.shape[2]
-    spot = spot_of(GROUP)
-    kept = jnp.where(spot % 2 == 0, LOW, UPP)
-    half[0] = own[kept]
-    lead = wide(own[1 - kept])
-    terms = product(lead, beside(tall(near[kept]), tall(near[1 - kept]), tall(near[RHS])))
-    half[1] = parts(low(terms[:, :order]))
-    half[2] = parts(low(-terms[:, order : 2 * order]))
-    half_rhs[...] = parts(low(tall(own[RHS]).astype(jnp.float32) - terms[:, 2 * order :]))
-
-
 def on_edge(there, here):
     spot = spot_of(GROUP)
-    edge = (spot == 0) | (spot == GROUP - 1)
+    edge = (spot == 1) | (spot == 2)
     return lambda place: jnp.where(edge, there[place], here[place])
 
 
-def first_couplings_kernel(half_in, half_out, level, inner, new, spread):
-    order = spread.shape[1]
-    side = jnp.where(spot_of(GROUP) < GROUP // 2, UPP, LOW)
-    half = on_edge(half_out, half_in)
-    far = on_edge(level, inner)
-    terms = product(wide(half(0)), beside(tall(far(1 - side)), tall(far(side))))
-    spread[...] = parts(
-        inverse_less_one(tall(half(1)).astype(jnp.float32) + terms[:, :order])
-    )
-    new[side] = parts(solved(spread[...], -terms[:, order:]))
-    new[1 - side] = parts(solved(spread[...], tall(half(2))))
-
-
-def first_injections_kernel(half_in, half_out, spread, rhs_in, rhs_out, level, inner, new):
-    raw = tall(on_edge(rhs_out, rhs_in)(...)).astype(jnp.float32)
-    lead = wide(on_edge(half_out, half_in)(0))
-    raw = raw - product(lead, tall(on_edge(level, inner)(RHS)))
-    new[...] = parts(solved(spread[...], raw))
+def first_letter():
+    return jnp.where(spot_of(GROUP) < GROUP // 2, LOW, UPP)
+
+
+def pack_kernel(held, rhs, packed):
+    packed[:2] = held[...]
+    packed[2] = rhs[...]
+
+
+def first_couplings_kernel(held, crossed, core, onward, level, new, spread):
+    row_couplings(
+        first_letter(),
+        on_edge(crossed, core), on_edge(onward, held), on_edge(level, crossed),
+        new, spread,
+    )
+
+
+def first_injections_kernel(
+    crossed, spread, rhs, crossed_rhs, core, onward_rhs, level, new
+):
+    spot = spot_of(GROUP)
+    edge = (spot == 1) | (spot == 2)
+    own_rhs = jnp.where(edge, crossed_rhs[...], core[RHS])
+    near = jnp.where(edge, onward_rhs[...], rhs[...])
+    far = jnp.where(edge, level[RHS], crossed_rhs[...])
+    new[...] = row_injections(
+        first_letter(), on_edge(crossed, core), spread, own_rhs, near, far
+    )
 
 
 def at(ref):
@@ -117,7 +115,7 @@
 
 
 def second_letter():
-    return jnp.where(spot_of(GROUP) % 2 == 0, LOW, UPP)
+    return jnp.where(spot_of(GROUP) % 2 == 0, UPP, LOW)
 
 
 def later_couplings_kernel(held, core, level, new, spread):
@@ -164,27 +162,34 @@
             value, "chain", [(a, b) for a, b in moves if 0 <= a < length and 0 <= b < length]
         )
 
-    crossed = ((0, 3), (3, 0))
-    inside = ((1, 2), (2, 1))
-    levels = ((0, -GROUP), (3, 3 + GROUP))
+    mirrored = ((0, 2), (1, 3), (2, 0), (3, 1))
+    inward = ((1, 0), (2, 3))
+    outward = ((0, 1), (3, 2))
+    levels = ((0, 1 - GROUP), (3, 2 + GROUP))
     in_core = ((0, 1), (1, 0), (2, 3), (3, 2))
-    between = ((0, 1 + GROUP), (1, -GROUP), (2, 3 + GROUP), (3, 2 - GROUP))
+    between = ((0, 1 - GROUP), (1, GROUP), (2, 3 - GROUP), (3, 2 + GROUP))
     upward = tuple((i, i + GROUP) for i in range(GROUP))
     downward = tuple((i, i - GROUP) for i in range(GROUP))
-    home = ((0, 3), (1, 1), (2, 2), (3, 0))
-
-    own = jnp.concatenate([lower, upper, right_side], axis=0)
-    inner = move(own, *inside)
-    near = move(own, *in_core)
-    level = move(own, *levels)
-    half, half_rhs = run(near_kernel, ((3,) + block, block), own, near)
-    outer, outer_rhs = move(half, *crossed), move(half_rhs, *crossed)
-    held, spread = run(first_couplings_kernel, (pair, block), half, outer, level, inner)
+    home = ((0, 1), (1, 3), (2, 0), (3, 2))
+
+    held = jnp.concatenate([lower, upper], axis=0)
+    rhs = right_side[0]
+    crossed = move(held, *mirrored)
+    (packed,) = run(pack_kernel, ((3,) + block,), held, rhs)
+    level = move(packed, *levels)
+    core = move(packed, *inward)
+    crossed_rhs = move(rhs, *mirrored)
+    onward = move(crossed, *outward)
+    onward_rhs = move(crossed_rhs, *outward)
+    new_held, spread = run(
+        first_couplings_kernel, (pair, block), held, crossed, core, onward, level, weight=1
+    )
     (rhs,) = run(
         first_injections_kernel, (block,),
-        half, outer, spread, half_rhs, outer_rhs, level, inner,
-        weight=10**11,
-    )
+        crossed, spread, rhs, crossed_rhs, core, onward_rhs, level,
+        weight=1,
+    )
+    held = new_held
 
     core, level = move(held, *in_core), move(held, *between)
     core_rhs, level_rhs = move(rhs, *in_core), move(rhs, *between)

time: 66.1 us -> 62.3 us (0.943)
  starting transfers between devices: 31.5 us -> 29.4 us
  local copies, waits for them, and re-layouts: 2.72 us -> 1.79 us
    ppermute x14 -> x15, starting transfers between devices: 31.5 us -> 29.4 us  [move(): lax.ppermute(value, 'chain', [(a, b) for a, b in moves if 0 <= a < length...]
    unnamed x7 -> x6, local copies, waits for them, and re-layouts: 2.66 us -> 1.73 us
    ppermute x14 -> x15, waiting for transfers between devices: 22.8 us -> 22.2 us  [move(): lax.ppermute(value, 'chain', [(a, b) for a, b in moves if 0 <= a < length...]
  transfers between devices with their start and end apart: 14 -> 15, of which waited for: 6 -> 6; matrix products, arithmetic and copies ran while one was open for 0% -> 0% of each run, Pallas kernels for 11% -> 12%
where the time goes in v4:
time: 62.3 us; the launch traced here: 61.9 us
  starting transfers between devices  29.4 us (47%)
  waiting for transfers between devices  22.2 us (36%)
  Pallas kernels  8.28 us (13%)
  local copies, waits for them, and re-layouts  1.79 us (3%)
    ppermute x15, starting transfers between devices, move(): lax.ppermute(value, 'chain', [(a, b) for a, b in moves if 0 <= a < length...  29.4 us
    ppermute x15, waiting for transfers between devices, move(): lax.ppermute(value, 'chain', [(a, b) for a, b in moves if 0 <= a < length...  22.2 us
    pallas_call x7, Pallas kernels, run(): pl.pallas_call(kernel, out_shape=[jax.ShapeDtypeStruct(s, jnp.bfloat16) f...  8.28 us
    unnamed x6, local copies, waits for them, and re-layouts  1.73 us
  transfers between devices with their start and end apart: 15, of which 6 were waited for; matrix products, arithmetic and copies ran while one was open for 0% of the time, Pallas kernels for 12%

profile of v4, /device:TPU:0, one launch (start us, length us, event | category | flops | bytes accessed | tf_op | source)
XLA Modules:
  0.0 61.9 jit_solution(6082165188327606871)
XLA Ops:
  0.0 0.0 copy-start.1
  0.0 1.0 %constant_dynamic-update-slice_fusion.1 = bf16[2,2,256,256]{3,2,1,0:T(8,128)(2,1)S(1)} fusion(bf16[1,2,256,256]{3,2,1,0:T(8,128)(2,1)} %param.3), kind=kLoop, calls=%fused_computation.3 | loop fusion | bytes 524288
  1.0 0.0 copy-done.1
  1.0 0.0 copy-start
  1.1 3.0 %collective-permute-start = (bf16[2,2,256,256]{3,2,1,0:T(8,128)(2,1)S(1)}, bf16[2,2,256,256]{3,2,1,0:T(8,128)(2,1)S(1)}, u32[]{:S(2)}, u32[]{:S(2)}) collective-permute-start(bf16[2,2,256,256]{3,2,1,0:T(8,128)(2,1)S(1)} %constant_dynamic-update-slice_fusion.held), channel_id=1, source_target_pairs={{0,2},{1,3},{2,0},{3,1},{4,6},{5,7},{6,4},{7,5},{8,10},{9,11},{10,... | collective-permute-start | bytes 1572872 | tf_op jit(solution)/shard_map/ppermute | solution.py:161
  4.1 0.0 copy-done
  4.1 0.1 shard_map.37
  4.2 0.7 %collective-permute-start.3 = (bf16[3,2,256,256]{3,2,1,0:T(8,128)(2,1)S(1)}, bf16[3,2,256,256]{3,2,1,0:T(8,128)(2,1)S(1)}, u32[]{:S(2)}, u32[]{:S(2)}) collective-permute-start(bf16[3,2,256,256]{3,2,1,0:T(8,128)(2,1)S(1)} %shard_map.37), channel_id=1, source_target_pairs={{3,6},{4,1},{7,10},{8,5},{11,14},{12,9},{19,22},{20,17},{23,26},{2... | collective-permute-start | bytes 2359304 | tf_op jit(solution)/shard_map/ppermute | solution.py:161
  4.9 1.3 %collective-permute-start.1 = (bf16[3,2,256,256]{3,2,1,0:T(8,128)(2,1)S(1)}, bf16[3,2,256,256]{3,2,1,0:T(8,128)(2,1)S(1)}, u32[]{:S(2)}, u32[]{:S(2)}) collective-permute-start(bf16[3,2,256,256]{3,2,1,0:T(8,128)(2,1)S(1)} %shard_map.37), channel_id=1, source_target_pairs={{1,0},{2,3},{5,4},{6,7},{9,8},{10,11},{13,12},{14,15},{17,16},{18,... | collective-permute-start | bytes 2359304 | tf_op jit(solution)/shard_map/ppermute | solution.py:161
  6.2 9.8 %collective-permute-done.crossed = bf16[2,2,256,256]{3,2,1,0:T(8,128)(2,1)S(1)} collective-permute-done((bf16[2,2,256,256]{3,2,1,0:T(8,128)(2,1)S(1)}, bf16[2,2,256,256]{3,2,1,0:T(8,128)(2,1)S(1)}, u32[]{:S(2)}, u32[]{:S(2)}) %collective-permute-start) | collective-permute-done | bytes 524320 | tf_op jit(solution)/shard_map/ppermute | solution.py:161
  16.0 1.3 %collective-permute-start.2 = (bf16[2,2,256,256]{3,2,1,0:T(8,128)(2,1)S(1)}, bf16[2,2,256,256]{3,2,1,0:T(8,128)(2,1)S(1)}, u32[]{:S(2)}, u32[]{:S(2)}) collective-permute-start(bf16[2,2,256,256]{3,2,1,0:T(8,128)(2,1)S(1)} %collective-permute-done.crossed), channel_id=1, source_target_pairs={{0,1},{3,2},{4,5},{7,6},{8,9},{11,10},{12,13},{15,14},{16,17},{19,... | collective-permute-start | bytes 1572872 | tf_op jit(solution)/shard_map/ppermute | solution.py:161
  17.3 1.8 %collective-permute-start.8 = (bf16[2,256,256]{2,1,0:T(8,128)(2,1)S(1)}, bf16[2,256,256]{2,1,0:T(8,128)(2,1)S(1)}, u32[]{:S(2)}, u32[]{:S(2)}) collective-permute-start(bf16[2,256,256]{2,1,0:T(8,128)(2,1)S(1)} %bitcast.7), channel_id=1, source_target_pairs={{0,2},{1,3},{2,0},{3,1},{4,6},{5,7},{6,4},{7,5},{8,10},{9,11},{10,... | collective-permute-start | bytes 786440 | tf_op jit(solution)/shard_map/ppermute | solution.py:161
  19.1 0.0 collective-permute-done.3.level
  19.1 0.0 collective-permute-done.1.core
  19.1 0.0 collective-permute-done.2.onward
  19.1 1.9 %shard_map.38 = (bf16[2,2,256,256]{3,2,1,0:T(8,128)(2,1)S(1)}, bf16[2,256,256]{2,1,0:T(8,128)(2,1)S(1)}) custom-call(bf16[2,2,256,256]{3,2,1,0:T(8,128)(2,1)S(1)} %constant_dynamic-update-slice_fusion.held, bf16[2,2,256,256]{3,2,1,0:T(8,128)(2,1)S(1)} %collective-permute-done.crossed, bf16[3,2,256,256]{3,2,1,0:T(8,128)(2,1)S(1)} %collective-permute-done.1.core, ...), custom_call_target="tpu_custom_call" | custom-call | flops 1 | bytes 1 | tf_op jit(solution)/shard_map/pallas_call | solution.py:144
  21.1 0.7 %collective-permute-start.5 = (bf16[2,2,256,256]{3,2,1,0:T(8,128)(2,1)S(1)}, bf16[2,2,256,256]{3,2,1,0:T(8,128)(2,1)S(1)}, u32[]{:S(2)}, u32[]{:S(2)}) collective-permute-start(bf16[2,2,256,256]{3,2,1,0:T(8,128)(2,1)S(1)} %get-tuple-element.9.held), channel_id=1, source_target_pairs={{1,4},{3,6},{4,1},{5,8},{6,3},{7,10},{8,5},{9,12},{10,7},{11,14},{... | collective-permute-start | bytes 1572872 | tf_op jit(solution)/shard_map/ppermute | solution.py:161
  21.8 3.0 %collective-permute-start.4 = (bf16[2,2,256,256]{3,2,1,0:T(8,128)(2,1)S(1)}, bf16[2,2,256,256]{3,2,1,0:T(8,128)(2,1)S(1)}, u32[]{:S(2)}, u32[]{:S(2)}) collective-permute-start(bf16[2,2,256,256]{3,2,1,0:T(8,128)(2,1)S(1)} %get-tuple-element.9.held), channel_id=1, source_target_pairs={{0,1},{1,0},{2,3},{3,2},{4,5},{5,4},{6,7},{7,6},{8,9},{9,8},{10,11... | collective-permute-start | bytes 1572872 | tf_op jit(solution)/shard_map/ppermute | solution.py:161
  24.8 1.7 %collective-permute-done.8.crossed_rhs = bf16[2,256,256]{2,1,0:T(8,128)(2,1)S(1)} collective-permute-done((bf16[2,256,256]{2,1,0:T(8,128)(2,1)S(1)}, bf16[2,256,256]{2,1,0:T(8,128)(2,1)S(1)}, u32[]{:S(2)}, u32[]{:S(2)}) %collective-permute-start.8) | collective-permute-done | bytes 262176 | tf_op jit(solution)/shard_map/ppermute | solution.py:161
  26.4 2.0 %collective-permute-start.9 = (bf16[2,256,256]{2,1,0:T(8,128)(2,1)S(1)}, bf16[2,256,256]{2,1,0:T(8,128)(2,1)S(1)}, u32[]{:S(2)}, u32[]{:S(2)}) collective-permute-start(bf16[2,256,256]{2,1,0:T(8,128)(2,1)S(1)} %collective-permute-done.8.crossed_rhs), channel_id=1, source_target_pairs={{0,1},{3,2},{4,5},{7,6},{8,9},{11,10},{12,13},{15,14},{16,17},{19,... | collective-permute-start | bytes 786440 | tf_op jit(solution)/shard_map/ppermute | solution.py:161
  28.5 1.1 %collective-permute-done.9.onward_rhs = bf16[2,256,256]{2,1,0:T(8,128)(2,1)S(1)} collective-permute-done((bf16[2,256,256]{2,1,0:T(8,128)(2,1)S(1)}, bf16[2,256,256]{2,1,0:T(8,128)(2,1)S(1)}, u32[]{:S(2)}, u32[]{:S(2)}) %collective-permute-start.9) | collective-permute-done | bytes 262176 | tf_op jit(solution)/shard_map/ppermute | solution.py:161
  29.6 0.9 %shard_map.41.rhs = bf16[2,256,256]{2,1,0:T(8,128)(2,1)S(1)} custom-call(bf16[2,2,256,256]{3,2,1,0:T(8,128)(2,1)S(1)} %collective-permute-done.crossed, bf16[2,256,256]{2,1,0:T(8,128)(2,1)S(1)} %get-tuple-element.12.spread, bf16[2,256,256]{2,1,0:T(8,128)(2,1)S(1)} %bitcast.8, bf16[2,256,256]{2,1,0:T(8,128)(2,1)S(1)} %collective-permute-done.8.crossed_rhs, ...), custom_call_target="tpu_custom_call" | custom-call | flops 1 | bytes 1 | tf_op jit(solution)/shard_map/pallas_call | solution.py:144
  30.5 0.7 %collective-permute-start.11 = (bf16[2,256,256]{2,1,0:T(8,128)(2,1)S(1)}, bf16[2,256,256]{2,1,0:T(8,128)(2,1)S(1)}, u32[]{:S(2)}, u32[]{:S(2)}) collective-permute-start(bf16[2,256,256]{2,1,0:T(8,128)(2,1)S(1)} %shard_map.41.rhs), channel_id=1, source_target_pairs={{1,4},{3,6},{4,1},{5,8},{6,3},{7,10},{8,5},{9,12},{10,7},{11,14},{... | collective-permute-start | bytes 786440 | tf_op jit(solution)/shard_map/ppermute | solution.py:161
  31.2 3.2 %collective-permute-start.10 = (bf16[2,256,256]{2,1,0:T(8,128)(2,1)S(1)}, bf16[2,256,256]{2,1,0:T(8,128)(2,1)S(1)}, u32[]{:S(2)}, u32[]{:S(2)}) collective-permute-start(bf16[2,256,256]{2,1,0:T(8,128)(2,1)S(1)} %shard_map.41.rhs), channel_id=1, source_target_pairs={{0,1},{1,0},{2,3},{3,2},{4,5},{5,4},{6,7},{7,6},{8,9},{9,8},{10,11... | collective-permute-start | bytes 786440 | tf_op jit(solution)/shard_map/ppermute | solution.py:161
  34.4 0.0 collective-permute-done.5.level
  34.4 0.0 collective-permute-done.4.core
  34.4 1.9 %shard_map.39 = (bf16[2,2,256,256]{3,2,1,0:T(8,128)(2,1)S(1)}, bf16[2,256,256]{2,1,0:T(8,128)(2,1)S(1)}) custom-call(bf16[2,2,256,256]{3,2,1,0:T(8,128)(2,1)S(1)} %get-tuple-element.9.held, bf16[2,2,256,256]{3,2,1,0:T(8,128)(2,1)S(1)} %collective-permute-done.4.core, bf16[2,2,256,256]{3,2,1,0:T(8,128)(2,1)S(1)} %collective-permute-done.5.level), custom_call_target="tpu_custom_call" | custom-call | flops 1 | bytes 1 | tf_op jit(solution)/shard_map/pallas_call | solution.py:144
  36.4 1.3 %collective-permute-start.7 = (bf16[2,256,256]{2,1,0:T(8,128)(2,1)S(1)}, bf16[2,256,256]{2,1,0:T(8,128)(2,1)S(1)}, u32[]{:S(2)}, u32[]{:S(2)}) collective-permute-start(bf16[2,256,256]{2,1,0:T(8,128)(2,1)S(1)} %get-tuple-element.13), channel_id=1, source_target_pairs={{4,0},{5,1},{6,2},{7,3},{8,4},{9,5},{10,6},{11,7},{12,8},{13,9},{1... | collective-permute-start | bytes 786440 | tf_op jit(solution)/shard_map/ppermute | solution.py:161
  37.7 4.6 %collective-permute-start.6 = (bf16[2,256,256]{2,1,0:T(8,128)(2,1)S(1)}, bf16[2,256,256]{2,1,0:T(8,128)(2,1)S(1)}, u32[]{:S(2)}, u32[]{:S(2)}) collective-permute-start(bf16[2,256,256]{2,1,0:T(8,128)(2,1)S(1)} %get-tuple-element.14), channel_id=1, source_target_pairs={{0,4},{1,5},{2,6},{3,7},{4,8},{5,9},{6,10},{7,11},{8,12},{9,13},{1... | collective-permute-start | bytes 786440 | tf_op jit(solution)/shard_map/ppermute | solution.py:161
  42.3 0.0 collective-permute-done.11.level
  42.3 0.0 collective-permute-done.10.core
  42.3 0.9 %shard_map.42.rhs = bf16[2,256,256]{2,1,0:T(8,128)(2,1)S(1)} custom-call(bf16[2,2,256,256]{3,2,1,0:T(8,128)(2,1)S(1)} %get-tuple-element.9.held, bf16[2,256,256]{2,1,0:T(8,128)(2,1)S(1)} %get-tuple-element.11.spread, bf16[2,256,256]{2,1,0:T(8,128)(2,1)S(1)} %shard_map.41.rhs, bf16[2,256,256]{2,1,0:T(8,128)(2,1)S(1)} %collective-permute-done.10.core, ...), custom_call_target="tpu_custom_call" | custom-call | flops 1 | bytes 1 | tf_op jit(solution)/shard_map/pallas_call | solution.py:144
  43.2 1.3 %collective-permute-start.13 = (bf16[2,256,256]{2,1,0:T(8,128)(2,1)S(1)}, bf16[2,256,256]{2,1,0:T(8,128)(2,1)S(1)}, u32[]{:S(2)}, u32[]{:S(2)}) collective-permute-start(bf16[2,256,256]{2,1,0:T(8,128)(2,1)S(1)} %shard_map.42.rhs), channel_id=1, source_target_pairs={{4,0},{5,1},{6,2},{7,3},{8,4},{9,5},{10,6},{11,7},{12,8},{13,9},{1... | collective-permute-start | bytes 786440 | tf_op jit(solution)/shard_map/ppermute | solution.py:161
  44.5 4.6 %collective-permute-start.12 = (bf16[2,256,256]{2,1,0:T(8,128)(2,1)S(1)}, bf16[2,256,256]{2,1,0:T(8,128)(2,1)S(1)}, u32[]{:S(2)}, u32[]{:S(2)}) collective-permute-start(bf16[2,256,256]{2,1,0:T(8,128)(2,1)S(1)} %shard_map.42.rhs), channel_id=1, source_target_pairs={{0,4},{1,5},{2,6},{3,7},{4,8},{5,9},{6,10},{7,11},{8,12},{9,13},{1... | collective-permute-start | bytes 786440 | tf_op jit(solution)/shard_map/ppermute | solution.py:161
  49.1 0.0 collective-permute-done.7.above_lower
  49.1 0.0 collective-permute-done.6.below_upper
  49.1 1.7 %shard_map.40.spread = bf16[2,256,256]{2,1,0:T(8,128)(2,1)S(1)} custom-call(bf16[2,2,256,256]{3,2,1,0:T(8,128)(2,1)S(1)} %get-tuple-element.10.held, bf16[2,256,256]{2,1,0:T(8,128)(2,1)S(1)} %collective-permute-done.6.below_upper, bf16[2,256,256]{2,1,0:T(8,128)(2,1)S(1)} %collective-permute-done.7.above_lower), custom_call_target="tpu_custom_call" | custom-call | flops 1 | bytes 1 | tf_op jit(solution)/shard_map/pallas_call | solution.py:144
  50.7 2.0 %collective-permute-done.13.above = bf16[2,256,256]{2,1,0:T(8,128)(2,1)S(1)} collective-permute-done((bf16[2,256,256]{2,1,0:T(8,128)(2,1)S(1)}, bf16[2,256,256]{2,1,0:T(8,128)(2,1)S(1)}, u32[]{:S(2)}, u32[]{:S(2)}) %collective-permute-start.13) | collective-permute-done | bytes 262176 | tf_op jit(solution)/shard_map/ppermute | solution.py:161
  52.8 1.2 %collective-permute-done.12.below = bf16[2,256,256]{2,1,0:T(8,128)(2,1)S(1)} collective-permute-done((bf16[2,256,256]{2,1,0:T(8,128)(2,1)S(1)}, bf16[2,256,256]{2,1,0:T(8,128)(2,1)S(1)}, u32[]{:S(2)}, u32[]{:S(2)}) %collective-permute-start.12) | collective-permute-done | bytes 262176 | tf_op jit(solution)/shard_map/ppermute | solution.py:161
  54.0 0.9 %shard_map.43 = bf16[2,256,256]{2,1,0:T(8,128)(2,1)S(1)} custom-call(bf16[2,2,256,256]{3,2,1,0:T(8,128)(2,1)S(1)} %get-tuple-element.10.held, bf16[2,256,256]{2,1,0:T(8,128)(2,1)S(1)} %shard_map.40.spread, bf16[2,256,256]{2,1,0:T(8,128)(2,1)S(1)} %shard_map.42.rhs, bf16[2,256,256]{2,1,0:T(8,128)(2,1)S(1)} %collective-permute-done.12.below, ...), custom_call_target="tpu_custom_call" | custom-call | flops 1 | bytes 1 | tf_op jit(solution)/shard_map/pallas_call | solution.py:144
  54.9 0.0 collective-permute-start.14
  54.9 6.4 %collective-permute-done.14 = bf16[2,256,256]{2,1,0:T(8,128)(2,1)S(1)} collective-permute-done((bf16[2,256,256]{2,1,0:T(8,128)(2,1)S(1)}, bf16[2,256,256]{2,1,0:T(8,128)(2,1)S(1)}, u32[]{:S(2)}, u32[]{:S(2)}) %collective-permute-start.14) | collective-permute-done | bytes 262176 | tf_op jit(solution)/shard_map/ppermute | solution.py:161
  61.2 0.7 %copy.6 = bf16[1,2,256,256]{3,2,1,0:T(8,128)(2,1)} copy(bf16[1,2,256,256]{3,2,1,0:T(8,128)(2,1)S(1)} %bitcast.9) | data formatting | bytes 524288
  (2 shorter events, 0.1 us)
Async XLA Ops:
  0.0 1.0 %copy-start.1 = (bf16[1,2,256,256]{3,2,1,0:T(8,128)(2,1)S(1)}, bf16[1,2,256,256]{3,2,1,0:T(8,128)(2,1)}, u32[]{:S(2)}) copy-start(bf16[1,2,256,256]{3,2,1,0:T(8,128)(2,1)} %param.4) | copy-start | bytes 786436
  1.0 3.1 %copy-start = (bf16[1,2,256,256]{3,2,1,0:T(8,128)(2,1)S(1)}, bf16[1,2,256,256]{3,2,1,0:T(8,128)(2,1)}, u32[]{:S(2)}) copy-start(bf16[1,2,256,256]{3,2,1,0:T(8,128)(2,1)} %param.5) | copy-start | bytes 786436
  1.1 15.0 %collective-permute-start = (bf16[2,2,256,256]{3,2,1,0:T(8,128)(2,1)S(1)}, bf16[2,2,256,256]{3,2,1,0:T(8,128)(2,1)S(1)}, u32[]{:S(2)}, u32[]{:S(2)}) collective-permute-start(bf16[2,2,256,256]{3,2,1,0:T(8,128)(2,1)S(1)} %constant_dynamic-update-slice_fusion.held), channel_id=1, source_target_pairs={{0,2},{1,3},{2,0},{3,1},{4,6},{5,7},{6,4},{7,5},{8,10},{9,11},{10,... | collective-permute-start | bytes 1572872 | tf_op jit(solution)/shard_map/ppermute | solution.py:161
  4.2 15.0 %collective-permute-start.3 = (bf16[3,2,256,256]{3,2,1,0:T(8,128)(2,1)S(1)}, bf16[3,2,256,256]{3,2,1,0:T(8,128)(2,1)S(1)}, u32[]{:S(2)}, u32[]{:S(2)}) collective-permute-start(bf16[3,2,256,256]{3,2,1,0:T(8,128)(2,1)S(1)} %shard_map.37), channel_id=1, source_target_pairs={{3,6},{4,1},{7,10},{8,5},{11,14},{12,9},{19,22},{20,17},{23,26},{2... | collective-permute-start | bytes 2359304 | tf_op jit(solution)/shard_map/ppermute | solution.py:161
  4.9 14.2 %collective-permute-start.1 = (bf16[3,2,256,256]{3,2,1,0:T(8,128)(2,1)S(1)}, bf16[3,2,256,256]{3,2,1,0:T(8,128)(2,1)S(1)}, u32[]{:S(2)}, u32[]{:S(2)}) collective-permute-start(bf16[3,2,256,256]{3,2,1,0:T(8,128)(2,1)S(1)} %shard_map.37), channel_id=1, source_target_pairs={{1,0},{2,3},{5,4},{6,7},{9,8},{10,11},{13,12},{14,15},{17,16},{18,... | collective-permute-start | bytes 2359304 | tf_op jit(solution)/shard_map/ppermute | solution.py:161
  16.0 3.1 %collective-permute-start.2 = (bf16[2,2,256,256]{3,2,1,0:T(8,128)(2,1)S(1)}, bf16[2,2,256,256]{3,2,1,0:T(8,128)(2,1)S(1)}, u32[]{:S(2)}, u32[]{:S(2)}) collective-permute-start(bf16[2,2,256,256]{3,2,1,0:T(8,128)(2,1)S(1)} %collective-permute-done.crossed), channel_id=1, source_target_pairs={{0,1},{3,2},{4,5},{7,6},{8,9},{11,10},{12,13},{15,14},{16,17},{19,... | collective-permute-start | bytes 1572872 | tf_op jit(solution)/shard_map/ppermute | solution.py:161
  17.3 9.1 %collective-permute-start.8 = (bf16[2,256,256]{2,1,0:T(8,128)(2,1)S(1)}, bf16[2,256,256]{2,1,0:T(8,128)(2,1)S(1)}, u32[]{:S(2)}, u32[]{:S(2)}) collective-permute-start(bf16[2,256,256]{2,1,0:T(8,128)(2,1)S(1)} %bitcast.7), channel_id=1, source_target_pairs={{0,2},{1,3},{2,0},{3,1},{4,6},{5,7},{6,4},{7,5},{8,10},{9,11},{10,... | collective-permute-start | bytes 786440 | tf_op jit(solution)/shard_map/ppermute | solution.py:161
  21.1 13.3 %collective-permute-start.5 = (bf16[2,2,256,256]{3,2,1,0:T(8,128)(2,1)S(1)}, bf16[2,2,256,256]{3,2,1,0:T(8,128)(2,1)S(1)}, u32[]{:S(2)}, u32[]{:S(2)}) collective-permute-start(bf16[2,2,256,256]{3,2,1,0:T(8,128)(2,1)S(1)} %get-tuple-element.9.held), channel_id=1, source_target_pairs={{1,4},{3,6},{4,1},{5,8},{6,3},{7,10},{8,5},{9,12},{10,7},{11,14},{... | collective-permute-start | bytes 1572872 | tf_op jit(solution)/shard_map/ppermute | solution.py:161
  21.8 12.6 %collective-permute-start.4 = (bf16[2,2,256,256]{3,2,1,0:T(8,128)(2,1)S(1)}, bf16[2,2,256,256]{3,2,1,0:T(8,128)(2,1)S(1)}, u32[]{:S(2)}, u32[]{:S(2)}) collective-permute-start(bf16[2,2,256,256]{3,2,1,0:T(8,128)(2,1)S(1)} %get-tuple-element.9.held), channel_id=1, source_target_pairs={{0,1},{1,0},{2,3},{3,2},{4,5},{5,4},{6,7},{7,6},{8,9},{9,8},{10,11... | collective-permute-start | bytes 1572872 | tf_op jit(solution)/shard_map/ppermute | solution.py:161
  26.4 3.2 %collective-permute-start.9 = (bf16[2,256,256]{2,1,0:T(8,128)(2,1)S(1)}, bf16[2,256,256]{2,1,0:T(8,128)(2,1)S(1)}, u32[]{:S(2)}, u32[]{:S(2)}) collective-permute-start(bf16[2,256,256]{2,1,0:T(8,128)(2,1)S(1)} %collective-permute-done.8.crossed_rhs), channel_id=1, source_target_pairs={{0,1},{3,2},{4,5},{7,6},{8,9},{11,10},{12,13},{15,14},{16,17},{19,... | collective-permute-start | bytes 786440 | tf_op jit(solution)/shard_map/ppermute | solution.py:161
  30.5 11.8 %collective-permute-start.11 = (bf16[2,256,256]{2,1,0:T(8,128)(2,1)S(1)}, bf16[2,256,256]{2,1,0:T(8,128)(2,1)S(1)}, u32[]{:S(2)}, u32[]{:S(2)}) collective-permute-start(bf16[2,256,256]{2,1,0:T(8,128)(2,1)S(1)} %shard_map.41.rhs), channel_id=1, source_target_pairs={{1,4},{3,6},{4,1},{5,8},{6,3},{7,10},{8,5},{9,12},{10,7},{11,14},{... | collective-permute-start | bytes 786440 | tf_op jit(solution)/shard_map/ppermute | solution.py:161
  31.2 11.1 %collective-permute-start.10 = (bf16[2,256,256]{2,1,0:T(8,128)(2,1)S(1)}, bf16[2,256,256]{2,1,0:T(8,128)(2,1)S(1)}, u32[]{:S(2)}, u32[]{:S(2)}) collective-permute-start(bf16[2,256,256]{2,1,0:T(8,128)(2,1)S(1)} %shard_map.41.rhs), channel_id=1, source_target_pairs={{0,1},{1,0},{2,3},{3,2},{4,5},{5,4},{6,7},{7,6},{8,9},{9,8},{10,11... | collective-permute-start | bytes 786440 | tf_op jit(solution)/shard_map/ppermute | solution.py:161
  36.4 12.7 %collective-permute-start.7 = (bf16[2,256,256]{2,1,0:T(8,128)(2,1)S(1)}, bf16[2,256,256]{2,1,0:T(8,128)(2,1)S(1)}, u32[]{:S(2)}, u32[]{:S(2)}) collective-permute-start(bf16[2,256,256]{2,1,0:T(8,128)(2,1)S(1)} %get-tuple-element.13), channel_id=1, source_target_pairs={{4,0},{5,1},{6,2},{7,3},{8,4},{9,5},{10,6},{11,7},{12,8},{13,9},{1... | collective-permute-start | bytes 786440 | tf_op jit(solution)/shard_map/ppermute | solution.py:161
  37.7 11.4 %collective-permute-start.6 = (bf16[2,256,256]{2,1,0:T(8,128)(2,1)S(1)}, bf16[2,256,256]{2,1,0:T(8,128)(2,1)S(1)}, u32[]{:S(2)}, u32[]{:S(2)}) collective-permute-start(bf16[2,256,256]{2,1,0:T(8,128)(2,1)S(1)} %get-tuple-element.14), channel_id=1, source_target_pairs={{0,4},{1,5},{2,6},{3,7},{4,8},{5,9},{6,10},{7,11},{8,12},{9,13},{1... | collective-permute-start | bytes 786440 | tf_op jit(solution)/shard_map/ppermute | solution.py:161
  43.2 9.6 %collective-permute-start.13 = (bf16[2,256,256]{2,1,0:T(8,128)(2,1)S(1)}, bf16[2,256,256]{2,1,0:T(8,128)(2,1)S(1)}, u32[]{:S(2)}, u32[]{:S(2)}) collective-permute-start(bf16[2,256,256]{2,1,0:T(8,128)(2,1)S(1)} %shard_map.42.rhs), channel_id=1, source_target_pairs={{4,0},{5,1},{6,2},{7,3},{8,4},{9,5},{10,6},{11,7},{12,8},{13,9},{1... | collective-permute-start | bytes 786440 | tf_op jit(solution)/shard_map/ppermute | solution.py:161
  44.5 9.5 %collective-permute-start.12 = (bf16[2,256,256]{2,1,0:T(8,128)(2,1)S(1)}, bf16[2,256,256]{2,1,0:T(8,128)(2,1)S(1)}, u32[]{:S(2)}, u32[]{:S(2)}) collective-permute-start(bf16[2,256,256]{2,1,0:T(8,128)(2,1)S(1)} %shard_map.42.rhs), channel_id=1, source_target_pairs={{0,4},{1,5},{2,6},{3,7},{4,8},{5,9},{6,10},{7,11},{8,12},{9,13},{1... | collective-permute-start | bytes 786440 | tf_op jit(solution)/shard_map/ppermute | solution.py:161
  54.9 6.4 %collective-permute-start.14 = (bf16[2,256,256]{2,1,0:T(8,128)(2,1)S(1)}, bf16[2,256,256]{2,1,0:T(8,128)(2,1)S(1)}, u32[]{:S(2)}, u32[]{:S(2)}) collective-permute-start(bf16[2,256,256]{2,1,0:T(8,128)(2,1)S(1)} %shard_map.43), channel_id=1, source_target_pairs={{0,1},{1,3},{2,0},{3,2},{4,5},{5,7},{6,4},{7,6},{8,9},{9,11},{10,8... | collective-permute-start | bytes 786440 | tf_op jit(solution)/shard_map/ppermute | solution.py:161

commit v5 on v4

--- a/solution.py
+++ b/solution.py
@@ -54,15 +54,17 @@
     return low(raw.astype(jnp.float32) + product(wide(spread), low(raw)))
 
 
-def row_couplings(letter, own, near, far, new, spread):
+def row_couplings(letter, own, near, far, spread):
     order = spread.shape[1]
     other = 1 - letter
     by_near = product(wide(own(letter)), beside(tall(near(other)), tall(near(letter))))
     by_far = product(wide(own(other)), beside(tall(far(letter)), tall(far(other))))
     spread[...] = parts(inverse_less_one(by_near[:, :order] + by_far[:, :order]))
     solution_of = spread[...]
-    new[letter] = parts(solved(solution_of, -by_near[:, order:]))
-    new[other] = parts(solved(solution_of, -by_far[:, order:]))
+    return (
+        parts(solved(solution_of, -by_near[:, order:])),
+        parts(solved(solution_of, -by_far[:, order:])),
+    )
 
 
 def row_injections(letter, own, spread, rhs, near, far):
@@ -90,10 +92,9 @@
 
 
 def first_couplings_kernel(held, crossed, core, onward, level, new, spread):
-    row_couplings(
-        first_letter(),
-        on_edge(crossed, core), on_edge(onward, held), on_edge(level, crossed),
-        new, spread,
+    letter = first_letter()
+    new[letter], new[1 - letter] = row_couplings(
+        letter, on_edge(crossed, core), on_edge(onward, held), on_edge(level, crossed), spread
     )
 
 
@@ -118,8 +119,16 @@
     return jnp.where(spot_of(GROUP) % 2 == 0, UPP, LOW)
 
 
-def later_couplings_kernel(held, core, level, new, spread):
-    row_couplings(second_letter(), at(held), at(core), at(level), new, spread)
+def even_group():
+    return lax.axis_index("chain") // GROUP % 2 == 0
+
+
+def later_couplings_kernel(held, core, level, pairing, joining, spread):
+    letter = second_letter()
+    near, far = row_couplings(letter, at(held), at(core), at(level), spread)
+    keep = (letter == UPP) == even_group()
+    pairing[...] = jnp.where(keep, near, far)
+    joining[...] = jnp.where(keep, far, near)
 
 
 def later_injections_kernel(held, spread, rhs, core, level, new):
@@ -128,16 +137,16 @@
     )
 
 
-def last_couplings_kernel(held, below_upper, above_lower, spread):
-    coupling = product(wide(held[LOW]), tall(below_upper[...]))
-    coupling = coupling + product(wide(held[UPP]), tall(above_lower[...]))
+def last_couplings_kernel(pairing, joining, paired, joined, spread):
+    coupling = product(wide(pairing), tall(paired[...]))
+    coupling = coupling + product(wide(joining), tall(joined[...]))
     spread[...] = parts(inverse_less_one(coupling))
 
 
-def last_injections_kernel(held, spread, rhs, below, above, new):
-    new[...] = row_injections(
-        LOW, at(held), spread, rhs[...], below[...], above[...]
-    )
+def last_injections_kernel(pairing, joining, spread, rhs, paired, joined, new):
+    raw = tall(rhs[...]).astype(jnp.float32) - product(wide(pairing), tall(paired[...]))
+    raw = raw - product(wide(joining), tall(joined[...]))
+    new[...] = parts(solved(spread[...], raw))
 
 
 def run(kernel, outs, *operands, weight=1):
@@ -156,11 +165,13 @@
     pair = (2,) + block
     groups = range(0, length, GROUP)
 
+    def trade(value, pairs):
+        return lax.ppermute(
+            value, "chain", [(a, b) for a, b in pairs if 0 <= a < length and 0 <= b < length]
+        )
+
     def move(value, *pairs):
-        moves = [(g + a, g + b) for g in groups for a, b in pairs]
-        return lax.ppermute(
-            value, "chain", [(a, b) for a, b in moves if 0 <= a < length and 0 <= b < length]
-        )
+        return trade(value, [(g + a, g + b) for g in groups for a, b in pairs])
 
     mirrored = ((0, 2), (1, 3), (2, 0), (3, 1))
     inward = ((1, 0), (2, 3))
@@ -168,8 +179,6 @@
     levels = ((0, 1 - GROUP), (3, 2 + GROUP))
     in_core = ((0, 1), (1, 0), (2, 3), (3, 2))
     between = ((0, 1 - GROUP), (1, GROUP), (2, 3 - GROUP), (3, 2 + GROUP))
-    upward = tuple((i, i + GROUP) for i in range(GROUP))
-    downward = tuple((i, i - GROUP) for i in range(GROUP))
     home = ((0, 1), (1, 3), (2, 0), (3, 2))
 
     held = jnp.concatenate([lower, upper], axis=0)
@@ -193,19 +202,28 @@
 
     core, level = move(held, *in_core), move(held, *between)
     core_rhs, level_rhs = move(rhs, *in_core), move(rhs, *between)
-    new_held, spread = run(
-        later_couplings_kernel, (pair, block), held, core, level
-    )
+    pairing, joining, spread = run(later_couplings_kernel, (block,) * 3, held, core, level)
     (rhs,) = run(
         later_injections_kernel, (block,),
         held, spread, rhs, core_rhs, level_rhs,
     )
-    held = new_held
-
-    below, above = move(held[UPP], *upward), move(held[LOW], *downward)
-    below_rhs, above_rhs = move(rhs, *upward), move(rhs, *downward)
-    (spread,) = run(last_couplings_kernel, (block,), held, below, above)
-    (result,) = run(last_injections_kernel, (block,), held, spread, rhs, below_rhs, above_rhs)
+
+    at_joint, in_pair = (
+        [
+            (g * GROUP + a, (g + by) * GROUP + a)
+            for g in range(length // GROUP)
+            for by in ((1 if g % 2 == start else -1),)
+            for a in range(GROUP)
+        ]
+        for start in (1, 0)
+    )
+    joined, joined_rhs = trade(joining, at_joint), trade(rhs, at_joint)
+    paired, paired_rhs = trade(pairing, in_pair), trade(rhs, in_pair)
+    (spread,) = run(last_couplings_kernel, (block,), pairing, joining, paired, joined)
+    (result,) = run(
+        last_injections_kernel, (block,),
+        pairing, joining, spread, rhs, paired_rhs, joined_rhs,
+    )
     return move(result, *home)[None]
 
 

time: 62.3 us -> 59.5 us (0.955)
  starting transfers between devices: 29.4 us -> 25.7 us
  waiting for transfers between devices: 22.2 us -> 23.2 us
    ppermute x15, starting transfers between devices: 29.4 us -> 25.7 us  [trade(): lax.ppermute(value, 'chain', [(a, b) for a, b in pairs if 0 <= a < length...]
    ppermute x15, waiting for transfers between devices: 22.2 us -> 23.2 us  [trade(): lax.ppermute(value, 'chain', [(a, b) for a, b in pairs if 0 <= a < length...]
  transfers between devices with their start and end apart: 15 -> 15, of which waited for: 6 -> 5; matrix products, arithmetic and copies ran while one was open for 0% -> 0% of each run, Pallas kernels for 12% -> 13%
where the time goes in v5:
time: 59.5 us; the launch traced here: 59.1 us
  starting transfers between devices  25.7 us (43%)
  waiting for transfers between devices  23.2 us (39%)
  Pallas kernels  8.28 us (14%)
  local copies, waits for them, and re-layouts  1.75 us (3%)
    ppermute x15, starting transfers between devices, trade(): lax.ppermute(value, 'chain', [(a, b) for a, b in pairs if 0 <= a < length...  25.7 us
    ppermute x15, waiting for transfers between devices, trade(): lax.ppermute(value, 'chain', [(a, b) for a, b in pairs if 0 <= a < length...  23.2 us
    pallas_call x7, Pallas kernels, run(): pl.pallas_call(kernel, out_shape=[jax.ShapeDtypeStruct(s, jnp.bfloat16) f...  8.28 us
    unnamed x6, local copies, waits for them, and re-layouts  1.73 us
  transfers between devices with their start and end apart: 15, of which 5 were waited for; matrix products, arithmetic and copies ran while one was open for 0% of the time, Pallas kernels for 13%

profile of v5, /device:TPU:0, one launch (start us, length us, event | category | flops | bytes accessed | tf_op | source)
XLA Modules:
  0.0 59.1 jit_solution(12416656814188015344)
XLA Ops:
  0.0 0.0 copy-start.1
  0.0 1.0 %constant_dynamic-update-slice_fusion.1 = bf16[2,2,256,256]{3,2,1,0:T(8,128)(2,1)S(1)} fusion(bf16[1,2,256,256]{3,2,1,0:T(8,128)(2,1)} %param.3), kind=kLoop, calls=%fused_computation.1 | loop fusion | bytes 524288
  1.0 0.0 copy-done.1
  1.0 0.0 copy-start
  1.1 3.0 %collective-permute-start = (bf16[2,2,256,256]{3,2,1,0:T(8,128)(2,1)S(1)}, bf16[2,2,256,256]{3,2,1,0:T(8,128)(2,1)S(1)}, u32[]{:S(2)}, u32[]{:S(2)}) collective-permute-start(bf16[2,2,256,256]{3,2,1,0:T(8,128)(2,1)S(1)} %constant_dynamic-update-slice_fusion.held), channel_id=1, source_target_pairs={{0,2},{1,3},{2,0},{3,1},{4,6},{5,7},{6,4},{7,5},{8,10},{9,11},{10,... | collective-permute-start | bytes 1572872 | tf_op jit(solution)/shard_map/ppermute | solution.py:169
  4.1 0.0 copy-done
  4.1 0.1 shard_map.37
  4.2 0.7 %collective-permute-start.3 = (bf16[3,2,256,256]{3,2,1,0:T(8,128)(2,1)S(1)}, bf16[3,2,256,256]{3,2,1,0:T(8,128)(2,1)S(1)}, u32[]{:S(2)}, u32[]{:S(2)}) collective-permute-start(bf16[3,2,256,256]{3,2,1,0:T(8,128)(2,1)S(1)} %shard_map.37), channel_id=1, source_target_pairs={{3,6},{4,1},{7,10},{8,5},{11,14},{12,9},{19,22},{20,17},{23,26},{2... | collective-permute-start | bytes 2359304 | tf_op jit(solution)/shard_map/ppermute | solution.py:169
  4.9 1.3 %collective-permute-start.1 = (bf16[3,2,256,256]{3,2,1,0:T(8,128)(2,1)S(1)}, bf16[3,2,256,256]{3,2,1,0:T(8,128)(2,1)S(1)}, u32[]{:S(2)}, u32[]{:S(2)}) collective-permute-start(bf16[3,2,256,256]{3,2,1,0:T(8,128)(2,1)S(1)} %shard_map.37), channel_id=1, source_target_pairs={{1,0},{2,3},{5,4},{6,7},{9,8},{10,11},{13,12},{14,15},{17,16},{18,... | collective-permute-start | bytes 2359304 | tf_op jit(solution)/shard_map/ppermute | solution.py:169
  6.2 9.8 %collective-permute-done.crossed = bf16[2,2,256,256]{3,2,1,0:T(8,128)(2,1)S(1)} collective-permute-done((bf16[2,2,256,256]{3,2,1,0:T(8,128)(2,1)S(1)}, bf16[2,2,256,256]{3,2,1,0:T(8,128)(2,1)S(1)}, u32[]{:S(2)}, u32[]{:S(2)}) %collective-permute-start) | collective-permute-done | bytes 524320 | tf_op jit(solution)/shard_map/ppermute | solution.py:169
  16.0 1.3 %collective-permute-start.2 = (bf16[2,2,256,256]{3,2,1,0:T(8,128)(2,1)S(1)}, bf16[2,2,256,256]{3,2,1,0:T(8,128)(2,1)S(1)}, u32[]{:S(2)}, u32[]{:S(2)}) collective-permute-start(bf16[2,2,256,256]{3,2,1,0:T(8,128)(2,1)S(1)} %collective-permute-done.crossed), channel_id=1, source_target_pairs={{0,1},{3,2},{4,5},{7,6},{8,9},{11,10},{12,13},{15,14},{16,17},{19,... | collective-permute-start | bytes 1572872 | tf_op jit(solution)/shard_map/ppermute | solution.py:169
  17.3 1.8 %collective-permute-start.8 = (bf16[2,256,256]{2,1,0:T(8,128)(2,1)S(1)}, bf16[2,256,256]{2,1,0:T(8,128)(2,1)S(1)}, u32[]{:S(2)}, u32[]{:S(2)}) collective-permute-start(bf16[2,256,256]{2,1,0:T(8,128)(2,1)S(1)} %bitcast.3), channel_id=1, source_target_pairs={{0,2},{1,3},{2,0},{3,1},{4,6},{5,7},{6,4},{7,5},{8,10},{9,11},{10,... | collective-permute-start | bytes 786440 | tf_op jit(solution)/shard_map/ppermute | solution.py:169
  19.1 0.0 collective-permute-done.3.level
  19.1 0.0 collective-permute-done.1.core
  19.1 0.0 collective-permute-done.2.onward
  19.1 1.9 %shard_map.38 = (bf16[2,2,256,256]{3,2,1,0:T(8,128)(2,1)S(1)}, bf16[2,256,256]{2,1,0:T(8,128)(2,1)S(1)}) custom-call(bf16[2,2,256,256]{3,2,1,0:T(8,128)(2,1)S(1)} %constant_dynamic-update-slice_fusion.held, bf16[2,2,256,256]{3,2,1,0:T(8,128)(2,1)S(1)} %collective-permute-done.crossed, bf16[3,2,256,256]{3,2,1,0:T(8,128)(2,1)S(1)} %collective-permute-done.1.core, ...), custom_call_target="tpu_custom_call" | custom-call | flops 1 | bytes 1 | tf_op jit(solution)/shard_map/pallas_call | solution.py:153
  21.1 0.7 %collective-permute-start.5 = (bf16[2,2,256,256]{3,2,1,0:T(8,128)(2,1)S(1)}, bf16[2,2,256,256]{3,2,1,0:T(8,128)(2,1)S(1)}, u32[]{:S(2)}, u32[]{:S(2)}) collective-permute-start(bf16[2,2,256,256]{3,2,1,0:T(8,128)(2,1)S(1)} %get-tuple-element.10.held), channel_id=1, source_target_pairs={{1,4},{3,6},{4,1},{5,8},{6,3},{7,10},{8,5},{9,12},{10,7},{11,14},{... | collective-permute-start | bytes 1572872 | tf_op jit(solution)/shard_map/ppermute | solution.py:169
  21.8 3.0 %collective-permute-start.4 = (bf16[2,2,256,256]{3,2,1,0:T(8,128)(2,1)S(1)}, bf16[2,2,256,256]{3,2,1,0:T(8,128)(2,1)S(1)}, u32[]{:S(2)}, u32[]{:S(2)}) collective-permute-start(bf16[2,2,256,256]{3,2,1,0:T(8,128)(2,1)S(1)} %get-tuple-element.10.held), channel_id=1, source_target_pairs={{0,1},{1,0},{2,3},{3,2},{4,5},{5,4},{6,7},{7,6},{8,9},{9,8},{10,11... | collective-permute-start | bytes 1572872 | tf_op jit(solution)/shard_map/ppermute | solution.py:169
  24.8 1.7 %collective-permute-done.8.crossed_rhs = bf16[2,256,256]{2,1,0:T(8,128)(2,1)S(1)} collective-permute-done((bf16[2,256,256]{2,1,0:T(8,128)(2,1)S(1)}, bf16[2,256,256]{2,1,0:T(8,128)(2,1)S(1)}, u32[]{:S(2)}, u32[]{:S(2)}) %collective-permute-start.8) | collective-permute-done | bytes 262176 | tf_op jit(solution)/shard_map/ppermute | solution.py:169
  26.4 2.0 %collective-permute-start.9 = (bf16[2,256,256]{2,1,0:T(8,128)(2,1)S(1)}, bf16[2,256,256]{2,1,0:T(8,128)(2,1)S(1)}, u32[]{:S(2)}, u32[]{:S(2)}) collective-permute-start(bf16[2,256,256]{2,1,0:T(8,128)(2,1)S(1)} %collective-permute-done.8.crossed_rhs), channel_id=1, source_target_pairs={{0,1},{3,2},{4,5},{7,6},{8,9},{11,10},{12,13},{15,14},{16,17},{19,... | collective-permute-start | bytes 786440 | tf_op jit(solution)/shard_map/ppermute | solution.py:169
  28.5 1.1 %collective-permute-done.9.onward_rhs = bf16[2,256,256]{2,1,0:T(8,128)(2,1)S(1)} collective-permute-done((bf16[2,256,256]{2,1,0:T(8,128)(2,1)S(1)}, bf16[2,256,256]{2,1,0:T(8,128)(2,1)S(1)}, u32[]{:S(2)}, u32[]{:S(2)}) %collective-permute-start.9) | collective-permute-done | bytes 262176 | tf_op jit(solution)/shard_map/ppermute | solution.py:169
  29.6 0.9 %shard_map.41.rhs = bf16[2,256,256]{2,1,0:T(8,128)(2,1)S(1)} custom-call(bf16[2,2,256,256]{3,2,1,0:T(8,128)(2,1)S(1)} %collective-permute-done.crossed, bf16[2,256,256]{2,1,0:T(8,128)(2,1)S(1)} %get-tuple-element.14.spread, bf16[2,256,256]{2,1,0:T(8,128)(2,1)S(1)} %bitcast.4, bf16[2,256,256]{2,1,0:T(8,128)(2,1)S(1)} %collective-permute-done.8.crossed_rhs, ...), custom_call_target="tpu_custom_call" | custom-call | flops 1 | bytes 1 | tf_op jit(solution)/shard_map/pallas_call | solution.py:153
  30.5 0.7 %collective-permute-start.11 = (bf16[2,256,256]{2,1,0:T(8,128)(2,1)S(1)}, bf16[2,256,256]{2,1,0:T(8,128)(2,1)S(1)}, u32[]{:S(2)}, u32[]{:S(2)}) collective-permute-start(bf16[2,256,256]{2,1,0:T(8,128)(2,1)S(1)} %shard_map.41.rhs), channel_id=1, source_target_pairs={{1,4},{3,6},{4,1},{5,8},{6,3},{7,10},{8,5},{9,12},{10,7},{11,14},{... | collective-permute-start | bytes 786440 | tf_op jit(solution)/shard_map/ppermute | solution.py:169
  31.2 3.2 %collective-permute-start.10 = (bf16[2,256,256]{2,1,0:T(8,128)(2,1)S(1)}, bf16[2,256,256]{2,1,0:T(8,128)(2,1)S(1)}, u32[]{:S(2)}, u32[]{:S(2)}) collective-permute-start(bf16[2,256,256]{2,1,0:T(8,128)(2,1)S(1)} %shard_map.41.rhs), channel_id=1, source_target_pairs={{0,1},{1,0},{2,3},{3,2},{4,5},{5,4},{6,7},{7,6},{8,9},{9,8},{10,11... | collective-permute-start | bytes 786440 | tf_op jit(solution)/shard_map/ppermute | solution.py:169
  34.4 0.0 collective-permute-done.5.level
  34.4 0.0 collective-permute-done.4.core
  34.4 1.9 %shard_map.39 = (bf16[2,256,256]{2,1,0:T(8,128)(2,1)S(1)}, bf16[2,256,256]{2,1,0:T(8,128)(2,1)S(1)}, bf16[2,256,256]{2,1,0:T(8,128)(2,1)S(1)}) custom-call(bf16[2,2,256,256]{3,2,1,0:T(8,128)(2,1)S(1)} %get-tuple-element.10.held, bf16[2,2,256,256]{3,2,1,0:T(8,128)(2,1)S(1)} %collective-permute-done.4.core, ...), custom_call_target="tpu_custom_call" | custom-call | flops 1 | bytes 1 | tf_op jit(solution)/shard_map/pallas_call | solution.py:153
  36.4 1.6 %collective-permute-start.6 = (bf16[2,256,256]{2,1,0:T(8,128)(2,1)S(1)}, bf16[2,256,256]{2,1,0:T(8,128)(2,1)S(1)}, u32[]{:S(2)}, u32[]{:S(2)}) collective-permute-start(bf16[2,256,256]{2,1,0:T(8,128)(2,1)S(1)} %get-tuple-element.11.pairing), channel_id=1, source_target_pairs={{0,4},{1,5},{2,6},{3,7},{4,0},{5,1},{6,2},{7,3},{8,12},{9,13},{10,... | collective-permute-start | bytes 786440 | tf_op jit(solution)/shard_map/ppermute | solution.py:169
  38.0 0.7 %collective-permute-start.7 = (bf16[2,256,256]{2,1,0:T(8,128)(2,1)S(1)}, bf16[2,256,256]{2,1,0:T(8,128)(2,1)S(1)}, u32[]{:S(2)}, u32[]{:S(2)}) collective-permute-start(bf16[2,256,256]{2,1,0:T(8,128)(2,1)S(1)} %get-tuple-element.12.joining), channel_id=1, source_target_pairs={{4,8},{5,9},{6,10},{7,11},{8,4},{9,5},{10,6},{11,7},{20,24},{21,25... | collective-permute-start | bytes 786440 | tf_op jit(solution)/shard_map/ppermute | solution.py:169
  38.7 0.0 collective-permute-done.11.level
  38.7 0.0 collective-permute-done.10.core
  38.7 0.9 %shard_map.42.rhs = bf16[2,256,256]{2,1,0:T(8,128)(2,1)S(1)} custom-call(bf16[2,2,256,256]{3,2,1,0:T(8,128)(2,1)S(1)} %get-tuple-element.10.held, bf16[2,256,256]{2,1,0:T(8,128)(2,1)S(1)} %get-tuple-element.13.spread, bf16[2,256,256]{2,1,0:T(8,128)(2,1)S(1)} %shard_map.41.rhs, bf16[2,256,256]{2,1,0:T(8,128)(2,1)S(1)} %collective-permute-done.10.core, ...), custom_call_target="tpu_custom_call" | custom-call | flops 1 | bytes 1 | tf_op jit(solution)/shard_map/pallas_call | solution.py:153
  39.6 0.7 %collective-permute-start.13 = (bf16[2,256,256]{2,1,0:T(8,128)(2,1)S(1)}, bf16[2,256,256]{2,1,0:T(8,128)(2,1)S(1)}, u32[]{:S(2)}, u32[]{:S(2)}) collective-permute-start(bf16[2,256,256]{2,1,0:T(8,128)(2,1)S(1)} %shard_map.42.rhs), channel_id=1, source_target_pairs={{4,8},{5,9},{6,10},{7,11},{8,4},{9,5},{10,6},{11,7},{20,24},{21,25... | collective-permute-start | bytes 786440 | tf_op jit(solution)/shard_map/ppermute | solution.py:169
  40.3 5.0 %collective-permute-start.12 = (bf16[2,256,256]{2,1,0:T(8,128)(2,1)S(1)}, bf16[2,256,256]{2,1,0:T(8,128)(2,1)S(1)}, u32[]{:S(2)}, u32[]{:S(2)}) collective-permute-start(bf16[2,256,256]{2,1,0:T(8,128)(2,1)S(1)} %shard_map.42.rhs), channel_id=1, source_target_pairs={{0,4},{1,5},{2,6},{3,7},{4,0},{5,1},{6,2},{7,3},{8,12},{9,13},{10,... | collective-permute-start | bytes 786440 | tf_op jit(solution)/shard_map/ppermute | solution.py:169
  45.3 0.0 collective-permute-done.6.paired
  45.3 0.0 collective-permute-done.7.joined
  45.3 1.7 %shard_map.40.spread = bf16[2,256,256]{2,1,0:T(8,128)(2,1)S(1)} custom-call(bf16[2,256,256]{2,1,0:T(8,128)(2,1)S(1)} %get-tuple-element.11.pairing, bf16[2,256,256]{2,1,0:T(8,128)(2,1)S(1)} %get-tuple-element.12.joining, bf16[2,256,256]{2,1,0:T(8,128)(2,1)S(1)} %collective-permute-done.6.paired, bf16[2,256,256]{2,1,0:T(8,128)(2,1)S(1)} %collective-permute-done.7.joined), custom_call_target="tpu_custom_call" | custom-call | flops 1 | bytes 1 | tf_op jit(solution)/shard_map/pallas_call | solution.py:153
  46.9 0.0 collective-permute-done.13.joined
  47.0 4.2 %collective-permute-done.12.paired = bf16[2,256,256]{2,1,0:T(8,128)(2,1)S(1)} collective-permute-done((bf16[2,256,256]{2,1,0:T(8,128)(2,1)S(1)}, bf16[2,256,256]{2,1,0:T(8,128)(2,1)S(1)}, u32[]{:S(2)}, u32[]{:S(2)}) %collective-permute-start.12) | collective-permute-done | bytes 262176 | tf_op jit(solution)/shard_map/ppermute | solution.py:169
  51.1 0.9 %shard_map.43 = bf16[2,256,256]{2,1,0:T(8,128)(2,1)S(1)} custom-call(bf16[2,256,256]{2,1,0:T(8,128)(2,1)S(1)} %get-tuple-element.11.pairing, bf16[2,256,256]{2,1,0:T(8,128)(2,1)S(1)} %get-tuple-element.12.joining, bf16[2,256,256]{2,1,0:T(8,128)(2,1)S(1)} %shard_map.40.spread, bf16[2,256,256]{2,1,0:T(8,128)(2,1)S(1)} %shard_map.42.rhs, ...), custom_call_target="tpu_custom_call" | custom-call | flops 1 | bytes 1 | tf_op jit(solution)/shard_map/pallas_call | solution.py:153
  52.0 0.0 collective-permute-start.14
  52.1 6.4 %collective-permute-done.14 = bf16[2,256,256]{2,1,0:T(8,128)(2,1)S(1)} collective-permute-done((bf16[2,256,256]{2,1,0:T(8,128)(2,1)S(1)}, bf16[2,256,256]{2,1,0:T(8,128)(2,1)S(1)}, u32[]{:S(2)}, u32[]{:S(2)}) %collective-permute-start.14) | collective-permute-done | bytes 262176 | tf_op jit(solution)/shard_map/ppermute | solution.py:169
  58.4 0.7 %copy.6 = bf16[1,2,256,256]{3,2,1,0:T(8,128)(2,1)} copy(bf16[1,2,256,256]{3,2,1,0:T(8,128)(2,1)S(1)} %bitcast.5) | data formatting | bytes 524288
  (1 shorter events, 0.0 us)
Async XLA Ops:
  0.0 1.0 %copy-start.1 = (bf16[1,2,256,256]{3,2,1,0:T(8,128)(2,1)S(1)}, bf16[1,2,256,256]{3,2,1,0:T(8,128)(2,1)}, u32[]{:S(2)}) copy-start(bf16[1,2,256,256]{3,2,1,0:T(8,128)(2,1)} %param.4) | copy-start | bytes 786436
  1.0 3.1 %copy-start = (bf16[1,2,256,256]{3,2,1,0:T(8,128)(2,1)S(1)}, bf16[1,2,256,256]{3,2,1,0:T(8,128)(2,1)}, u32[]{:S(2)}) copy-start(bf16[1,2,256,256]{3,2,1,0:T(8,128)(2,1)} %param.5) | copy-start | bytes 786436
  1.1 15.0 %collective-permute-start = (bf16[2,2,256,256]{3,2,1,0:T(8,128)(2,1)S(1)}, bf16[2,2,256,256]{3,2,1,0:T(8,128)(2,1)S(1)}, u32[]{:S(2)}, u32[]{:S(2)}) collective-permute-start(bf16[2,2,256,256]{3,2,1,0:T(8,128)(2,1)S(1)} %constant_dynamic-update-slice_fusion.held), channel_id=1, source_target_pairs={{0,2},{1,3},{2,0},{3,1},{4,6},{5,7},{6,4},{7,5},{8,10},{9,11},{10,... | collective-permute-start | bytes 1572872 | tf_op jit(solution)/shard_map/ppermute | solution.py:169
  4.2 15.0 %collective-permute-start.3 = (bf16[3,2,256,256]{3,2,1,0:T(8,128)(2,1)S(1)}, bf16[3,2,256,256]{3,2,1,0:T(8,128)(2,1)S(1)}, u32[]{:S(2)}, u32[]{:S(2)}) collective-permute-start(bf16[3,2,256,256]{3,2,1,0:T(8,128)(2,1)S(1)} %shard_map.37), channel_id=1, source_target_pairs={{3,6},{4,1},{7,10},{8,5},{11,14},{12,9},{19,22},{20,17},{23,26},{2... | collective-permute-start | bytes 2359304 | tf_op jit(solution)/shard_map/ppermute | solution.py:169
  4.9 14.2 %collective-permute-start.1 = (bf16[3,2,256,256]{3,2,1,0:T(8,128)(2,1)S(1)}, bf16[3,2,256,256]{3,2,1,0:T(8,128)(2,1)S(1)}, u32[]{:S(2)}, u32[]{:S(2)}) collective-permute-start(bf16[3,2,256,256]{3,2,1,0:T(8,128)(2,1)S(1)} %shard_map.37), channel_id=1, source_target_pairs={{1,0},{2,3},{5,4},{6,7},{9,8},{10,11},{13,12},{14,15},{17,16},{18,... | collective-permute-start | bytes 2359304 | tf_op jit(solution)/shard_map/ppermute | solution.py:169
  16.0 3.1 %collective-permute-start.2 = (bf16[2,2,256,256]{3,2,1,0:T(8,128)(2,1)S(1)}, bf16[2,2,256,256]{3,2,1,0:T(8,128)(2,1)S(1)}, u32[]{:S(2)}, u32[]{:S(2)}) collective-permute-start(bf16[2,2,256,256]{3,2,1,0:T(8,128)(2,1)S(1)} %collective-permute-done.crossed), channel_id=1, source_target_pairs={{0,1},{3,2},{4,5},{7,6},{8,9},{11,10},{12,13},{15,14},{16,17},{19,... | collective-permute-start | bytes 1572872 | tf_op jit(solution)/shard_map/ppermute | solution.py:169
  17.3 9.1 %collective-permute-start.8 = (bf16[2,256,256]{2,1,0:T(8,128)(2,1)S(1)}, bf16[2,256,256]{2,1,0:T(8,128)(2,1)S(1)}, u32[]{:S(2)}, u32[]{:S(2)}) collective-permute-start(bf16[2,256,256]{2,1,0:T(8,128)(2,1)S(1)} %bitcast.3), channel_id=1, source_target_pairs={{0,2},{1,3},{2,0},{3,1},{4,6},{5,7},{6,4},{7,5},{8,10},{9,11},{10,... | collective-permute-start | bytes 786440 | tf_op jit(solution)/shard_map/ppermute | solution.py:169
  21.1 13.3 %collective-permute-start.5 = (bf16[2,2,256,256]{3,2,1,0:T(8,128)(2,1)S(1)}, bf16[2,2,256,256]{3,2,1,0:T(8,128)(2,1)S(1)}, u32[]{:S(2)}, u32[]{:S(2)}) collective-permute-start(bf16[2,2,256,256]{3,2,1,0:T(8,128)(2,1)S(1)} %get-tuple-element.10.held), channel_id=1, source_target_pairs={{1,4},{3,6},{4,1},{5,8},{6,3},{7,10},{8,5},{9,12},{10,7},{11,14},{... | collective-permute-start | bytes 1572872 | tf_op jit(solution)/shard_map/ppermute | solution.py:169
  21.8 12.6 %collective-permute-start.4 = (bf16[2,2,256,256]{3,2,1,0:T(8,128)(2,1)S(1)}, bf16[2,2,256,256]{3,2,1,0:T(8,128)(2,1)S(1)}, u32[]{:S(2)}, u32[]{:S(2)}) collective-permute-start(bf16[2,2,256,256]{3,2,1,0:T(8,128)(2,1)S(1)} %get-tuple-element.10.held), channel_id=1, source_target_pairs={{0,1},{1,0},{2,3},{3,2},{4,5},{5,4},{6,7},{7,6},{8,9},{9,8},{10,11... | collective-permute-start | bytes 1572872 | tf_op jit(solution)/shard_map/ppermute | solution.py:169
  26.4 3.2 %collective-permute-start.9 = (bf16[2,256,256]{2,1,0:T(8,128)(2,1)S(1)}, bf16[2,256,256]{2,1,0:T(8,128)(2,1)S(1)}, u32[]{:S(2)}, u32[]{:S(2)}) collective-permute-start(bf16[2,256,256]{2,1,0:T(8,128)(2,1)S(1)} %collective-permute-done.8.crossed_rhs), channel_id=1, source_target_pairs={{0,1},{3,2},{4,5},{7,6},{8,9},{11,10},{12,13},{15,14},{16,17},{19,... | collective-permute-start | bytes 786440 | tf_op jit(solution)/shard_map/ppermute | solution.py:169
  30.5 8.2 %collective-permute-start.11 = (bf16[2,256,256]{2,1,0:T(8,128)(2,1)S(1)}, bf16[2,256,256]{2,1,0:T(8,128)(2,1)S(1)}, u32[]{:S(2)}, u32[]{:S(2)}) collective-permute-start(bf16[2,256,256]{2,1,0:T(8,128)(2,1)S(1)} %shard_map.41.rhs), channel_id=1, source_target_pairs={{1,4},{3,6},{4,1},{5,8},{6,3},{7,10},{8,5},{9,12},{10,7},{11,14},{... | collective-permute-start | bytes 786440 | tf_op jit(solution)/shard_map/ppermute | solution.py:169
  31.2 7.5 %collective-permute-start.10 = (bf16[2,256,256]{2,1,0:T(8,128)(2,1)S(1)}, bf16[2,256,256]{2,1,0:T(8,128)(2,1)S(1)}, u32[]{:S(2)}, u32[]{:S(2)}) collective-permute-start(bf16[2,256,256]{2,1,0:T(8,128)(2,1)S(1)} %shard_map.41.rhs), channel_id=1, source_target_pairs={{0,1},{1,0},{2,3},{3,2},{4,5},{5,4},{6,7},{7,6},{8,9},{9,8},{10,11... | collective-permute-start | bytes 786440 | tf_op jit(solution)/shard_map/ppermute | solution.py:169
  36.4 8.9 %collective-permute-start.6 = (bf16[2,256,256]{2,1,0:T(8,128)(2,1)S(1)}, bf16[2,256,256]{2,1,0:T(8,128)(2,1)S(1)}, u32[]{:S(2)}, u32[]{:S(2)}) collective-permute-start(bf16[2,256,256]{2,1,0:T(8,128)(2,1)S(1)} %get-tuple-element.11.pairing), channel_id=1, source_target_pairs={{0,4},{1,5},{2,6},{3,7},{4,0},{5,1},{6,2},{7,3},{8,12},{9,13},{10,... | collective-permute-start | bytes 786440 | tf_op jit(solution)/shard_map/ppermute | solution.py:169
  38.0 7.3 %collective-permute-start.7 = (bf16[2,256,256]{2,1,0:T(8,128)(2,1)S(1)}, bf16[2,256,256]{2,1,0:T(8,128)(2,1)S(1)}, u32[]{:S(2)}, u32[]{:S(2)}) collective-permute-start(bf16[2,256,256]{2,1,0:T(8,128)(2,1)S(1)} %get-tuple-element.12.joining), channel_id=1, source_target_pairs={{4,8},{5,9},{6,10},{7,11},{8,4},{9,5},{10,6},{11,7},{20,24},{21,25... | collective-permute-start | bytes 786440 | tf_op jit(solution)/shard_map/ppermute | solution.py:169
  39.6 7.4 %collective-permute-start.13 = (bf16[2,256,256]{2,1,0:T(8,128)(2,1)S(1)}, bf16[2,256,256]{2,1,0:T(8,128)(2,1)S(1)}, u32[]{:S(2)}, u32[]{:S(2)}) collective-permute-start(bf16[2,256,256]{2,1,0:T(8,128)(2,1)S(1)} %shard_map.42.rhs), channel_id=1, source_target_pairs={{4,8},{5,9},{6,10},{7,11},{8,4},{9,5},{10,6},{11,7},{20,24},{21,25... | collective-permute-start | bytes 786440 | tf_op jit(solution)/shard_map/ppermute | solution.py:169
  40.3 10.9 %collective-permute-start.12 = (bf16[2,256,256]{2,1,0:T(8,128)(2,1)S(1)}, bf16[2,256,256]{2,1,0:T(8,128)(2,1)S(1)}, u32[]{:S(2)}, u32[]{:S(2)}) collective-permute-start(bf16[2,256,256]{2,1,0:T(8,128)(2,1)S(1)} %shard_map.42.rhs), channel_id=1, source_target_pairs={{0,4},{1,5},{2,6},{3,7},{4,0},{5,1},{6,2},{7,3},{8,12},{9,13},{10,... | collective-permute-start | bytes 786440 | tf_op jit(solution)/shard_map/ppermute | solution.py:169
  52.0 6.4 %collective-permute-start.14 = (bf16[2,256,256]{2,1,0:T(8,128)(2,1)S(1)}, bf16[2,256,256]{2,1,0:T(8,128)(2,1)S(1)}, u32[]{:S(2)}, u32[]{:S(2)}) collective-permute-start(bf16[2,256,256]{2,1,0:T(8,128)(2,1)S(1)} %shard_map.43), channel_id=1, source_target_pairs={{0,1},{1,3},{2,0},{3,2},{4,5},{5,7},{6,4},{7,6},{8,9},{9,11},{10,8... | collective-permute-start | bytes 786440 | tf_op jit(solution)/shard_map/ppermute | solution.py:169

commit v6 on v5

--- a/solution.py
+++ b/solution.py
@@ -131,10 +131,13 @@
     joining[...] = jnp.where(keep, far, near)
 
 
-def later_injections_kernel(held, spread, rhs, core, level, new):
-    new[...] = row_injections(
+def later_injections_kernel(held, spread, rhs, core, level, left, right):
+    new = row_injections(
         second_letter(), at(held), spread, rhs[...], core[...], level[...]
     )
+    half = left.shape[2]
+    left[...] = new[:, :, :half]
+    right[...] = new[:, :, half:]
 
 
 def last_couplings_kernel(pairing, joining, paired, joined, spread):
@@ -203,8 +206,9 @@
     core, level = move(held, *in_core), move(held, *between)
     core_rhs, level_rhs = move(rhs, *in_core), move(rhs, *between)
     pairing, joining, spread = run(later_couplings_kernel, (block,) * 3, held, core, level)
-    (rhs,) = run(
-        later_injections_kernel, (block,),
+    half_block = block[:2] + (block[2] // 2,)
+    halves = run(
+        later_injections_kernel, (half_block,) * 2,
         held, spread, rhs, core_rhs, level_rhs,
     )
 
@@ -217,14 +221,18 @@
         ]
         for start in (1, 0)
     )
-    joined, joined_rhs = trade(joining, at_joint), trade(rhs, at_joint)
-    paired, paired_rhs = trade(pairing, in_pair), trade(rhs, in_pair)
+    joined, paired = trade(joining, at_joint), trade(pairing, in_pair)
+    arrived = [(trade(half, in_pair), trade(half, at_joint)) for half in halves]
     (spread,) = run(last_couplings_kernel, (block,), pairing, joining, paired, joined)
-    (result,) = run(
-        last_injections_kernel, (block,),
-        pairing, joining, spread, rhs, paired_rhs, joined_rhs,
-    )
-    return move(result, *home)[None]
+    results = []
+    for half, (paired_half, joined_half), weight in zip(halves, arrived, (1, 1)):
+        (result,) = run(
+            last_injections_kernel, (half_block,),
+            pairing, joining, spread, half, paired_half, joined_half,
+            weight=weight,
+        )
+        results.append(move(result, *home))
+    return jnp.concatenate(results, axis=-1)[None]
 
 
 def solution(mesh):

time: 59.5 us -> 58.6 us (0.985)
  waiting for transfers between devices: 23.2 us -> 18.3 us
  starting transfers between devices: 25.7 us -> 29.2 us
  other arithmetic: 0 us -> 0.73 us
  local copies, waits for them, and re-layouts: 1.75 us -> 1.05 us
    ppermute x15 -> x18, waiting for transfers between devices: 23.2 us -> 18.3 us  [trade(): lax.ppermute(value, 'chain', [(a, b) for a, b in pairs if 0 <= a < length...]
    ppermute x15 -> x18, starting transfers between devices: 25.7 us -> 29.2 us  [trade(): lax.ppermute(value, 'chain', [(a, b) for a, b in pairs if 0 <= a < length...]
    broadcast_in_dim x0 -> x1, other arithmetic: none -> 0.73 us  [local(): return jnp.concatenate(results, axis=-1)[None]]
    unnamed x6 -> x5, local copies, waits for them, and re-layouts: 1.73 us -> 1.03 us
    pallas_call x7 -> x8, Pallas kernels: 8.28 us -> 8.78 us  [run(): pl.pallas_call(kernel, out_shape=[jax.ShapeDtypeStruct(s, jnp.bfloat16) f...]
  transfers between devices with their start and end apart: 15 -> 18, of which waited for: 5 -> 6; matrix products, arithmetic and copies ran while one was open for 0% -> 0% of each run, Pallas kernels for 13% -> 15%
where the time goes in v6:
time: 58.6 us; the launch traced here: 58.3 us
  starting transfers between devices  29.2 us (50%)
  waiting for transfers between devices  18.3 us (31%)
  Pallas kernels  8.78 us (15%)
  local copies, waits for them, and re-layouts  1.05 us (2%)
  other arithmetic  0.73 us (1%)
    ppermute x18, starting transfers between devices, trade(): lax.ppermute(value, 'chain', [(a, b) for a, b in pairs if 0 <= a < length...  29.2 us
    ppermute x18, waiting for transfers between devices, trade(): lax.ppermute(value, 'chain', [(a, b) for a, b in pairs if 0 <= a < length...  18.3 us
    pallas_call x8, Pallas kernels, run(): pl.pallas_call(kernel, out_shape=[jax.ShapeDtypeStruct(s, jnp.bfloat16) f...  8.78 us
  transfers between devices with their start and end apart: 18, of which 6 were waited for; matrix products, arithmetic and copies ran while one was open for 0% of the time, Pallas kernels for 15%

profile of v6, /device:TPU:0, one launch (start us, length us, event | category | flops | bytes accessed | tf_op | source)
XLA Modules:
  0.0 58.3 jit_solution(3349855893967626481)
XLA Ops:
  0.0 0.0 copy-start.1
  0.0 1.0 %constant_dynamic-update-slice_fusion.1 = bf16[2,2,256,256]{3,2,1,0:T(8,128)(2,1)S(1)} fusion(bf16[1,2,256,256]{3,2,1,0:T(8,128)(2,1)} %param.3), kind=kLoop, calls=%fused_computation.2 | loop fusion | bytes 524288
  1.0 0.0 copy-done.1
  1.0 0.0 copy-start
  1.1 3.0 %collective-permute-start = (bf16[2,2,256,256]{3,2,1,0:T(8,128)(2,1)S(1)}, bf16[2,2,256,256]{3,2,1,0:T(8,128)(2,1)S(1)}, u32[]{:S(2)}, u32[]{:S(2)}) collective-permute-start(bf16[2,2,256,256]{3,2,1,0:T(8,128)(2,1)S(1)} %constant_dynamic-update-slice_fusion.held), channel_id=1, source_target_pairs={{0,2},{1,3},{2,0},{3,1},{4,6},{5,7},{6,4},{7,5},{8,10},{9,11},{10,... | collective-permute-start | bytes 1572872 | tf_op jit(solution)/shard_map/ppermute | solution.py:172
  4.1 0.0 copy-done
  4.1 0.1 shard_map.37
  4.2 0.7 %collective-permute-start.3 = (bf16[3,2,256,256]{3,2,1,0:T(8,128)(2,1)S(1)}, bf16[3,2,256,256]{3,2,1,0:T(8,128)(2,1)S(1)}, u32[]{:S(2)}, u32[]{:S(2)}) collective-permute-start(bf16[3,2,256,256]{3,2,1,0:T(8,128)(2,1)S(1)} %shard_map.37), channel_id=1, source_target_pairs={{3,6},{4,1},{7,10},{8,5},{11,14},{12,9},{19,22},{20,17},{23,26},{2... | collective-permute-start | bytes 2359304 | tf_op jit(solution)/shard_map/ppermute | solution.py:172
  4.9 1.3 %collective-permute-start.1 = (bf16[3,2,256,256]{3,2,1,0:T(8,128)(2,1)S(1)}, bf16[3,2,256,256]{3,2,1,0:T(8,128)(2,1)S(1)}, u32[]{:S(2)}, u32[]{:S(2)}) collective-permute-start(bf16[3,2,256,256]{3,2,1,0:T(8,128)(2,1)S(1)} %shard_map.37), channel_id=1, source_target_pairs={{1,0},{2,3},{5,4},{6,7},{9,8},{10,11},{13,12},{14,15},{17,16},{18,... | collective-permute-start | bytes 2359304 | tf_op jit(solution)/shard_map/ppermute | solution.py:172
  6.2 9.8 %collective-permute-done.crossed = bf16[2,2,256,256]{3,2,1,0:T(8,128)(2,1)S(1)} collective-permute-done((bf16[2,2,256,256]{3,2,1,0:T(8,128)(2,1)S(1)}, bf16[2,2,256,256]{3,2,1,0:T(8,128)(2,1)S(1)}, u32[]{:S(2)}, u32[]{:S(2)}) %collective-permute-start) | collective-permute-done | bytes 524320 | tf_op jit(solution)/shard_map/ppermute | solution.py:172
  16.0 1.3 %collective-permute-start.2 = (bf16[2,2,256,256]{3,2,1,0:T(8,128)(2,1)S(1)}, bf16[2,2,256,256]{3,2,1,0:T(8,128)(2,1)S(1)}, u32[]{:S(2)}, u32[]{:S(2)}) collective-permute-start(bf16[2,2,256,256]{3,2,1,0:T(8,128)(2,1)S(1)} %collective-permute-done.crossed), channel_id=1, source_target_pairs={{0,1},{3,2},{4,5},{7,6},{8,9},{11,10},{12,13},{15,14},{16,17},{19,... | collective-permute-start | bytes 1572872 | tf_op jit(solution)/shard_map/ppermute | solution.py:172
  17.3 1.8 %collective-permute-start.8 = (bf16[2,256,256]{2,1,0:T(8,128)(2,1)S(1)}, bf16[2,256,256]{2,1,0:T(8,128)(2,1)S(1)}, u32[]{:S(2)}, u32[]{:S(2)}) collective-permute-start(bf16[2,256,256]{2,1,0:T(8,128)(2,1)S(1)} %bitcast.4), channel_id=1, source_target_pairs={{0,2},{1,3},{2,0},{3,1},{4,6},{5,7},{6,4},{7,5},{8,10},{9,11},{10,... | collective-permute-start | bytes 786440 | tf_op jit(solution)/shard_map/ppermute | solution.py:172
  19.1 0.0 collective-permute-done.3.level
  19.1 0.0 collective-permute-done.1.core
  19.1 0.0 collective-permute-done.2.onward
  19.1 1.9 %shard_map.38 = (bf16[2,2,256,256]{3,2,1,0:T(8,128)(2,1)S(1)}, bf16[2,256,256]{2,1,0:T(8,128)(2,1)S(1)}) custom-call(bf16[2,2,256,256]{3,2,1,0:T(8,128)(2,1)S(1)} %constant_dynamic-update-slice_fusion.held, bf16[2,2,256,256]{3,2,1,0:T(8,128)(2,1)S(1)} %collective-permute-done.crossed, bf16[3,2,256,256]{3,2,1,0:T(8,128)(2,1)S(1)} %collective-permute-done.1.core, ...), custom_call_target="tpu_custom_call" | custom-call | flops 1 | bytes 1 | tf_op jit(solution)/shard_map/pallas_call | solution.py:156
  21.1 0.7 %collective-permute-start.5 = (bf16[2,2,256,256]{3,2,1,0:T(8,128)(2,1)S(1)}, bf16[2,2,256,256]{3,2,1,0:T(8,128)(2,1)S(1)}, u32[]{:S(2)}, u32[]{:S(2)}) collective-permute-start(bf16[2,2,256,256]{3,2,1,0:T(8,128)(2,1)S(1)} %get-tuple-element.12.held), channel_id=1, source_target_pairs={{1,4},{3,6},{4,1},{5,8},{6,3},{7,10},{8,5},{9,12},{10,7},{11,14},{... | collective-permute-start | bytes 1572872 | tf_op jit(solution)/shard_map/ppermute | solution.py:172
  21.8 3.0 %collective-permute-start.4 = (bf16[2,2,256,256]{3,2,1,0:T(8,128)(2,1)S(1)}, bf16[2,2,256,256]{3,2,1,0:T(8,128)(2,1)S(1)}, u32[]{:S(2)}, u32[]{:S(2)}) collective-permute-start(bf16[2,2,256,256]{3,2,1,0:T(8,128)(2,1)S(1)} %get-tuple-element.12.held), channel_id=1, source_target_pairs={{0,1},{1,0},{2,3},{3,2},{4,5},{5,4},{6,7},{7,6},{8,9},{9,8},{10,11... | collective-permute-start | bytes 1572872 | tf_op jit(solution)/shard_map/ppermute | solution.py:172
  24.8 1.7 %collective-permute-done.8.crossed_rhs = bf16[2,256,256]{2,1,0:T(8,128)(2,1)S(1)} collective-permute-done((bf16[2,256,256]{2,1,0:T(8,128)(2,1)S(1)}, bf16[2,256,256]{2,1,0:T(8,128)(2,1)S(1)}, u32[]{:S(2)}, u32[]{:S(2)}) %collective-permute-start.8) | collective-permute-done | bytes 262176 | tf_op jit(solution)/shard_map/ppermute | solution.py:172
  26.4 2.0 %collective-permute-start.9 = (bf16[2,256,256]{2,1,0:T(8,128)(2,1)S(1)}, bf16[2,256,256]{2,1,0:T(8,128)(2,1)S(1)}, u32[]{:S(2)}, u32[]{:S(2)}) collective-permute-start(bf16[2,256,256]{2,1,0:T(8,128)(2,1)S(1)} %collective-permute-done.8.crossed_rhs), channel_id=1, source_target_pairs={{0,1},{3,2},{4,5},{7,6},{8,9},{11,10},{12,13},{15,14},{16,17},{19,... | collective-permute-start | bytes 786440 | tf_op jit(solution)/shard_map/ppermute | solution.py:172
  28.5 1.1 %collective-permute-done.9.onward_rhs = bf16[2,256,256]{2,1,0:T(8,128)(2,1)S(1)} collective-permute-done((bf16[2,256,256]{2,1,0:T(8,128)(2,1)S(1)}, bf16[2,256,256]{2,1,0:T(8,128)(2,1)S(1)}, u32[]{:S(2)}, u32[]{:S(2)}) %collective-permute-start.9) | collective-permute-done | bytes 262176 | tf_op jit(solution)/shard_map/ppermute | solution.py:172
  29.6 0.9 %shard_map.41.rhs = bf16[2,256,256]{2,1,0:T(8,128)(2,1)S(1)} custom-call(bf16[2,2,256,256]{3,2,1,0:T(8,128)(2,1)S(1)} %collective-permute-done.crossed, bf16[2,256,256]{2,1,0:T(8,128)(2,1)S(1)} %get-tuple-element.16.spread, bf16[2,256,256]{2,1,0:T(8,128)(2,1)S(1)} %bitcast.5, bf16[2,256,256]{2,1,0:T(8,128)(2,1)S(1)} %collective-permute-done.8.crossed_rhs, ...), custom_call_target="tpu_custom_call" | custom-call | flops 1 | bytes 1 | tf_op jit(solution)/shard_map/pallas_call | solution.py:156
  30.5 0.7 %collective-permute-start.11 = (bf16[2,256,256]{2,1,0:T(8,128)(2,1)S(1)}, bf16[2,256,256]{2,1,0:T(8,128)(2,1)S(1)}, u32[]{:S(2)}, u32[]{:S(2)}) collective-permute-start(bf16[2,256,256]{2,1,0:T(8,128)(2,1)S(1)} %shard_map.41.rhs), channel_id=1, source_target_pairs={{1,4},{3,6},{4,1},{5,8},{6,3},{7,10},{8,5},{9,12},{10,7},{11,14},{... | collective-permute-start | bytes 786440 | tf_op jit(solution)/shard_map/ppermute | solution.py:172
  31.2 3.2 %collective-permute-start.10 = (bf16[2,256,256]{2,1,0:T(8,128)(2,1)S(1)}, bf16[2,256,256]{2,1,0:T(8,128)(2,1)S(1)}, u32[]{:S(2)}, u32[]{:S(2)}) collective-permute-start(bf16[2,256,256]{2,1,0:T(8,128)(2,1)S(1)} %shard_map.41.rhs), channel_id=1, source_target_pairs={{0,1},{1,0},{2,3},{3,2},{4,5},{5,4},{6,7},{7,6},{8,9},{9,8},{10,11... | collective-permute-start | bytes 786440 | tf_op jit(solution)/shard_map/ppermute | solution.py:172
  34.4 0.0 collective-permute-done.5.level
  34.4 0.0 collective-permute-done.4.core
  34.4 1.9 %shard_map.39 = (bf16[2,256,256]{2,1,0:T(8,128)(2,1)S(1)}, bf16[2,256,256]{2,1,0:T(8,128)(2,1)S(1)}, bf16[2,256,256]{2,1,0:T(8,128)(2,1)S(1)}) custom-call(bf16[2,2,256,256]{3,2,1,0:T(8,128)(2,1)S(1)} %get-tuple-element.12.held, bf16[2,2,256,256]{3,2,1,0:T(8,128)(2,1)S(1)} %collective-permute-done.4.core, ...), custom_call_target="tpu_custom_call" | custom-call | flops 1 | bytes 1 | tf_op jit(solution)/shard_map/pallas_call | solution.py:156
  36.4 1.6 %collective-permute-start.6 = (bf16[2,256,256]{2,1,0:T(8,128)(2,1)S(1)}, bf16[2,256,256]{2,1,0:T(8,128)(2,1)S(1)}, u32[]{:S(2)}, u32[]{:S(2)}) collective-permute-start(bf16[2,256,256]{2,1,0:T(8,128)(2,1)S(1)} %get-tuple-element.13.pairing), channel_id=1, source_target_pairs={{0,4},{1,5},{2,6},{3,7},{4,0},{5,1},{6,2},{7,3},{8,12},{9,13},{10,... | collective-permute-start | bytes 786440 | tf_op jit(solution)/shard_map/ppermute | solution.py:172
  38.0 0.7 %collective-permute-start.7 = (bf16[2,256,256]{2,1,0:T(8,128)(2,1)S(1)}, bf16[2,256,256]{2,1,0:T(8,128)(2,1)S(1)}, u32[]{:S(2)}, u32[]{:S(2)}) collective-permute-start(bf16[2,256,256]{2,1,0:T(8,128)(2,1)S(1)} %get-tuple-element.14.joining), channel_id=1, source_target_pairs={{4,8},{5,9},{6,10},{7,11},{8,4},{9,5},{10,6},{11,7},{20,24},{21,25... | collective-permute-start | bytes 786440 | tf_op jit(solution)/shard_map/ppermute | solution.py:172
  38.7 0.0 collective-permute-done.11.level
  38.7 0.0 collective-permute-done.10.core
  38.7 0.9 %shard_map.42 = (bf16[2,256,128]{2,1,0:T(8,128)(2,1)S(1)}, bf16[2,256,128]{2,1,0:T(8,128)(2,1)S(1)}) custom-call(bf16[2,2,256,256]{3,2,1,0:T(8,128)(2,1)S(1)} %get-tuple-element.12.held, bf16[2,256,256]{2,1,0:T(8,128)(2,1)S(1)} %get-tuple-element.15.spread, bf16[2,256,256]{2,1,0:T(8,128)(2,1)S(1)} %shard_map.41.rhs, ...), custom_call_target="tpu_custom_call" | custom-call | flops 1 | bytes 1 | tf_op jit(solution)/shard_map/pallas_call | solution.py:156
  39.6 0.7 %collective-permute-start.13 = (bf16[2,256,128]{2,1,0:T(8,128)(2,1)S(1)}, bf16[2,256,128]{2,1,0:T(8,128)(2,1)S(1)}, u32[]{:S(2)}, u32[]{:S(2)}) collective-permute-start(bf16[2,256,128]{2,1,0:T(8,128)(2,1)S(1)} %get-tuple-element.17.rhs), channel_id=1, source_target_pairs={{4,8},{5,9},{6,10},{7,11},{8,4},{9,5},{10,6},{11,7},{20,24},{21,25... | collective-permute-start | bytes 393224 | tf_op jit(solution)/shard_map/ppermute | solution.py:172
  40.3 5.0 %collective-permute-start.12 = (bf16[2,256,128]{2,1,0:T(8,128)(2,1)S(1)}, bf16[2,256,128]{2,1,0:T(8,128)(2,1)S(1)}, u32[]{:S(2)}, u32[]{:S(2)}) collective-permute-start(bf16[2,256,128]{2,1,0:T(8,128)(2,1)S(1)} %get-tuple-element.17.rhs), channel_id=1, source_target_pairs={{0,4},{1,5},{2,6},{3,7},{4,0},{5,1},{6,2},{7,3},{8,12},{9,13},{10,... | collective-permute-start | bytes 393224 | tf_op jit(solution)/shard_map/ppermute | solution.py:172
  45.3 0.7 %collective-permute-start.16 = (bf16[2,256,128]{2,1,0:T(8,128)(2,1)S(1)}, bf16[2,256,128]{2,1,0:T(8,128)(2,1)S(1)}, u32[]{:S(2)}, u32[]{:S(2)}) collective-permute-start(bf16[2,256,128]{2,1,0:T(8,128)(2,1)S(1)} %get-tuple-element.18.rhs), channel_id=1, source_target_pairs={{4,8},{5,9},{6,10},{7,11},{8,4},{9,5},{10,6},{11,7},{20,24},{21,25... | collective-permute-start | bytes 393224 | tf_op jit(solution)/shard_map/ppermute | solution.py:172
  45.9 0.0 collective-permute-done.6.paired
  46.0 2.8 %collective-permute-start.15 = (bf16[2,256,128]{2,1,0:T(8,128)(2,1)S(1)}, bf16[2,256,128]{2,1,0:T(8,128)(2,1)S(1)}, u32[]{:S(2)}, u32[]{:S(2)}) collective-permute-start(bf16[2,256,128]{2,1,0:T(8,128)(2,1)S(1)} %get-tuple-element.18.rhs), channel_id=1, source_target_pairs={{0,4},{1,5},{2,6},{3,7},{4,0},{5,1},{6,2},{7,3},{8,12},{9,13},{10,... | collective-permute-start | bytes 393224 | tf_op jit(solution)/shard_map/ppermute | solution.py:172
  48.8 0.0 collective-permute-done.7.joined
  48.8 1.7 %shard_map.40.spread = bf16[2,256,256]{2,1,0:T(8,128)(2,1)S(1)} custom-call(bf16[2,256,256]{2,1,0:T(8,128)(2,1)S(1)} %get-tuple-element.13.pairing, bf16[2,256,256]{2,1,0:T(8,128)(2,1)S(1)} %get-tuple-element.14.joining, bf16[2,256,256]{2,1,0:T(8,128)(2,1)S(1)} %collective-permute-done.6.paired, bf16[2,256,256]{2,1,0:T(8,128)(2,1)S(1)} %collective-permute-done.7.joined), custom_call_target="tpu_custom_call" | custom-call | flops 1 | bytes 1 | tf_op jit(solution)/shard_map/pallas_call | solution.py:156
  50.4 0.0 collective-permute-done.13.joined
  50.4 0.0 collective-permute-done.12.paired
  50.5 0.7 %shard_map.43 = bf16[2,256,128]{2,1,0:T(8,128)(2,1)S(1)} custom-call(bf16[2,256,256]{2,1,0:T(8,128)(2,1)S(1)} %get-tuple-element.13.pairing, bf16[2,256,256]{2,1,0:T(8,128)(2,1)S(1)} %get-tuple-element.14.joining, bf16[2,256,256]{2,1,0:T(8,128)(2,1)S(1)} %shard_map.40.spread, bf16[2,256,128]{2,1,0:T(8,128)(2,1)S(1)} %get-tuple-element.17.rhs, ...), custom_call_target="tpu_custom_call" | custom-call | flops 1 | bytes 1 | tf_op jit(solution)/shard_map/pallas_call | solution.py:156
  51.2 0.0 collective-permute-start.14
  51.2 0.0 collective-permute-done.16.joined
  51.2 0.6 collective-permute-done.15.paired
  51.8 0.7 %shard_map.44 = bf16[2,256,128]{2,1,0:T(8,128)(2,1)S(1)} custom-call(bf16[2,256,256]{2,1,0:T(8,128)(2,1)S(1)} %get-tuple-element.13.pairing, bf16[2,256,256]{2,1,0:T(8,128)(2,1)S(1)} %get-tuple-element.14.joining, bf16[2,256,256]{2,1,0:T(8,128)(2,1)S(1)} %shard_map.40.spread, bf16[2,256,128]{2,1,0:T(8,128)(2,1)S(1)} %get-tuple-element.18.rhs, ...), custom_call_target="tpu_custom_call" | custom-call | flops 1 | bytes 1 | tf_op jit(solution)/shard_map/pallas_call | solution.py:156
  52.5 0.0 collective-permute-start.17
  52.5 3.6 %collective-permute-done.14 = bf16[2,256,128]{2,1,0:T(8,128)(2,1)S(1)} collective-permute-done((bf16[2,256,128]{2,1,0:T(8,128)(2,1)S(1)}, bf16[2,256,128]{2,1,0:T(8,128)(2,1)S(1)}, u32[]{:S(2)}, u32[]{:S(2)}) %collective-permute-start.14) | collective-permute-done | bytes 131104 | tf_op jit(solution)/shard_map/ppermute | solution.py:172
  56.1 1.4 %collective-permute-done.17 = bf16[2,256,128]{2,1,0:T(8,128)(2,1)S(1)} collective-permute-done((bf16[2,256,128]{2,1,0:T(8,128)(2,1)S(1)}, bf16[2,256,128]{2,1,0:T(8,128)(2,1)S(1)}, u32[]{:S(2)}, u32[]{:S(2)}) %collective-permute-start.17) | collective-permute-done | bytes 131104 | tf_op jit(solution)/shard_map/ppermute | solution.py:172
  57.5 0.7 %maximum_bitcast_fusion = bf16[1,2,256,256]{3,2,1,0:T(8,128)(2,1)} fusion(bf16[2,256,128]{2,1,0:T(8,128)(2,1)S(1)} %collective-permute-done.17, bf16[2,256,128]{2,1,0:T(8,128)(2,1)S(1)} %collective-permute-done.14), kind=kLoop, calls=%fused_computation | loop fusion | flops 524288 | bytes 524288 | tf_op jit(solution)/shard_map/broadcast_in_dim | solution.py:235
  (1 shorter events, 0.0 us)
Async XLA Ops:
  0.0 1.0 %copy-start.1 = (bf16[1,2,256,256]{3,2,1,0:T(8,128)(2,1)S(1)}, bf16[1,2,256,256]{3,2,1,0:T(8,128)(2,1)}, u32[]{:S(2)}) copy-start(bf16[1,2,256,256]{3,2,1,0:T(8,128)(2,1)} %param.4) | copy-start | bytes 786436
  1.0 3.1 %copy-start = (bf16[1,2,256,256]{3,2,1,0:T(8,128)(2,1)S(1)}, bf16[1,2,256,256]{3,2,1,0:T(8,128)(2,1)}, u32[]{:S(2)}) copy-start(bf16[1,2,256,256]{3,2,1,0:T(8,128)(2,1)} %param.5) | copy-start | bytes 786436
  1.1 15.0 %collective-permute-start = (bf16[2,2,256,256]{3,2,1,0:T(8,128)(2,1)S(1)}, bf16[2,2,256,256]{3,2,1,0:T(8,128)(2,1)S(1)}, u32[]{:S(2)}, u32[]{:S(2)}) collective-permute-start(bf16[2,2,256,256]{3,2,1,0:T(8,128)(2,1)S(1)} %constant_dynamic-update-slice_fusion.held), channel_id=1, source_target_pairs={{0,2},{1,3},{2,0},{3,1},{4,6},{5,7},{6,4},{7,5},{8,10},{9,11},{10,... | collective-permute-start | bytes 1572872 | tf_op jit(solution)/shard_map/ppermute | solution.py:172
  4.2 15.0 %collective-permute-start.3 = (bf16[3,2,256,256]{3,2,1,0:T(8,128)(2,1)S(1)}, bf16[3,2,256,256]{3,2,1,0:T(8,128)(2,1)S(1)}, u32[]{:S(2)}, u32[]{:S(2)}) collective-permute-start(bf16[3,2,256,256]{3,2,1,0:T(8,128)(2,1)S(1)} %shard_map.37), channel_id=1, source_target_pairs={{3,6},{4,1},{7,10},{8,5},{11,14},{12,9},{19,22},{20,17},{23,26},{2... | collective-permute-start | bytes 2359304 | tf_op jit(solution)/shard_map/ppermute | solution.py:172
  4.9 14.2 %collective-permute-start.1 = (bf16[3,2,256,256]{3,2,1,0:T(8,128)(2,1)S(1)}, bf16[3,2,256,256]{3,2,1,0:T(8,128)(2,1)S(1)}, u32[]{:S(2)}, u32[]{:S(2)}) collective-permute-start(bf16[3,2,256,256]{3,2,1,0:T(8,128)(2,1)S(1)} %shard_map.37), channel_id=1, source_target_pairs={{1,0},{2,3},{5,4},{6,7},{9,8},{10,11},{13,12},{14,15},{17,16},{18,... | collective-permute-start | bytes 2359304 | tf_op jit(solution)/shard_map/ppermute | solution.py:172
  16.0 3.1 %collective-permute-start.2 = (bf16[2,2,256,256]{3,2,1,0:T(8,128)(2,1)S(1)}, bf16[2,2,256,256]{3,2,1,0:T(8,128)(2,1)S(1)}, u32[]{:S(2)}, u32[]{:S(2)}) collective-permute-start(bf16[2,2,256,256]{3,2,1,0:T(8,128)(2,1)S(1)} %collective-permute-done.crossed), channel_id=1, source_target_pairs={{0,1},{3,2},{4,5},{7,6},{8,9},{11,10},{12,13},{15,14},{16,17},{19,... | collective-permute-start | bytes 1572872 | tf_op jit(solution)/shard_map/ppermute | solution.py:172
  17.3 9.1 %collective-permute-start.8 = (bf16[2,256,256]{2,1,0:T(8,128)(2,1)S(1)}, bf16[2,256,256]{2,1,0:T(8,128)(2,1)S(1)}, u32[]{:S(2)}, u32[]{:S(2)}) collective-permute-start(bf16[2,256,256]{2,1,0:T(8,128)(2,1)S(1)} %bitcast.4), channel_id=1, source_target_pairs={{0,2},{1,3},{2,0},{3,1},{4,6},{5,7},{6,4},{7,5},{8,10},{9,11},{10,... | collective-permute-start | bytes 786440 | tf_op jit(solution)/shard_map/ppermute | solution.py:172
  21.1 13.3 %collective-permute-start.5 = (bf16[2,2,256,256]{3,2,1,0:T(8,128)(2,1)S(1)}, bf16[2,2,256,256]{3,2,1,0:T(8,128)(2,1)S(1)}, u32[]{:S(2)}, u32[]{:S(2)}) collective-permute-start(bf16[2,2,256,256]{3,2,1,0:T(8,128)(2,1)S(1)} %get-tuple-element.12.held), channel_id=1, source_target_pairs={{1,4},{3,6},{4,1},{5,8},{6,3},{7,10},{8,5},{9,12},{10,7},{11,14},{... | collective-permute-start | bytes 1572872 | tf_op jit(solution)/shard_map/ppermute | solution.py:172
  21.8 12.6 %collective-permute-start.4 = (bf16[2,2,256,256]{3,2,1,0:T(8,128)(2,1)S(1)}, bf16[2,2,256,256]{3,2,1,0:T(8,128)(2,1)S(1)}, u32[]{:S(2)}, u32[]{:S(2)}) collective-permute-start(bf16[2,2,256,256]{3,2,1,0:T(8,128)(2,1)S(1)} %get-tuple-element.12.held), channel_id=1, source_target_pairs={{0,1},{1,0},{2,3},{3,2},{4,5},{5,4},{6,7},{7,6},{8,9},{9,8},{10,11... | collective-permute-start | bytes 1572872 | tf_op jit(solution)/shard_map/ppermute | solution.py:172
  26.4 3.2 %collective-permute-start.9 = (bf16[2,256,256]{2,1,0:T(8,128)(2,1)S(1)}, bf16[2,256,256]{2,1,0:T(8,128)(2,1)S(1)}, u32[]{:S(2)}, u32[]{:S(2)}) collective-permute-start(bf16[2,256,256]{2,1,0:T(8,128)(2,1)S(1)} %collective-permute-done.8.crossed_rhs), channel_id=1, source_target_pairs={{0,1},{3,2},{4,5},{7,6},{8,9},{11,10},{12,13},{15,14},{16,17},{19,... | collective-permute-start | bytes 786440 | tf_op jit(solution)/shard_map/ppermute | solution.py:172
  30.5 8.2 %collective-permute-start.11 = (bf16[2,256,256]{2,1,0:T(8,128)(2,1)S(1)}, bf16[2,256,256]{2,1,0:T(8,128)(2,1)S(1)}, u32[]{:S(2)}, u32[]{:S(2)}) collective-permute-start(bf16[2,256,256]{2,1,0:T(8,128)(2,1)S(1)} %shard_map.41.rhs), channel_id=1, source_target_pairs={{1,4},{3,6},{4,1},{5,8},{6,3},{7,10},{8,5},{9,12},{10,7},{11,14},{... | collective-permute-start | bytes 786440 | tf_op jit(solution)/shard_map/ppermute | solution.py:172
  31.2 7.5 %collective-permute-start.10 = (bf16[2,256,256]{2,1,0:T(8,128)(2,1)S(1)}, bf16[2,256,256]{2,1,0:T(8,128)(2,1)S(1)}, u32[]{:S(2)}, u32[]{:S(2)}) collective-permute-start(bf16[2,256,256]{2,1,0:T(8,128)(2,1)S(1)} %shard_map.41.rhs), channel_id=1, source_target_pairs={{0,1},{1,0},{2,3},{3,2},{4,5},{5,4},{6,7},{7,6},{8,9},{9,8},{10,11... | collective-permute-start | bytes 786440 | tf_op jit(solution)/shard_map/ppermute | solution.py:172
  36.4 9.6 %collective-permute-start.6 = (bf16[2,256,256]{2,1,0:T(8,128)(2,1)S(1)}, bf16[2,256,256]{2,1,0:T(8,128)(2,1)S(1)}, u32[]{:S(2)}, u32[]{:S(2)}) collective-permute-start(bf16[2,256,256]{2,1,0:T(8,128)(2,1)S(1)} %get-tuple-element.13.pairing), channel_id=1, source_target_pairs={{0,4},{1,5},{2,6},{3,7},{4,0},{5,1},{6,2},{7,3},{8,12},{9,13},{10,... | collective-permute-start | bytes 786440 | tf_op jit(solution)/shard_map/ppermute | solution.py:172
  38.0 10.8 %collective-permute-start.7 = (bf16[2,256,256]{2,1,0:T(8,128)(2,1)S(1)}, bf16[2,256,256]{2,1,0:T(8,128)(2,1)S(1)}, u32[]{:S(2)}, u32[]{:S(2)}) collective-permute-start(bf16[2,256,256]{2,1,0:T(8,128)(2,1)S(1)} %get-tuple-element.14.joining), channel_id=1, source_target_pairs={{4,8},{5,9},{6,10},{7,11},{8,4},{9,5},{10,6},{11,7},{20,24},{21,25... | collective-permute-start | bytes 786440 | tf_op jit(solution)/shard_map/ppermute | solution.py:172
  39.6 10.8 %collective-permute-start.13 = (bf16[2,256,128]{2,1,0:T(8,128)(2,1)S(1)}, bf16[2,256,128]{2,1,0:T(8,128)(2,1)S(1)}, u32[]{:S(2)}, u32[]{:S(2)}) collective-permute-start(bf16[2,256,128]{2,1,0:T(8,128)(2,1)S(1)} %get-tuple-element.17.rhs), channel_id=1, source_target_pairs={{4,8},{5,9},{6,10},{7,11},{8,4},{9,5},{10,6},{11,7},{20,24},{21,25... | collective-permute-start | bytes 393224 | tf_op jit(solution)/shard_map/ppermute | solution.py:172
  40.3 10.2 %collective-permute-start.12 = (bf16[2,256,128]{2,1,0:T(8,128)(2,1)S(1)}, bf16[2,256,128]{2,1,0:T(8,128)(2,1)S(1)}, u32[]{:S(2)}, u32[]{:S(2)}) collective-permute-start(bf16[2,256,128]{2,1,0:T(8,128)(2,1)S(1)} %get-tuple-element.17.rhs), channel_id=1, source_target_pairs={{0,4},{1,5},{2,6},{3,7},{4,0},{5,1},{6,2},{7,3},{8,12},{9,13},{10,... | collective-permute-start | bytes 393224 | tf_op jit(solution)/shard_map/ppermute | solution.py:172
  45.3 5.9 %collective-permute-start.16 = (bf16[2,256,128]{2,1,0:T(8,128)(2,1)S(1)}, bf16[2,256,128]{2,1,0:T(8,128)(2,1)S(1)}, u32[]{:S(2)}, u32[]{:S(2)}) collective-permute-start(bf16[2,256,128]{2,1,0:T(8,128)(2,1)S(1)} %get-tuple-element.18.rhs), channel_id=1, source_target_pairs={{4,8},{5,9},{6,10},{7,11},{8,4},{9,5},{10,6},{11,7},{20,24},{21,25... | collective-permute-start | bytes 393224 | tf_op jit(solution)/shard_map/ppermute | solution.py:172
  46.0 5.8 %collective-permute-start.15 = (bf16[2,256,128]{2,1,0:T(8,128)(2,1)S(1)}, bf16[2,256,128]{2,1,0:T(8,128)(2,1)S(1)}, u32[]{:S(2)}, u32[]{:S(2)}) collective-permute-start(bf16[2,256,128]{2,1,0:T(8,128)(2,1)S(1)} %get-tuple-element.18.rhs), channel_id=1, source_target_pairs={{0,4},{1,5},{2,6},{3,7},{4,0},{5,1},{6,2},{7,3},{8,12},{9,13},{10,... | collective-permute-start | bytes 393224 | tf_op jit(solution)/shard_map/ppermute | solution.py:172
  51.2 5.0 %collective-permute-start.14 = (bf16[2,256,128]{2,1,0:T(8,128)(2,1)S(1)}, bf16[2,256,128]{2,1,0:T(8,128)(2,1)S(1)}, u32[]{:S(2)}, u32[]{:S(2)}) collective-permute-start(bf16[2,256,128]{2,1,0:T(8,128)(2,1)S(1)} %shard_map.43), channel_id=1, source_target_pairs={{0,1},{1,3},{2,0},{3,2},{4,5},{5,7},{6,4},{7,6},{8,9},{9,11},{10,8... | collective-permute-start | bytes 393224 | tf_op jit(solution)/shard_map/ppermute | solution.py:172
  52.5 5.1 %collective-permute-start.17 = (bf16[2,256,128]{2,1,0:T(8,128)(2,1)S(1)}, bf16[2,256,128]{2,1,0:T(8,128)(2,1)S(1)}, u32[]{:S(2)}, u32[]{:S(2)}) collective-permute-start(bf16[2,256,128]{2,1,0:T(8,128)(2,1)S(1)} %shard_map.44), channel_id=1, source_target_pairs={{0,1},{1,3},{2,0},{3,2},{4,5},{5,7},{6,4},{7,6},{8,9},{9,11},{10,8... | collective-permute-start | bytes 393224 | tf_op jit(solution)/shard_map/ppermute | solution.py:172

commit v7 on v6

--- a/solution.py
+++ b/solution.py
@@ -98,13 +98,17 @@
     )
 
 
-def first_injections_kernel(
-    crossed, spread, rhs, crossed_rhs, core, onward_rhs, level, new
-):
+def near_injections_kernel(packed, core, sent):
+    letter = jnp.where(spot_of(GROUP) < GROUP // 2, UPP, LOW)
+    raw = tall(packed[RHS]).astype(jnp.float32)
+    sent[...] = parts(low(raw - product(wide(packed[letter]), tall(core[RHS]))))
+
+
+def first_injections_kernel(crossed, spread, rhs, crossed_rhs, core, level, new):
     spot = spot_of(GROUP)
     edge = (spot == 1) | (spot == 2)
     own_rhs = jnp.where(edge, crossed_rhs[...], core[RHS])
-    near = jnp.where(edge, onward_rhs[...], rhs[...])
+    near = jnp.where(edge, jnp.zeros(rhs.shape, rhs.dtype), rhs[...])
     far = jnp.where(edge, level[RHS], crossed_rhs[...])
     new[...] = row_injections(
         first_letter(), on_edge(crossed, core), spread, own_rhs, near, far
@@ -190,16 +194,16 @@
     (packed,) = run(pack_kernel, ((3,) + block,), held, rhs)
     level = move(packed, *levels)
     core = move(packed, *inward)
-    crossed_rhs = move(rhs, *mirrored)
+    (sent_rhs,) = run(near_injections_kernel, (block,), packed, core)
+    crossed_rhs = move(sent_rhs, *mirrored)
     onward = move(crossed, *outward)
-    onward_rhs = move(crossed_rhs, *outward)
     new_held, spread = run(
         first_couplings_kernel, (pair, block), held, crossed, core, onward, level, weight=1
     )
     (rhs,) = run(
         first_injections_kernel, (block,),
-        crossed, spread, rhs, crossed_rhs, core, onward_rhs, level,
-        weight=1,
+        crossed, spread, rhs, crossed_rhs, core, level,
+        weight=10**11,
     )
     held = new_held
 

time: 58.6 us -> 57.4 us (0.980)
  waiting for transfers between devices: 18.3 us -> 17.3 us
    ppermute x18 -> x17, waiting for transfers between devices: 18.3 us -> 17.3 us  [trade(): lax.ppermute(value, 'chain', [(a, b) for a, b in pairs if 0 <= a < length...]
    ppermute x18 -> x17, starting transfers between devices: 29.2 us -> 28.7 us  [trade(): lax.ppermute(value, 'chain', [(a, b) for a, b in pairs if 0 <= a < length...]
    pallas_call x8 -> x9, Pallas kernels: 8.78 us -> 9.04 us  [run(): pl.pallas_call(kernel, out_shape=[jax.ShapeDtypeStruct(s, jnp.bfloat16) f...]
  transfers between devices with their start and end apart: 18 -> 17, of which waited for: 6 -> 5; matrix products, arithmetic and copies ran while one was open for 0% -> 0% of each run, Pallas kernels for 15% -> 16%
where the time goes in v7:
time: 57.4 us; the launch traced here: 57.1 us
  starting transfers between devices  28.7 us (50%)
  waiting for transfers between devices  17.3 us (30%)
  Pallas kernels  9.04 us (16%)
  local copies, waits for them, and re-layouts  1.05 us (2%)
  other arithmetic  0.73 us (1%)
    ppermute x17, starting transfers between devices, trade(): lax.ppermute(value, 'chain', [(a, b) for a, b in pairs if 0 <= a < length...  28.7 us
    ppermute x17, waiting for transfers between devices, trade(): lax.ppermute(value, 'chain', [(a, b) for a, b in pairs if 0 <= a < length...  17.3 us
    pallas_call x9, Pallas kernels, run(): pl.pallas_call(kernel, out_shape=[jax.ShapeDtypeStruct(s, jnp.bfloat16) f...  9.04 us
  transfers between devices with their start and end apart: 17, of which 5 were waited for; matrix products, arithmetic and copies ran while one was open for 0% of the time, Pallas kernels for 16%

profile of v7, /device:TPU:0, one launch (start us, length us, event | category | flops | bytes accessed | tf_op | source)
XLA Modules:
  0.0 57.1 jit_solution(17961437593600696008)
XLA Ops:
  0.0 0.0 copy-start.1
  0.0 1.0 %constant_dynamic-update-slice_fusion.1 = bf16[2,2,256,256]{3,2,1,0:T(8,128)(2,1)S(1)} fusion(bf16[1,2,256,256]{3,2,1,0:T(8,128)(2,1)} %param.3), kind=kLoop, calls=%fused_computation.2 | loop fusion | bytes 524288
  1.0 0.0 copy-done.1
  1.0 0.0 copy-start
  1.1 3.0 %collective-permute-start = (bf16[2,2,256,256]{3,2,1,0:T(8,128)(2,1)S(1)}, bf16[2,2,256,256]{3,2,1,0:T(8,128)(2,1)S(1)}, u32[]{:S(2)}, u32[]{:S(2)}) collective-permute-start(bf16[2,2,256,256]{3,2,1,0:T(8,128)(2,1)S(1)} %constant_dynamic-update-slice_fusion.held), channel_id=1, source_target_pairs={{0,2},{1,3},{2,0},{3,1},{4,6},{5,7},{6,4},{7,5},{8,10},{9,11},{10,... | collective-permute-start | bytes 1572872 | tf_op jit(solution)/shard_map/ppermute | solution.py:176
  4.1 0.0 copy-done
  4.1 0.1 shard_map.37.packed
  4.2 1.3 %collective-permute-start.1 = (bf16[3,2,256,256]{3,2,1,0:T(8,128)(2,1)S(1)}, bf16[3,2,256,256]{3,2,1,0:T(8,128)(2,1)S(1)}, u32[]{:S(2)}, u32[]{:S(2)}) collective-permute-start(bf16[3,2,256,256]{3,2,1,0:T(8,128)(2,1)S(1)} %shard_map.37.packed), channel_id=1, source_target_pairs={{1,0},{2,3},{5,4},{6,7},{9,8},{10,11},{13,12},{14,15},{17,16},{18,... | collective-permute-start | bytes 2359304 | tf_op jit(solution)/shard_map/ppermute | solution.py:176
  5.5 0.7 %collective-permute-start.3 = (bf16[3,2,256,256]{3,2,1,0:T(8,128)(2,1)S(1)}, bf16[3,2,256,256]{3,2,1,0:T(8,128)(2,1)S(1)}, u32[]{:S(2)}, u32[]{:S(2)}) collective-permute-start(bf16[3,2,256,256]{3,2,1,0:T(8,128)(2,1)S(1)} %shard_map.37.packed), channel_id=1, source_target_pairs={{3,6},{4,1},{7,10},{8,5},{11,14},{12,9},{19,22},{20,17},{23,26},{2... | collective-permute-start | bytes 2359304 | tf_op jit(solution)/shard_map/ppermute | solution.py:176
  6.2 9.8 %collective-permute-done.crossed = bf16[2,2,256,256]{3,2,1,0:T(8,128)(2,1)S(1)} collective-permute-done((bf16[2,2,256,256]{3,2,1,0:T(8,128)(2,1)S(1)}, bf16[2,2,256,256]{3,2,1,0:T(8,128)(2,1)S(1)}, u32[]{:S(2)}, u32[]{:S(2)}) %collective-permute-start) | collective-permute-done | bytes 524320 | tf_op jit(solution)/shard_map/ppermute | solution.py:176
  16.0 1.3 %collective-permute-start.2 = (bf16[2,2,256,256]{3,2,1,0:T(8,128)(2,1)S(1)}, bf16[2,2,256,256]{3,2,1,0:T(8,128)(2,1)S(1)}, u32[]{:S(2)}, u32[]{:S(2)}) collective-permute-start(bf16[2,2,256,256]{3,2,1,0:T(8,128)(2,1)S(1)} %collective-permute-done.crossed), channel_id=1, source_target_pairs={{0,1},{3,2},{4,5},{7,6},{8,9},{11,10},{12,13},{15,14},{16,17},{19,... | collective-permute-start | bytes 1572872 | tf_op jit(solution)/shard_map/ppermute | solution.py:176
  17.3 0.0 collective-permute-done.1.core
  17.4 0.3 shard_map.41
  17.7 1.8 %collective-permute-start.8 = (bf16[2,256,256]{2,1,0:T(8,128)(2,1)S(1)}, bf16[2,256,256]{2,1,0:T(8,128)(2,1)S(1)}, u32[]{:S(2)}, u32[]{:S(2)}) collective-permute-start(bf16[2,256,256]{2,1,0:T(8,128)(2,1)S(1)} %shard_map.41), channel_id=1, source_target_pairs={{0,2},{1,3},{2,0},{3,1},{4,6},{5,7},{6,4},{7,5},{8,10},{9,11},{10,... | collective-permute-start | bytes 786440 | tf_op jit(solution)/shard_map/ppermute | solution.py:176
  19.4 0.0 collective-permute-done.3.level
  19.4 0.0 collective-permute-done.2.onward
  19.4 1.9 %shard_map.38 = (bf16[2,2,256,256]{3,2,1,0:T(8,128)(2,1)S(1)}, bf16[2,256,256]{2,1,0:T(8,128)(2,1)S(1)}) custom-call(bf16[2,2,256,256]{3,2,1,0:T(8,128)(2,1)S(1)} %constant_dynamic-update-slice_fusion.held, bf16[2,2,256,256]{3,2,1,0:T(8,128)(2,1)S(1)} %collective-permute-done.crossed, bf16[3,2,256,256]{3,2,1,0:T(8,128)(2,1)S(1)} %collective-permute-done.1.core, ...), custom_call_target="tpu_custom_call" | custom-call | flops 1 | bytes 1 | tf_op jit(solution)/shard_map/pallas_call | solution.py:160
  21.4 0.7 %collective-permute-start.5 = (bf16[2,2,256,256]{3,2,1,0:T(8,128)(2,1)S(1)}, bf16[2,2,256,256]{3,2,1,0:T(8,128)(2,1)S(1)}, u32[]{:S(2)}, u32[]{:S(2)}) collective-permute-start(bf16[2,2,256,256]{3,2,1,0:T(8,128)(2,1)S(1)} %get-tuple-element.12.held), channel_id=1, source_target_pairs={{1,4},{3,6},{4,1},{5,8},{6,3},{7,10},{8,5},{9,12},{10,7},{11,14},{... | collective-permute-start | bytes 1572872 | tf_op jit(solution)/shard_map/ppermute | solution.py:176
  22.1 3.0 %collective-permute-start.4 = (bf16[2,2,256,256]{3,2,1,0:T(8,128)(2,1)S(1)}, bf16[2,2,256,256]{3,2,1,0:T(8,128)(2,1)S(1)}, u32[]{:S(2)}, u32[]{:S(2)}) collective-permute-start(bf16[2,2,256,256]{3,2,1,0:T(8,128)(2,1)S(1)} %get-tuple-element.12.held), channel_id=1, source_target_pairs={{0,1},{1,0},{2,3},{3,2},{4,5},{5,4},{6,7},{7,6},{8,9},{9,8},{10,11... | collective-permute-start | bytes 1572872 | tf_op jit(solution)/shard_map/ppermute | solution.py:176
  25.0 1.7 %collective-permute-done.8.crossed_rhs = bf16[2,256,256]{2,1,0:T(8,128)(2,1)S(1)} collective-permute-done((bf16[2,256,256]{2,1,0:T(8,128)(2,1)S(1)}, bf16[2,256,256]{2,1,0:T(8,128)(2,1)S(1)}, u32[]{:S(2)}, u32[]{:S(2)}) %collective-permute-start.8) | collective-permute-done | bytes 262176 | tf_op jit(solution)/shard_map/ppermute | solution.py:176
  26.7 0.9 %shard_map.42.rhs = bf16[2,256,256]{2,1,0:T(8,128)(2,1)S(1)} custom-call(bf16[2,2,256,256]{3,2,1,0:T(8,128)(2,1)S(1)} %collective-permute-done.crossed, bf16[2,256,256]{2,1,0:T(8,128)(2,1)S(1)} %get-tuple-element.16.spread, bf16[2,256,256]{2,1,0:T(8,128)(2,1)S(1)} %bitcast.4, bf16[2,256,256]{2,1,0:T(8,128)(2,1)S(1)} %collective-permute-done.8.crossed_rhs, ...), custom_call_target="tpu_custom_call" | custom-call | flops 99999997952 | bytes 1 | tf_op jit(solution)/shard_map/pallas_call | solution.py:160
  27.6 0.7 %collective-permute-start.10 = (bf16[2,256,256]{2,1,0:T(8,128)(2,1)S(1)}, bf16[2,256,256]{2,1,0:T(8,128)(2,1)S(1)}, u32[]{:S(2)}, u32[]{:S(2)}) collective-permute-start(bf16[2,256,256]{2,1,0:T(8,128)(2,1)S(1)} %shard_map.42.rhs), channel_id=1, source_target_pairs={{1,4},{3,6},{4,1},{5,8},{6,3},{7,10},{8,5},{9,12},{10,7},{11,14},{... | collective-permute-start | bytes 786440 | tf_op jit(solution)/shard_map/ppermute | solution.py:176
  28.3 3.3 %collective-permute-start.9 = (bf16[2,256,256]{2,1,0:T(8,128)(2,1)S(1)}, bf16[2,256,256]{2,1,0:T(8,128)(2,1)S(1)}, u32[]{:S(2)}, u32[]{:S(2)}) collective-permute-start(bf16[2,256,256]{2,1,0:T(8,128)(2,1)S(1)} %shard_map.42.rhs), channel_id=1, source_target_pairs={{0,1},{1,0},{2,3},{3,2},{4,5},{5,4},{6,7},{7,6},{8,9},{9,8},{10,11... | collective-permute-start | bytes 786440 | tf_op jit(solution)/shard_map/ppermute | solution.py:176
  31.6 0.0 collective-permute-done.5.level
  31.6 0.0 collective-permute-done.4.core
  31.6 1.9 %shard_map.39 = (bf16[2,256,256]{2,1,0:T(8,128)(2,1)S(1)}, bf16[2,256,256]{2,1,0:T(8,128)(2,1)S(1)}, bf16[2,256,256]{2,1,0:T(8,128)(2,1)S(1)}) custom-call(bf16[2,2,256,256]{3,2,1,0:T(8,128)(2,1)S(1)} %get-tuple-element.12.held, bf16[2,2,256,256]{3,2,1,0:T(8,128)(2,1)S(1)} %collective-permute-done.4.core, ...), custom_call_target="tpu_custom_call" | custom-call | flops 1 | bytes 1 | tf_op jit(solution)/shard_map/pallas_call | solution.py:160
  33.6 1.9 %collective-permute-start.6 = (bf16[2,256,256]{2,1,0:T(8,128)(2,1)S(1)}, bf16[2,256,256]{2,1,0:T(8,128)(2,1)S(1)}, u32[]{:S(2)}, u32[]{:S(2)}) collective-permute-start(bf16[2,256,256]{2,1,0:T(8,128)(2,1)S(1)} %get-tuple-element.13.pairing), channel_id=1, source_target_pairs={{0,4},{1,5},{2,6},{3,7},{4,0},{5,1},{6,2},{7,3},{8,12},{9,13},{10,... | collective-permute-start | bytes 786440 | tf_op jit(solution)/shard_map/ppermute | solution.py:176
  35.5 0.7 %collective-permute-start.7 = (bf16[2,256,256]{2,1,0:T(8,128)(2,1)S(1)}, bf16[2,256,256]{2,1,0:T(8,128)(2,1)S(1)}, u32[]{:S(2)}, u32[]{:S(2)}) collective-permute-start(bf16[2,256,256]{2,1,0:T(8,128)(2,1)S(1)} %get-tuple-element.14.joining), channel_id=1, source_target_pairs={{4,8},{5,9},{6,10},{7,11},{8,4},{9,5},{10,6},{11,7},{20,24},{21,25... | collective-permute-start | bytes 786440 | tf_op jit(solution)/shard_map/ppermute | solution.py:176
  36.1 0.0 collective-permute-done.10.level
  36.1 0.0 collective-permute-done.9.core
  36.2 0.9 %shard_map.43 = (bf16[2,256,128]{2,1,0:T(8,128)(2,1)S(1)}, bf16[2,256,128]{2,1,0:T(8,128)(2,1)S(1)}) custom-call(bf16[2,2,256,256]{3,2,1,0:T(8,128)(2,1)S(1)} %get-tuple-element.12.held, bf16[2,256,256]{2,1,0:T(8,128)(2,1)S(1)} %get-tuple-element.15.spread, bf16[2,256,256]{2,1,0:T(8,128)(2,1)S(1)} %shard_map.42.rhs, ...), custom_call_target="tpu_custom_call" | custom-call | flops 1 | bytes 1 | tf_op jit(solution)/shard_map/pallas_call | solution.py:160
  37.1 0.7 %collective-permute-start.12 = (bf16[2,256,128]{2,1,0:T(8,128)(2,1)S(1)}, bf16[2,256,128]{2,1,0:T(8,128)(2,1)S(1)}, u32[]{:S(2)}, u32[]{:S(2)}) collective-permute-start(bf16[2,256,128]{2,1,0:T(8,128)(2,1)S(1)} %get-tuple-element.17.rhs), channel_id=1, source_target_pairs={{4,8},{5,9},{6,10},{7,11},{8,4},{9,5},{10,6},{11,7},{20,24},{21,25... | collective-permute-start | bytes 393224 | tf_op jit(solution)/shard_map/ppermute | solution.py:176
  37.7 5.7 %collective-permute-start.11 = (bf16[2,256,128]{2,1,0:T(8,128)(2,1)S(1)}, bf16[2,256,128]{2,1,0:T(8,128)(2,1)S(1)}, u32[]{:S(2)}, u32[]{:S(2)}) collective-permute-start(bf16[2,256,128]{2,1,0:T(8,128)(2,1)S(1)} %get-tuple-element.17.rhs), channel_id=1, source_target_pairs={{0,4},{1,5},{2,6},{3,7},{4,0},{5,1},{6,2},{7,3},{8,12},{9,13},{10,... | collective-permute-start | bytes 393224 | tf_op jit(solution)/shard_map/ppermute | solution.py:176
  43.4 0.7 %collective-permute-start.15 = (bf16[2,256,128]{2,1,0:T(8,128)(2,1)S(1)}, bf16[2,256,128]{2,1,0:T(8,128)(2,1)S(1)}, u32[]{:S(2)}, u32[]{:S(2)}) collective-permute-start(bf16[2,256,128]{2,1,0:T(8,128)(2,1)S(1)} %get-tuple-element.18.rhs), channel_id=1, source_target_pairs={{4,8},{5,9},{6,10},{7,11},{8,4},{9,5},{10,6},{11,7},{20,24},{21,25... | collective-permute-start | bytes 393224 | tf_op jit(solution)/shard_map/ppermute | solution.py:176
  44.1 0.0 collective-permute-done.6.paired
  44.1 3.3 %collective-permute-start.14 = (bf16[2,256,128]{2,1,0:T(8,128)(2,1)S(1)}, bf16[2,256,128]{2,1,0:T(8,128)(2,1)S(1)}, u32[]{:S(2)}, u32[]{:S(2)}) collective-permute-start(bf16[2,256,128]{2,1,0:T(8,128)(2,1)S(1)} %get-tuple-element.18.rhs), channel_id=1, source_target_pairs={{0,4},{1,5},{2,6},{3,7},{4,0},{5,1},{6,2},{7,3},{8,12},{9,13},{10,... | collective-permute-start | bytes 393224 | tf_op jit(solution)/shard_map/ppermute | solution.py:176
  47.5 0.0 collective-permute-done.7.joined
  47.5 1.7 %shard_map.40.spread = bf16[2,256,256]{2,1,0:T(8,128)(2,1)S(1)} custom-call(bf16[2,256,256]{2,1,0:T(8,128)(2,1)S(1)} %get-tuple-element.13.pairing, bf16[2,256,256]{2,1,0:T(8,128)(2,1)S(1)} %get-tuple-element.14.joining, bf16[2,256,256]{2,1,0:T(8,128)(2,1)S(1)} %collective-permute-done.6.paired, bf16[2,256,256]{2,1,0:T(8,128)(2,1)S(1)} %collective-permute-done.7.joined), custom_call_target="tpu_custom_call" | custom-call | flops 1 | bytes 1 | tf_op jit(solution)/shard_map/pallas_call | solution.py:160
  49.1 0.0 collective-permute-done.12.joined
  49.1 0.0 collective-permute-done.11.paired
  49.1 0.7 %shard_map.44 = bf16[2,256,128]{2,1,0:T(8,128)(2,1)S(1)} custom-call(bf16[2,256,256]{2,1,0:T(8,128)(2,1)S(1)} %get-tuple-element.13.pairing, bf16[2,256,256]{2,1,0:T(8,128)(2,1)S(1)} %get-tuple-element.14.joining, bf16[2,256,256]{2,1,0:T(8,128)(2,1)S(1)} %shard_map.40.spread, bf16[2,256,128]{2,1,0:T(8,128)(2,1)S(1)} %get-tuple-element.17.rhs, ...), custom_call_target="tpu_custom_call" | custom-call | flops 1 | bytes 1 | tf_op jit(solution)/shard_map/pallas_call | solution.py:160
  49.8 0.0 collective-permute-start.13
  49.9 0.0 collective-permute-done.15.joined
  49.9 0.5 collective-permute-done.14.paired
  50.4 0.7 %shard_map.45 = bf16[2,256,128]{2,1,0:T(8,128)(2,1)S(1)} custom-call(bf16[2,256,256]{2,1,0:T(8,128)(2,1)S(1)} %get-tuple-element.13.pairing, bf16[2,256,256]{2,1,0:T(8,128)(2,1)S(1)} %get-tuple-element.14.joining, bf16[2,256,256]{2,1,0:T(8,128)(2,1)S(1)} %shard_map.40.spread, bf16[2,256,128]{2,1,0:T(8,128)(2,1)S(1)} %get-tuple-element.18.rhs, ...), custom_call_target="tpu_custom_call" | custom-call | flops 1 | bytes 1 | tf_op jit(solution)/shard_map/pallas_call | solution.py:160
  51.1 0.0 collective-permute-start.16
  51.1 3.8 %collective-permute-done.13 = bf16[2,256,128]{2,1,0:T(8,128)(2,1)S(1)} collective-permute-done((bf16[2,256,128]{2,1,0:T(8,128)(2,1)S(1)}, bf16[2,256,128]{2,1,0:T(8,128)(2,1)S(1)}, u32[]{:S(2)}, u32[]{:S(2)}) %collective-permute-start.13) | collective-permute-done | bytes 131104 | tf_op jit(solution)/shard_map/ppermute | solution.py:176
  54.9 1.4 %collective-permute-done.16 = bf16[2,256,128]{2,1,0:T(8,128)(2,1)S(1)} collective-permute-done((bf16[2,256,128]{2,1,0:T(8,128)(2,1)S(1)}, bf16[2,256,128]{2,1,0:T(8,128)(2,1)S(1)}, u32[]{:S(2)}, u32[]{:S(2)}) %collective-permute-start.16) | collective-permute-done | bytes 131104 | tf_op jit(solution)/shard_map/ppermute | solution.py:176
  56.3 0.7 %maximum_bitcast_fusion = bf16[1,2,256,256]{3,2,1,0:T(8,128)(2,1)} fusion(bf16[2,256,128]{2,1,0:T(8,128)(2,1)S(1)} %collective-permute-done.16, bf16[2,256,128]{2,1,0:T(8,128)(2,1)S(1)} %collective-permute-done.13), kind=kLoop, calls=%fused_computation | loop fusion | flops 524288 | bytes 524288 | tf_op jit(solution)/shard_map/broadcast_in_dim | solution.py:239
  (1 shorter events, 0.0 us)
Async XLA Ops:
  0.0 1.0 %copy-start.1 = (bf16[1,2,256,256]{3,2,1,0:T(8,128)(2,1)S(1)}, bf16[1,2,256,256]{3,2,1,0:T(8,128)(2,1)}, u32[]{:S(2)}) copy-start(bf16[1,2,256,256]{3,2,1,0:T(8,128)(2,1)} %param.4) | copy-start | bytes 786436
  1.0 3.1 %copy-start = (bf16[1,2,256,256]{3,2,1,0:T(8,128)(2,1)S(1)}, bf16[1,2,256,256]{3,2,1,0:T(8,128)(2,1)}, u32[]{:S(2)}) copy-start(bf16[1,2,256,256]{3,2,1,0:T(8,128)(2,1)} %param.5) | copy-start | bytes 786436
  1.1 15.0 %collective-permute-start = (bf16[2,2,256,256]{3,2,1,0:T(8,128)(2,1)S(1)}, bf16[2,2,256,256]{3,2,1,0:T(8,128)(2,1)S(1)}, u32[]{:S(2)}, u32[]{:S(2)}) collective-permute-start(bf16[2,2,256,256]{3,2,1,0:T(8,128)(2,1)S(1)} %constant_dynamic-update-slice_fusion.held), channel_id=1, source_target_pairs={{0,2},{1,3},{2,0},{3,1},{4,6},{5,7},{6,4},{7,5},{8,10},{9,11},{10,... | collective-permute-start | bytes 1572872 | tf_op jit(solution)/shard_map/ppermute | solution.py:176
  4.2 13.2 %collective-permute-start.1 = (bf16[3,2,256,256]{3,2,1,0:T(8,128)(2,1)S(1)}, bf16[3,2,256,256]{3,2,1,0:T(8,128)(2,1)S(1)}, u32[]{:S(2)}, u32[]{:S(2)}) collective-permute-start(bf16[3,2,256,256]{3,2,1,0:T(8,128)(2,1)S(1)} %shard_map.37.packed), channel_id=1, source_target_pairs={{1,0},{2,3},{5,4},{6,7},{9,8},{10,11},{13,12},{14,15},{17,16},{18,... | collective-permute-start | bytes 2359304 | tf_op jit(solution)/shard_map/ppermute | solution.py:176
  5.5 14.0 %collective-permute-start.3 = (bf16[3,2,256,256]{3,2,1,0:T(8,128)(2,1)S(1)}, bf16[3,2,256,256]{3,2,1,0:T(8,128)(2,1)S(1)}, u32[]{:S(2)}, u32[]{:S(2)}) collective-permute-start(bf16[3,2,256,256]{3,2,1,0:T(8,128)(2,1)S(1)} %shard_map.37.packed), channel_id=1, source_target_pairs={{3,6},{4,1},{7,10},{8,5},{11,14},{12,9},{19,22},{20,17},{23,26},{2... | collective-permute-start | bytes 2359304 | tf_op jit(solution)/shard_map/ppermute | solution.py:176
  16.0 3.4 %collective-permute-start.2 = (bf16[2,2,256,256]{3,2,1,0:T(8,128)(2,1)S(1)}, bf16[2,2,256,256]{3,2,1,0:T(8,128)(2,1)S(1)}, u32[]{:S(2)}, u32[]{:S(2)}) collective-permute-start(bf16[2,2,256,256]{3,2,1,0:T(8,128)(2,1)S(1)} %collective-permute-done.crossed), channel_id=1, source_target_pairs={{0,1},{3,2},{4,5},{7,6},{8,9},{11,10},{12,13},{15,14},{16,17},{19,... | collective-permute-start | bytes 1572872 | tf_op jit(solution)/shard_map/ppermute | solution.py:176
  17.7 9.1 %collective-permute-start.8 = (bf16[2,256,256]{2,1,0:T(8,128)(2,1)S(1)}, bf16[2,256,256]{2,1,0:T(8,128)(2,1)S(1)}, u32[]{:S(2)}, u32[]{:S(2)}) collective-permute-start(bf16[2,256,256]{2,1,0:T(8,128)(2,1)S(1)} %shard_map.41), channel_id=1, source_target_pairs={{0,2},{1,3},{2,0},{3,1},{4,6},{5,7},{6,4},{7,5},{8,10},{9,11},{10,... | collective-permute-start | bytes 786440 | tf_op jit(solution)/shard_map/ppermute | solution.py:176
  21.4 10.3 %collective-permute-start.5 = (bf16[2,2,256,256]{3,2,1,0:T(8,128)(2,1)S(1)}, bf16[2,2,256,256]{3,2,1,0:T(8,128)(2,1)S(1)}, u32[]{:S(2)}, u32[]{:S(2)}) collective-permute-start(bf16[2,2,256,256]{3,2,1,0:T(8,128)(2,1)S(1)} %get-tuple-element.12.held), channel_id=1, source_target_pairs={{1,4},{3,6},{4,1},{5,8},{6,3},{7,10},{8,5},{9,12},{10,7},{11,14},{... | collective-permute-start | bytes 1572872 | tf_op jit(solution)/shard_map/ppermute | solution.py:176
  22.1 9.6 %collective-permute-start.4 = (bf16[2,2,256,256]{3,2,1,0:T(8,128)(2,1)S(1)}, bf16[2,2,256,256]{3,2,1,0:T(8,128)(2,1)S(1)}, u32[]{:S(2)}, u32[]{:S(2)}) collective-permute-start(bf16[2,2,256,256]{3,2,1,0:T(8,128)(2,1)S(1)} %get-tuple-element.12.held), channel_id=1, source_target_pairs={{0,1},{1,0},{2,3},{3,2},{4,5},{5,4},{6,7},{7,6},{8,9},{9,8},{10,11... | collective-permute-start | bytes 1572872 | tf_op jit(solution)/shard_map/ppermute | solution.py:176
  27.6 8.5 %collective-permute-start.10 = (bf16[2,256,256]{2,1,0:T(8,128)(2,1)S(1)}, bf16[2,256,256]{2,1,0:T(8,128)(2,1)S(1)}, u32[]{:S(2)}, u32[]{:S(2)}) collective-permute-start(bf16[2,256,256]{2,1,0:T(8,128)(2,1)S(1)} %shard_map.42.rhs), channel_id=1, source_target_pairs={{1,4},{3,6},{4,1},{5,8},{6,3},{7,10},{8,5},{9,12},{10,7},{11,14},{... | collective-permute-start | bytes 786440 | tf_op jit(solution)/shard_map/ppermute | solution.py:176
  28.3 7.8 %collective-permute-start.9 = (bf16[2,256,256]{2,1,0:T(8,128)(2,1)S(1)}, bf16[2,256,256]{2,1,0:T(8,128)(2,1)S(1)}, u32[]{:S(2)}, u32[]{:S(2)}) collective-permute-start(bf16[2,256,256]{2,1,0:T(8,128)(2,1)S(1)} %shard_map.42.rhs), channel_id=1, source_target_pairs={{0,1},{1,0},{2,3},{3,2},{4,5},{5,4},{6,7},{7,6},{8,9},{9,8},{10,11... | collective-permute-start | bytes 786440 | tf_op jit(solution)/shard_map/ppermute | solution.py:176
  33.6 10.5 %collective-permute-start.6 = (bf16[2,256,256]{2,1,0:T(8,128)(2,1)S(1)}, bf16[2,256,256]{2,1,0:T(8,128)(2,1)S(1)}, u32[]{:S(2)}, u32[]{:S(2)}) collective-permute-start(bf16[2,256,256]{2,1,0:T(8,128)(2,1)S(1)} %get-tuple-element.13.pairing), channel_id=1, source_target_pairs={{0,4},{1,5},{2,6},{3,7},{4,0},{5,1},{6,2},{7,3},{8,12},{9,13},{10,... | collective-permute-start | bytes 786440 | tf_op jit(solution)/shard_map/ppermute | solution.py:176
  35.5 12.0 %collective-permute-start.7 = (bf16[2,256,256]{2,1,0:T(8,128)(2,1)S(1)}, bf16[2,256,256]{2,1,0:T(8,128)(2,1)S(1)}, u32[]{:S(2)}, u32[]{:S(2)}) collective-permute-start(bf16[2,256,256]{2,1,0:T(8,128)(2,1)S(1)} %get-tuple-element.14.joining), channel_id=1, source_target_pairs={{4,8},{5,9},{6,10},{7,11},{8,4},{9,5},{10,6},{11,7},{20,24},{21,25... | collective-permute-start | bytes 786440 | tf_op jit(solution)/shard_map/ppermute | solution.py:176
  37.1 12.1 %collective-permute-start.12 = (bf16[2,256,128]{2,1,0:T(8,128)(2,1)S(1)}, bf16[2,256,128]{2,1,0:T(8,128)(2,1)S(1)}, u32[]{:S(2)}, u32[]{:S(2)}) collective-permute-start(bf16[2,256,128]{2,1,0:T(8,128)(2,1)S(1)} %get-tuple-element.17.rhs), channel_id=1, source_target_pairs={{4,8},{5,9},{6,10},{7,11},{8,4},{9,5},{10,6},{11,7},{20,24},{21,25... | collective-permute-start | bytes 393224 | tf_op jit(solution)/shard_map/ppermute | solution.py:176
  37.7 11.4 %collective-permute-start.11 = (bf16[2,256,128]{2,1,0:T(8,128)(2,1)S(1)}, bf16[2,256,128]{2,1,0:T(8,128)(2,1)S(1)}, u32[]{:S(2)}, u32[]{:S(2)}) collective-permute-start(bf16[2,256,128]{2,1,0:T(8,128)(2,1)S(1)} %get-tuple-element.17.rhs), channel_id=1, source_target_pairs={{0,4},{1,5},{2,6},{3,7},{4,0},{5,1},{6,2},{7,3},{8,12},{9,13},{10,... | collective-permute-start | bytes 393224 | tf_op jit(solution)/shard_map/ppermute | solution.py:176
  43.4 6.4 %collective-permute-start.15 = (bf16[2,256,128]{2,1,0:T(8,128)(2,1)S(1)}, bf16[2,256,128]{2,1,0:T(8,128)(2,1)S(1)}, u32[]{:S(2)}, u32[]{:S(2)}) collective-permute-start(bf16[2,256,128]{2,1,0:T(8,128)(2,1)S(1)} %get-tuple-element.18.rhs), channel_id=1, source_target_pairs={{4,8},{5,9},{6,10},{7,11},{8,4},{9,5},{10,6},{11,7},{20,24},{21,25... | collective-permute-start | bytes 393224 | tf_op jit(solution)/shard_map/ppermute | solution.py:176
  44.1 6.3 %collective-permute-start.14 = (bf16[2,256,128]{2,1,0:T(8,128)(2,1)S(1)}, bf16[2,256,128]{2,1,0:T(8,128)(2,1)S(1)}, u32[]{:S(2)}, u32[]{:S(2)}) collective-permute-start(bf16[2,256,128]{2,1,0:T(8,128)(2,1)S(1)} %get-tuple-element.18.rhs), channel_id=1, source_target_pairs={{0,4},{1,5},{2,6},{3,7},{4,0},{5,1},{6,2},{7,3},{8,12},{9,13},{10,... | collective-permute-start | bytes 393224 | tf_op jit(solution)/shard_map/ppermute | solution.py:176
  49.8 5.1 %collective-permute-start.13 = (bf16[2,256,128]{2,1,0:T(8,128)(2,1)S(1)}, bf16[2,256,128]{2,1,0:T(8,128)(2,1)S(1)}, u32[]{:S(2)}, u32[]{:S(2)}) collective-permute-start(bf16[2,256,128]{2,1,0:T(8,128)(2,1)S(1)} %shard_map.44), channel_id=1, source_target_pairs={{0,1},{1,3},{2,0},{3,2},{4,5},{5,7},{6,4},{7,6},{8,9},{9,11},{10,8... | collective-permute-start | bytes 393224 | tf_op jit(solution)/shard_map/ppermute | solution.py:176
  51.1 5.2 %collective-permute-start.16 = (bf16[2,256,128]{2,1,0:T(8,128)(2,1)S(1)}, bf16[2,256,128]{2,1,0:T(8,128)(2,1)S(1)}, u32[]{:S(2)}, u32[]{:S(2)}) collective-permute-start(bf16[2,256,128]{2,1,0:T(8,128)(2,1)S(1)} %shard_map.45), channel_id=1, source_target_pairs={{0,1},{1,3},{2,0},{3,2},{4,5},{5,7},{6,4},{7,6},{8,9},{9,11},{10,8... | collective-permute-start | bytes 393224 | tf_op jit(solution)/shard_map/ppermute | solution.py:176

commit v8 on v7

--- a/solution.py
+++ b/solution.py
@@ -150,7 +150,7 @@
     spread[...] = parts(inverse_less_one(coupling))
 
 
-def last_injections_kernel(pairing, joining, spread, rhs, paired, joined, new):
+def last_injections_kernel(pairing, joining, spread, rhs, joined, paired, new):
     raw = tall(rhs[...]).astype(jnp.float32) - product(wide(pairing), tall(paired[...]))
     raw = raw - product(wide(joining), tall(joined[...]))
     new[...] = parts(solved(spread[...], raw))
@@ -232,7 +232,7 @@
     for half, (paired_half, joined_half), weight in zip(halves, arrived, (1, 1)):
         (result,) = run(
             last_injections_kernel, (half_block,),
-            pairing, joining, spread, half, paired_half, joined_half,
+            pairing, joining, spread, half, joined_half, paired_half,
             weight=weight,
         )
         results.append(move(result, *home))

time: 57.4 us -> 56.1 us (0.977)
  the two profiles are of different devices: /device:TPU:0 before, /device:TPU:18 now
where the time goes in v8:
time: 56.1 us; the launch traced here: 55.8 us
  starting transfers between devices  26.3 us (47%)
  waiting for transfers between devices  18.5 us (33%)
  Pallas kernels  9.04 us (16%)
  local copies, waits for them, and re-layouts  1.05 us (2%)
  other arithmetic  0.73 us (1%)
    ppermute x17, starting transfers between devices, trade(): lax.ppermute(value, 'chain', [(a, b) for a, b in pairs if 0 <= a < length...  26.3 us
    ppermute x17, waiting for transfers between devices, trade(): lax.ppermute(value, 'chain', [(a, b) for a, b in pairs if 0 <= a < length...  18.5 us
    pallas_call x9, Pallas kernels, run(): pl.pallas_call(kernel, out_shape=[jax.ShapeDtypeStruct(s, jnp.bfloat16) f...  9.04 us
  transfers between devices with their start and end apart: 17, of which 8 were waited for; matrix products, arithmetic and copies ran while one was open for 0% of the time, Pallas kernels for 16%

profile of v8, /device:TPU:18, one launch (start us, length us, event | category | flops | bytes accessed | tf_op | source)
XLA Modules:
  0.0 55.8 jit_solution(7352673757129001806)
XLA Ops:
  0.0 0.0 copy-start.1
  0.0 1.0 %constant_dynamic-update-slice_fusion.1 = bf16[2,2,256,256]{3,2,1,0:T(8,128)(2,1)S(1)} fusion(bf16[1,2,256,256]{3,2,1,0:T(8,128)(2,1)} %param.3), kind=kLoop, calls=%fused_computation.2 | loop fusion | bytes 524288
  1.0 0.0 copy-done.1
  1.0 0.0 copy-start
  1.1 1.6 %collective-permute-start = (bf16[2,2,256,256]{3,2,1,0:T(8,128)(2,1)S(1)}, bf16[2,2,256,256]{3,2,1,0:T(8,128)(2,1)S(1)}, u32[]{:S(2)}, u32[]{:S(2)}) collective-permute-start(bf16[2,2,256,256]{3,2,1,0:T(8,128)(2,1)S(1)} %constant_dynamic-update-slice_fusion.held), channel_id=1, source_target_pairs={{0,2},{1,3},{2,0},{3,1},{4,6},{5,7},{6,4},{7,5},{8,10},{9,11},{10,... | collective-permute-start | bytes 1572872 | tf_op jit(solution)/shard_map/ppermute | solution.py:176
  2.7 0.0 copy-done
  2.7 0.1 shard_map.37.packed
  2.7 1.3 %collective-permute-start.1 = (bf16[3,2,256,256]{3,2,1,0:T(8,128)(2,1)S(1)}, bf16[3,2,256,256]{3,2,1,0:T(8,128)(2,1)S(1)}, u32[]{:S(2)}, u32[]{:S(2)}) collective-permute-start(bf16[3,2,256,256]{3,2,1,0:T(8,128)(2,1)S(1)} %shard_map.37.packed), channel_id=1, source_target_pairs={{1,0},{2,3},{5,4},{6,7},{9,8},{10,11},{13,12},{14,15},{17,16},{18,... | collective-permute-start | bytes 2359304 | tf_op jit(solution)/shard_map/ppermute | solution.py:176
  4.0 3.2 %collective-permute-start.3 = (bf16[3,2,256,256]{3,2,1,0:T(8,128)(2,1)S(1)}, bf16[3,2,256,256]{3,2,1,0:T(8,128)(2,1)S(1)}, u32[]{:S(2)}, u32[]{:S(2)}) collective-permute-start(bf16[3,2,256,256]{3,2,1,0:T(8,128)(2,1)S(1)} %shard_map.37.packed), channel_id=1, source_target_pairs={{3,6},{4,1},{7,10},{8,5},{11,14},{12,9},{19,22},{20,17},{23,26},{2... | collective-permute-start | bytes 2359304 | tf_op jit(solution)/shard_map/ppermute | solution.py:176
  7.2 7.6 %collective-permute-done.crossed = bf16[2,2,256,256]{3,2,1,0:T(8,128)(2,1)S(1)} collective-permute-done((bf16[2,2,256,256]{3,2,1,0:T(8,128)(2,1)S(1)}, bf16[2,2,256,256]{3,2,1,0:T(8,128)(2,1)S(1)}, u32[]{:S(2)}, u32[]{:S(2)}) %collective-permute-start) | collective-permute-done | bytes 524320 | tf_op jit(solution)/shard_map/ppermute | solution.py:176
  14.8 1.3 %collective-permute-start.2 = (bf16[2,2,256,256]{3,2,1,0:T(8,128)(2,1)S(1)}, bf16[2,2,256,256]{3,2,1,0:T(8,128)(2,1)S(1)}, u32[]{:S(2)}, u32[]{:S(2)}) collective-permute-start(bf16[2,2,256,256]{3,2,1,0:T(8,128)(2,1)S(1)} %collective-permute-done.crossed), channel_id=1, source_target_pairs={{0,1},{3,2},{4,5},{7,6},{8,9},{11,10},{12,13},{15,14},{16,17},{19,... | collective-permute-start | bytes 1572872 | tf_op jit(solution)/shard_map/ppermute | solution.py:176
  16.1 0.0 collective-permute-done.1.core
  16.1 0.3 shard_map.41
  16.4 1.6 %collective-permute-start.8 = (bf16[2,256,256]{2,1,0:T(8,128)(2,1)S(1)}, bf16[2,256,256]{2,1,0:T(8,128)(2,1)S(1)}, u32[]{:S(2)}, u32[]{:S(2)}) collective-permute-start(bf16[2,256,256]{2,1,0:T(8,128)(2,1)S(1)} %shard_map.41), channel_id=1, source_target_pairs={{0,2},{1,3},{2,0},{3,1},{4,6},{5,7},{6,4},{7,5},{8,10},{9,11},{10,... | collective-permute-start | bytes 786440 | tf_op jit(solution)/shard_map/ppermute | solution.py:176
  18.0 0.0 collective-permute-done.3.level
  18.0 0.0 collective-permute-done.2.onward
  18.0 1.9 %shard_map.38 = (bf16[2,2,256,256]{3,2,1,0:T(8,128)(2,1)S(1)}, bf16[2,256,256]{2,1,0:T(8,128)(2,1)S(1)}) custom-call(bf16[2,2,256,256]{3,2,1,0:T(8,128)(2,1)S(1)} %constant_dynamic-update-slice_fusion.held, bf16[2,2,256,256]{3,2,1,0:T(8,128)(2,1)S(1)} %collective-permute-done.crossed, bf16[3,2,256,256]{3,2,1,0:T(8,128)(2,1)S(1)} %collective-permute-done.1.core, ...), custom_call_target="tpu_custom_call" | custom-call | flops 1 | bytes 1 | tf_op jit(solution)/shard_map/pallas_call | solution.py:160
  19.9 2.8 %collective-permute-start.5 = (bf16[2,2,256,256]{3,2,1,0:T(8,128)(2,1)S(1)}, bf16[2,2,256,256]{3,2,1,0:T(8,128)(2,1)S(1)}, u32[]{:S(2)}, u32[]{:S(2)}) collective-permute-start(bf16[2,2,256,256]{3,2,1,0:T(8,128)(2,1)S(1)} %get-tuple-element.12.held), channel_id=1, source_target_pairs={{1,4},{3,6},{4,1},{5,8},{6,3},{7,10},{8,5},{9,12},{10,7},{11,14},{... | collective-permute-start | bytes 1572872 | tf_op jit(solution)/shard_map/ppermute | solution.py:176
  22.8 0.8 %collective-permute-start.4 = (bf16[2,2,256,256]{3,2,1,0:T(8,128)(2,1)S(1)}, bf16[2,2,256,256]{3,2,1,0:T(8,128)(2,1)S(1)}, u32[]{:S(2)}, u32[]{:S(2)}) collective-permute-start(bf16[2,2,256,256]{3,2,1,0:T(8,128)(2,1)S(1)} %get-tuple-element.12.held), channel_id=1, source_target_pairs={{0,1},{1,0},{2,3},{3,2},{4,5},{5,4},{6,7},{7,6},{8,9},{9,8},{10,11... | collective-permute-start | bytes 1572872 | tf_op jit(solution)/shard_map/ppermute | solution.py:176
  23.6 2.0 %collective-permute-done.8.crossed_rhs = bf16[2,256,256]{2,1,0:T(8,128)(2,1)S(1)} collective-permute-done((bf16[2,256,256]{2,1,0:T(8,128)(2,1)S(1)}, bf16[2,256,256]{2,1,0:T(8,128)(2,1)S(1)}, u32[]{:S(2)}, u32[]{:S(2)}) %collective-permute-start.8) | collective-permute-done | bytes 262176 | tf_op jit(solution)/shard_map/ppermute | solution.py:176
  25.6 0.9 %shard_map.42.rhs = bf16[2,256,256]{2,1,0:T(8,128)(2,1)S(1)} custom-call(bf16[2,2,256,256]{3,2,1,0:T(8,128)(2,1)S(1)} %collective-permute-done.crossed, bf16[2,256,256]{2,1,0:T(8,128)(2,1)S(1)} %get-tuple-element.16.spread, bf16[2,256,256]{2,1,0:T(8,128)(2,1)S(1)} %bitcast.4, bf16[2,256,256]{2,1,0:T(8,128)(2,1)S(1)} %collective-permute-done.8.crossed_rhs, ...), custom_call_target="tpu_custom_call" | custom-call | flops 99999997952 | bytes 1 | tf_op jit(solution)/shard_map/pallas_call | solution.py:160
  26.5 2.0 %collective-permute-start.10 = (bf16[2,256,256]{2,1,0:T(8,128)(2,1)S(1)}, bf16[2,256,256]{2,1,0:T(8,128)(2,1)S(1)}, u32[]{:S(2)}, u32[]{:S(2)}) collective-permute-start(bf16[2,256,256]{2,1,0:T(8,128)(2,1)S(1)} %shard_map.42.rhs), channel_id=1, source_target_pairs={{1,4},{3,6},{4,1},{5,8},{6,3},{7,10},{8,5},{9,12},{10,7},{11,14},{... | collective-permute-start | bytes 786440 | tf_op jit(solution)/shard_map/ppermute | solution.py:176
  28.5 1.7 %collective-permute-start.9 = (bf16[2,256,256]{2,1,0:T(8,128)(2,1)S(1)}, bf16[2,256,256]{2,1,0:T(8,128)(2,1)S(1)}, u32[]{:S(2)}, u32[]{:S(2)}) collective-permute-start(bf16[2,256,256]{2,1,0:T(8,128)(2,1)S(1)} %shard_map.42.rhs), channel_id=1, source_target_pairs={{0,1},{1,0},{2,3},{3,2},{4,5},{5,4},{6,7},{7,6},{8,9},{9,8},{10,11... | collective-permute-start | bytes 786440 | tf_op jit(solution)/shard_map/ppermute | solution.py:176
  30.2 0.2 collective-permute-done.5.level
  30.4 0.0 collective-permute-done.4.core
  30.4 1.9 %shard_map.39 = (bf16[2,256,256]{2,1,0:T(8,128)(2,1)S(1)}, bf16[2,256,256]{2,1,0:T(8,128)(2,1)S(1)}, bf16[2,256,256]{2,1,0:T(8,128)(2,1)S(1)}) custom-call(bf16[2,2,256,256]{3,2,1,0:T(8,128)(2,1)S(1)} %get-tuple-element.12.held, bf16[2,2,256,256]{3,2,1,0:T(8,128)(2,1)S(1)} %collective-permute-done.4.core, ...), custom_call_target="tpu_custom_call" | custom-call | flops 1 | bytes 1 | tf_op jit(solution)/shard_map/pallas_call | solution.py:160
  32.4 1.6 %collective-permute-start.6 = (bf16[2,256,256]{2,1,0:T(8,128)(2,1)S(1)}, bf16[2,256,256]{2,1,0:T(8,128)(2,1)S(1)}, u32[]{:S(2)}, u32[]{:S(2)}) collective-permute-start(bf16[2,256,256]{2,1,0:T(8,128)(2,1)S(1)} %get-tuple-element.13.pairing), channel_id=1, source_target_pairs={{0,4},{1,5},{2,6},{3,7},{4,0},{5,1},{6,2},{7,3},{8,12},{9,13},{10,... | collective-permute-start | bytes 786440 | tf_op jit(solution)/shard_map/ppermute | solution.py:176
  34.0 1.9 %collective-permute-start.7 = (bf16[2,256,256]{2,1,0:T(8,128)(2,1)S(1)}, bf16[2,256,256]{2,1,0:T(8,128)(2,1)S(1)}, u32[]{:S(2)}, u32[]{:S(2)}) collective-permute-start(bf16[2,256,256]{2,1,0:T(8,128)(2,1)S(1)} %get-tuple-element.14.joining), channel_id=1, source_target_pairs={{4,8},{5,9},{6,10},{7,11},{8,4},{9,5},{10,6},{11,7},{20,24},{21,25... | collective-permute-start | bytes 786440 | tf_op jit(solution)/shard_map/ppermute | solution.py:176
  35.9 0.0 collective-permute-done.10.level
  35.9 0.0 collective-permute-done.9.core
  36.0 0.9 %shard_map.43 = (bf16[2,256,128]{2,1,0:T(8,128)(2,1)S(1)}, bf16[2,256,128]{2,1,0:T(8,128)(2,1)S(1)}) custom-call(bf16[2,2,256,256]{3,2,1,0:T(8,128)(2,1)S(1)} %get-tuple-element.12.held, bf16[2,256,256]{2,1,0:T(8,128)(2,1)S(1)} %get-tuple-element.15.spread, bf16[2,256,256]{2,1,0:T(8,128)(2,1)S(1)} %shard_map.42.rhs, ...), custom_call_target="tpu_custom_call" | custom-call | flops 1 | bytes 1 | tf_op jit(solution)/shard_map/pallas_call | solution.py:160
  36.9 0.1 collective-permute-start.12
  36.9 3.9 %collective-permute-start.11 = (bf16[2,256,128]{2,1,0:T(8,128)(2,1)S(1)}, bf16[2,256,128]{2,1,0:T(8,128)(2,1)S(1)}, u32[]{:S(2)}, u32[]{:S(2)}) collective-permute-start(bf16[2,256,128]{2,1,0:T(8,128)(2,1)S(1)} %get-tuple-element.17.rhs), channel_id=1, source_target_pairs={{4,8},{5,9},{6,10},{7,11},{8,4},{9,5},{10,6},{11,7},{20,24},{21,25... | collective-permute-start | bytes 393224 | tf_op jit(solution)/shard_map/ppermute | solution.py:176
  40.9 0.1 collective-permute-start.15
  40.9 0.5 collective-permute-done.6.paired
  41.4 2.3 %collective-permute-start.14 = (bf16[2,256,128]{2,1,0:T(8,128)(2,1)S(1)}, bf16[2,256,128]{2,1,0:T(8,128)(2,1)S(1)}, u32[]{:S(2)}, u32[]{:S(2)}) collective-permute-start(bf16[2,256,128]{2,1,0:T(8,128)(2,1)S(1)} %get-tuple-element.18.rhs), channel_id=1, source_target_pairs={{4,8},{5,9},{6,10},{7,11},{8,4},{9,5},{10,6},{11,7},{20,24},{21,25... | collective-permute-start | bytes 393224 | tf_op jit(solution)/shard_map/ppermute | solution.py:176
  43.8 1.4 %collective-permute-done.7.joined = bf16[2,256,256]{2,1,0:T(8,128)(2,1)S(1)} collective-permute-done((bf16[2,256,256]{2,1,0:T(8,128)(2,1)S(1)}, bf16[2,256,256]{2,1,0:T(8,128)(2,1)S(1)}, u32[]{:S(2)}, u32[]{:S(2)}) %collective-permute-start.7) | collective-permute-done | bytes 262176 | tf_op jit(solution)/shard_map/ppermute | solution.py:176
  45.1 1.7 %shard_map.40.spread = bf16[2,256,256]{2,1,0:T(8,128)(2,1)S(1)} custom-call(bf16[2,256,256]{2,1,0:T(8,128)(2,1)S(1)} %get-tuple-element.13.pairing, bf16[2,256,256]{2,1,0:T(8,128)(2,1)S(1)} %get-tuple-element.14.joining, bf16[2,256,256]{2,1,0:T(8,128)(2,1)S(1)} %collective-permute-done.6.paired, bf16[2,256,256]{2,1,0:T(8,128)(2,1)S(1)} %collective-permute-done.7.joined), custom_call_target="tpu_custom_call" | custom-call | flops 1 | bytes 1 | tf_op jit(solution)/shard_map/pallas_call | solution.py:160
  46.8 0.0 collective-permute-done.12.paired
  46.8 0.0 collective-permute-done.11.joined
  46.8 0.7 %shard_map.44 = bf16[2,256,128]{2,1,0:T(8,128)(2,1)S(1)} custom-call(bf16[2,256,256]{2,1,0:T(8,128)(2,1)S(1)} %get-tuple-element.13.pairing, bf16[2,256,256]{2,1,0:T(8,128)(2,1)S(1)} %get-tuple-element.14.joining, bf16[2,256,256]{2,1,0:T(8,128)(2,1)S(1)} %shard_map.40.spread, bf16[2,256,128]{2,1,0:T(8,128)(2,1)S(1)} %get-tuple-element.17.rhs, ...), custom_call_target="tpu_custom_call" | custom-call | flops 1 | bytes 1 | tf_op jit(solution)/shard_map/pallas_call | solution.py:160
  47.5 0.0 collective-permute-start.13
  47.5 0.0 collective-permute-done.15.paired
  47.5 1.8 %collective-permute-done.14.joined = bf16[2,256,128]{2,1,0:T(8,128)(2,1)S(1)} collective-permute-done((bf16[2,256,128]{2,1,0:T(8,128)(2,1)S(1)}, bf16[2,256,128]{2,1,0:T(8,128)(2,1)S(1)}, u32[]{:S(2)}, u32[]{:S(2)}) %collective-permute-start.14) | collective-permute-done | bytes 131104 | tf_op jit(solution)/shard_map/ppermute | solution.py:176
  49.3 0.7 %shard_map.45 = bf16[2,256,128]{2,1,0:T(8,128)(2,1)S(1)} custom-call(bf16[2,256,256]{2,1,0:T(8,128)(2,1)S(1)} %get-tuple-element.13.pairing, bf16[2,256,256]{2,1,0:T(8,128)(2,1)S(1)} %get-tuple-element.14.joining, bf16[2,256,256]{2,1,0:T(8,128)(2,1)S(1)} %shard_map.40.spread, bf16[2,256,128]{2,1,0:T(8,128)(2,1)S(1)} %get-tuple-element.18.rhs, ...), custom_call_target="tpu_custom_call" | custom-call | flops 1 | bytes 1 | tf_op jit(solution)/shard_map/pallas_call | solution.py:160
  50.0 0.0 collective-permute-start.16
  50.1 2.4 %collective-permute-done.13 = bf16[2,256,128]{2,1,0:T(8,128)(2,1)S(1)} collective-permute-done((bf16[2,256,128]{2,1,0:T(8,128)(2,1)S(1)}, bf16[2,256,128]{2,1,0:T(8,128)(2,1)S(1)}, u32[]{:S(2)}, u32[]{:S(2)}) %collective-permute-start.13) | collective-permute-done | bytes 131104 | tf_op jit(solution)/shard_map/ppermute | solution.py:176
  52.5 2.5 %collective-permute-done.16 = bf16[2,256,128]{2,1,0:T(8,128)(2,1)S(1)} collective-permute-done((bf16[2,256,128]{2,1,0:T(8,128)(2,1)S(1)}, bf16[2,256,128]{2,1,0:T(8,128)(2,1)S(1)}, u32[]{:S(2)}, u32[]{:S(2)}) %collective-permute-start.16) | collective-permute-done | bytes 131104 | tf_op jit(solution)/shard_map/ppermute | solution.py:176
  55.0 0.7 %maximum_bitcast_fusion = bf16[1,2,256,256]{3,2,1,0:T(8,128)(2,1)} fusion(bf16[2,256,128]{2,1,0:T(8,128)(2,1)S(1)} %collective-permute-done.16, bf16[2,256,128]{2,1,0:T(8,128)(2,1)S(1)} %collective-permute-done.13), kind=kLoop, calls=%fused_computation | loop fusion | flops 524288 | bytes 524288 | tf_op jit(solution)/shard_map/broadcast_in_dim | solution.py:239
  (1 shorter events, 0.0 us)
Async XLA Ops:
  0.0 1.0 %copy-start.1 = (bf16[1,2,256,256]{3,2,1,0:T(8,128)(2,1)S(1)}, bf16[1,2,256,256]{3,2,1,0:T(8,128)(2,1)}, u32[]{:S(2)}) copy-start(bf16[1,2,256,256]{3,2,1,0:T(8,128)(2,1)} %param.4) | copy-start | bytes 786436
  1.0 1.6 %copy-start = (bf16[1,2,256,256]{3,2,1,0:T(8,128)(2,1)S(1)}, bf16[1,2,256,256]{3,2,1,0:T(8,128)(2,1)}, u32[]{:S(2)}) copy-start(bf16[1,2,256,256]{3,2,1,0:T(8,128)(2,1)} %param.5) | copy-start | bytes 786436
  1.1 13.7 %collective-permute-start = (bf16[2,2,256,256]{3,2,1,0:T(8,128)(2,1)S(1)}, bf16[2,2,256,256]{3,2,1,0:T(8,128)(2,1)S(1)}, u32[]{:S(2)}, u32[]{:S(2)}) collective-permute-start(bf16[2,2,256,256]{3,2,1,0:T(8,128)(2,1)S(1)} %constant_dynamic-update-slice_fusion.held), channel_id=1, source_target_pairs={{0,2},{1,3},{2,0},{3,1},{4,6},{5,7},{6,4},{7,5},{8,10},{9,11},{10,... | collective-permute-start | bytes 1572872 | tf_op jit(solution)/shard_map/ppermute | solution.py:176
  2.7 13.4 %collective-permute-start.1 = (bf16[3,2,256,256]{3,2,1,0:T(8,128)(2,1)S(1)}, bf16[3,2,256,256]{3,2,1,0:T(8,128)(2,1)S(1)}, u32[]{:S(2)}, u32[]{:S(2)}) collective-permute-start(bf16[3,2,256,256]{3,2,1,0:T(8,128)(2,1)S(1)} %shard_map.37.packed), channel_id=1, source_target_pairs={{1,0},{2,3},{5,4},{6,7},{9,8},{10,11},{13,12},{14,15},{17,16},{18,... | collective-permute-start | bytes 2359304 | tf_op jit(solution)/shard_map/ppermute | solution.py:176
  4.0 14.0 %collective-permute-start.3 = (bf16[3,2,256,256]{3,2,1,0:T(8,128)(2,1)S(1)}, bf16[3,2,256,256]{3,2,1,0:T(8,128)(2,1)S(1)}, u32[]{:S(2)}, u32[]{:S(2)}) collective-permute-start(bf16[3,2,256,256]{3,2,1,0:T(8,128)(2,1)S(1)} %shard_map.37.packed), channel_id=1, source_target_pairs={{3,6},{4,1},{7,10},{8,5},{11,14},{12,9},{19,22},{20,17},{23,26},{2... | collective-permute-start | bytes 2359304 | tf_op jit(solution)/shard_map/ppermute | solution.py:176
  14.8 3.2 %collective-permute-start.2 = (bf16[2,2,256,256]{3,2,1,0:T(8,128)(2,1)S(1)}, bf16[2,2,256,256]{3,2,1,0:T(8,128)(2,1)S(1)}, u32[]{:S(2)}, u32[]{:S(2)}) collective-permute-start(bf16[2,2,256,256]{3,2,1,0:T(8,128)(2,1)S(1)} %collective-permute-done.crossed), channel_id=1, source_target_pairs={{0,1},{3,2},{4,5},{7,6},{8,9},{11,10},{12,13},{15,14},{16,17},{19,... | collective-permute-start | bytes 1572872 | tf_op jit(solution)/shard_map/ppermute | solution.py:176
  16.4 9.2 %collective-permute-start.8 = (bf16[2,256,256]{2,1,0:T(8,128)(2,1)S(1)}, bf16[2,256,256]{2,1,0:T(8,128)(2,1)S(1)}, u32[]{:S(2)}, u32[]{:S(2)}) collective-permute-start(bf16[2,256,256]{2,1,0:T(8,128)(2,1)S(1)} %shard_map.41), channel_id=1, source_target_pairs={{0,2},{1,3},{2,0},{3,1},{4,6},{5,7},{6,4},{7,5},{8,10},{9,11},{10,... | collective-permute-start | bytes 786440 | tf_op jit(solution)/shard_map/ppermute | solution.py:176
  19.9 10.5 %collective-permute-start.5 = (bf16[2,2,256,256]{3,2,1,0:T(8,128)(2,1)S(1)}, bf16[2,2,256,256]{3,2,1,0:T(8,128)(2,1)S(1)}, u32[]{:S(2)}, u32[]{:S(2)}) collective-permute-start(bf16[2,2,256,256]{3,2,1,0:T(8,128)(2,1)S(1)} %get-tuple-element.12.held), channel_id=1, source_target_pairs={{1,4},{3,6},{4,1},{5,8},{6,3},{7,10},{8,5},{9,12},{10,7},{11,14},{... | collective-permute-start | bytes 1572872 | tf_op jit(solution)/shard_map/ppermute | solution.py:176
  22.8 7.7 %collective-permute-start.4 = (bf16[2,2,256,256]{3,2,1,0:T(8,128)(2,1)S(1)}, bf16[2,2,256,256]{3,2,1,0:T(8,128)(2,1)S(1)}, u32[]{:S(2)}, u32[]{:S(2)}) collective-permute-start(bf16[2,2,256,256]{3,2,1,0:T(8,128)(2,1)S(1)} %get-tuple-element.12.held), channel_id=1, source_target_pairs={{0,1},{1,0},{2,3},{3,2},{4,5},{5,4},{6,7},{7,6},{8,9},{9,8},{10,11... | collective-permute-start | bytes 1572872 | tf_op jit(solution)/shard_map/ppermute | solution.py:176
  26.5 9.4 %collective-permute-start.10 = (bf16[2,256,256]{2,1,0:T(8,128)(2,1)S(1)}, bf16[2,256,256]{2,1,0:T(8,128)(2,1)S(1)}, u32[]{:S(2)}, u32[]{:S(2)}) collective-permute-start(bf16[2,256,256]{2,1,0:T(8,128)(2,1)S(1)} %shard_map.42.rhs), channel_id=1, source_target_pairs={{1,4},{3,6},{4,1},{5,8},{6,3},{7,10},{8,5},{9,12},{10,7},{11,14},{... | collective-permute-start | bytes 786440 | tf_op jit(solution)/shard_map/ppermute | solution.py:176
  28.5 7.4 %collective-permute-start.9 = (bf16[2,256,256]{2,1,0:T(8,128)(2,1)S(1)}, bf16[2,256,256]{2,1,0:T(8,128)(2,1)S(1)}, u32[]{:S(2)}, u32[]{:S(2)}) collective-permute-start(bf16[2,256,256]{2,1,0:T(8,128)(2,1)S(1)} %shard_map.42.rhs), channel_id=1, source_target_pairs={{0,1},{1,0},{2,3},{3,2},{4,5},{5,4},{6,7},{7,6},{8,9},{9,8},{10,11... | collective-permute-start | bytes 786440 | tf_op jit(solution)/shard_map/ppermute | solution.py:176
  32.4 9.0 %collective-permute-start.6 = (bf16[2,256,256]{2,1,0:T(8,128)(2,1)S(1)}, bf16[2,256,256]{2,1,0:T(8,128)(2,1)S(1)}, u32[]{:S(2)}, u32[]{:S(2)}) collective-permute-start(bf16[2,256,256]{2,1,0:T(8,128)(2,1)S(1)} %get-tuple-element.13.pairing), channel_id=1, source_target_pairs={{0,4},{1,5},{2,6},{3,7},{4,0},{5,1},{6,2},{7,3},{8,12},{9,13},{10,... | collective-permute-start | bytes 786440 | tf_op jit(solution)/shard_map/ppermute | solution.py:176
  34.0 11.1 %collective-permute-start.7 = (bf16[2,256,256]{2,1,0:T(8,128)(2,1)S(1)}, bf16[2,256,256]{2,1,0:T(8,128)(2,1)S(1)}, u32[]{:S(2)}, u32[]{:S(2)}) collective-permute-start(bf16[2,256,256]{2,1,0:T(8,128)(2,1)S(1)} %get-tuple-element.14.joining), channel_id=1, source_target_pairs={{4,8},{5,9},{6,10},{7,11},{8,4},{9,5},{10,6},{11,7},{20,24},{21,25... | collective-permute-start | bytes 786440 | tf_op jit(solution)/shard_map/ppermute | solution.py:176
  36.9 9.9 %collective-permute-start.12 = (bf16[2,256,128]{2,1,0:T(8,128)(2,1)S(1)}, bf16[2,256,128]{2,1,0:T(8,128)(2,1)S(1)}, u32[]{:S(2)}, u32[]{:S(2)}) collective-permute-start(bf16[2,256,128]{2,1,0:T(8,128)(2,1)S(1)} %get-tuple-element.17.rhs), channel_id=1, source_target_pairs={{0,4},{1,5},{2,6},{3,7},{4,0},{5,1},{6,2},{7,3},{8,12},{9,13},{10,... | collective-permute-start | bytes 393224 | tf_op jit(solution)/shard_map/ppermute | solution.py:176
  36.9 9.9 %collective-permute-start.11 = (bf16[2,256,128]{2,1,0:T(8,128)(2,1)S(1)}, bf16[2,256,128]{2,1,0:T(8,128)(2,1)S(1)}, u32[]{:S(2)}, u32[]{:S(2)}) collective-permute-start(bf16[2,256,128]{2,1,0:T(8,128)(2,1)S(1)} %get-tuple-element.17.rhs), channel_id=1, source_target_pairs={{4,8},{5,9},{6,10},{7,11},{8,4},{9,5},{10,6},{11,7},{20,24},{21,25... | collective-permute-start | bytes 393224 | tf_op jit(solution)/shard_map/ppermute | solution.py:176
  40.9 6.7 %collective-permute-start.15 = (bf16[2,256,128]{2,1,0:T(8,128)(2,1)S(1)}, bf16[2,256,128]{2,1,0:T(8,128)(2,1)S(1)}, u32[]{:S(2)}, u32[]{:S(2)}) collective-permute-start(bf16[2,256,128]{2,1,0:T(8,128)(2,1)S(1)} %get-tuple-element.18.rhs), channel_id=1, source_target_pairs={{0,4},{1,5},{2,6},{3,7},{4,0},{5,1},{6,2},{7,3},{8,12},{9,13},{10,... | collective-permute-start | bytes 393224 | tf_op jit(solution)/shard_map/ppermute | solution.py:176
  41.4 7.9 %collective-permute-start.14 = (bf16[2,256,128]{2,1,0:T(8,128)(2,1)S(1)}, bf16[2,256,128]{2,1,0:T(8,128)(2,1)S(1)}, u32[]{:S(2)}, u32[]{:S(2)}) collective-permute-start(bf16[2,256,128]{2,1,0:T(8,128)(2,1)S(1)} %get-tuple-element.18.rhs), channel_id=1, source_target_pairs={{4,8},{5,9},{6,10},{7,11},{8,4},{9,5},{10,6},{11,7},{20,24},{21,25... | collective-permute-start | bytes 393224 | tf_op jit(solution)/shard_map/ppermute | solution.py:176
  47.5 5.0 %collective-permute-start.13 = (bf16[2,256,128]{2,1,0:T(8,128)(2,1)S(1)}, bf16[2,256,128]{2,1,0:T(8,128)(2,1)S(1)}, u32[]{:S(2)}, u32[]{:S(2)}) collective-permute-start(bf16[2,256,128]{2,1,0:T(8,128)(2,1)S(1)} %shard_map.44), channel_id=1, source_target_pairs={{0,1},{1,3},{2,0},{3,2},{4,5},{5,7},{6,4},{7,6},{8,9},{9,11},{10,8... | collective-permute-start | bytes 393224 | tf_op jit(solution)/shard_map/ppermute | solution.py:176
  50.0 5.0 %collective-permute-start.16 = (bf16[2,256,128]{2,1,0:T(8,128)(2,1)S(1)}, bf16[2,256,128]{2,1,0:T(8,128)(2,1)S(1)}, u32[]{:S(2)}, u32[]{:S(2)}) collective-permute-start(bf16[2,256,128]{2,1,0:T(8,128)(2,1)S(1)} %shard_map.45), channel_id=1, source_target_pairs={{0,1},{1,3},{2,0},{3,2},{4,5},{5,7},{6,4},{7,6},{8,9},{9,11},{10,8... | collective-permute-start | bytes 393224 | tf_op jit(solution)/shard_map/ppermute | solution.py:176

commit v9 on v8

--- a/solution.py
+++ b/solution.py
@@ -144,22 +144,43 @@
     right[...] = new[:, :, half:]
 
 
-def last_couplings_kernel(pairing, joining, paired, joined, spread):
+def last_couplings_kernel(
+    pairing, joining, paired, joined, left, right, pair_lead, joint_lead, base_left, base_right
+):
+    order = pair_lead.shape[1]
+    half = left.shape[2]
     coupling = product(wide(pairing), tall(paired[...]))
     coupling = coupling + product(wide(joining), tall(joined[...]))
-    spread[...] = parts(inverse_less_one(coupling))
-
-
-def last_injections_kernel(pairing, joining, spread, rhs, joined, paired, new):
-    raw = tall(rhs[...]).astype(jnp.float32) - product(wide(pairing), tall(paired[...]))
-    raw = raw - product(wide(joining), tall(joined[...]))
-    new[...] = parts(solved(spread[...], raw))
+    own = beside(tall(pairing[...]), tall(joining[...]), tall(left[...]), tall(right[...]))
+    spread = wide(parts(inverse_less_one(coupling)))
+    ready = own.astype(jnp.float32) + product(spread, own)
+    pair_lead[...] = parts(low(ready[:, :order]))
+    joint_lead[...] = parts(low(ready[:, order : 2 * order]))
+    base_left[...] = parts(ready[:, 2 * order : 2 * order + half])
+    base_right[...] = parts(ready[:, 2 * order + half :])
+
+
+def last_injections_kernel(pair_lead, joint_lead, base, joined, paired, new):
+    raw = tall(base[...]) - product(wide(pair_lead), tall(paired[...]))
+    new[...] = parts(low(raw - product(wide(joint_lead), tall(joined[...]))))
+
+
+def place_kernel(first, part, *refs):
+    whole, sem = refs[-2:]
+    copy = pltpu.make_async_copy(
+        part, whole.at[0, :, :, pl.ds(first, part.shape[2])], sem
+    )
+    copy.start()
+    copy.wait()
 
 
 def run(kernel, outs, *operands, weight=1):
     return pl.pallas_call(
         kernel,
-        out_shape=[jax.ShapeDtypeStruct(s, jnp.bfloat16) for s in outs],
+        out_shape=[
+            jax.ShapeDtypeStruct(*o) if isinstance(o[0], tuple) else jax.ShapeDtypeStruct(o, jnp.bfloat16)
+            for o in outs
+        ],
         in_specs=[pl.BlockSpec(memory_space=pltpu.VMEM)] * len(operands),
         out_specs=[pl.BlockSpec(memory_space=pltpu.VMEM)] * len(outs),
         compiler_params=pltpu.CompilerParams(vmem_limit_bytes=24 * 1024 * 1024),
@@ -227,16 +248,30 @@
     )
     joined, paired = trade(joining, at_joint), trade(pairing, in_pair)
     arrived = [(trade(half, in_pair), trade(half, at_joint)) for half in halves]
-    (spread,) = run(last_couplings_kernel, (block,), pairing, joining, paired, joined)
+    pair_lead, joint_lead, *bases = run(
+        last_couplings_kernel, (block,) * 2 + ((half_block, jnp.float32),) * 2,
+        pairing, joining, paired, joined, *halves,
+    )
     results = []
-    for half, (paired_half, joined_half), weight in zip(halves, arrived, (1, 1)):
+    for base, (paired_half, joined_half) in zip(bases, arrived):
         (result,) = run(
             last_injections_kernel, (half_block,),
-            pairing, joining, spread, half, joined_half, paired_half,
-            weight=weight,
+            pair_lead, joint_lead, base, joined_half, paired_half,
         )
         results.append(move(result, *home))
-    return jnp.concatenate(results, axis=-1)[None]
+    whole = ()
+    for place, result in enumerate(results):
+        whole = pl.pallas_call(
+            functools.partial(place_kernel, place * half_block[2]),
+            out_shape=[jax.ShapeDtypeStruct((1,) + block, jnp.bfloat16)],
+            in_specs=[pl.BlockSpec(memory_space=pltpu.VMEM)]
+            + [pl.BlockSpec(memory_space=pltpu.HBM)] * len(whole),
+            out_specs=[pl.BlockSpec(memory_space=pltpu.HBM)],
+            scratch_shapes=[pltpu.SemaphoreType.DMA],
+            input_output_aliases={1: 0} if whole else {},
+            compiler_params=pltpu.CompilerParams(vmem_limit_bytes=4 * 1024 * 1024),
+        )(result, *whole)
+    return whole[0]
 
 
 def solution(mesh):

time: 56.1 us -> 55.7 us (level)
  Pallas kernels: 9.04 us -> 10.3 us
  waiting for transfers between devices: 18.5 us -> 17.6 us
  other arithmetic: 0.73 us -> 0 us
    pallas_call x9 -> x11, Pallas kernels: 9.04 us -> 10.3 us  [the longest x9 8.93 us: run(): pl.pallas_call(kernel, out_shape=[jax.ShapeDtypeStruct(*o) if isinstance(...]
    ppermute x17, waiting for transfers between devices: 18.5 us -> 17.6 us  [trade(): lax.ppermute(value, 'chain', [(a, b) for a, b in pairs if 0 <= a < length...]
    broadcast_in_dim x1 -> x0, other arithmetic: 0.73 us -> none  [local(): return jnp.concatenate(results, axis=-1)[None]]
  transfers between devices with their start and end apart: 17 -> 17, of which waited for: 8 -> 8; matrix products, arithmetic and copies ran while one was open for 0% -> 0% of each run, Pallas kernels for 16% -> 17%
where the time goes in v9:
time: 55.7 us; the launch traced here: 55.4 us
  starting transfers between devices  26.3 us (47%)
  waiting for transfers between devices  17.6 us (32%)
  Pallas kernels  10.3 us (18%)
  local copies, waits for them, and re-layouts  1.05 us (2%)
    ppermute x17, starting transfers between devices, trade(): lax.ppermute(value, 'chain', [(a, b) for a, b in pairs if 0 <= a < length...  26.3 us
    ppermute x17, waiting for transfers between devices, trade(): lax.ppermute(value, 'chain', [(a, b) for a, b in pairs if 0 <= a < length...  17.6 us
    pallas_call x9, Pallas kernels, run(): pl.pallas_call(kernel, out_shape=[jax.ShapeDtypeStruct(*o) if isinstance(...  8.93 us
    pallas_call x2, Pallas kernels, local(): pl.pallas_call(functools.partial(place_kernel, place * half_block[2]), ou...  1.33 us
  transfers between devices with their start and end apart: 17, of which 8 were waited for; matrix products, arithmetic and copies ran while one was open for 0% of the time, Pallas kernels for 17%

profile of v9, /device:TPU:18, one launch (start us, length us, event | category | flops | bytes accessed | tf_op | source)
XLA Modules:
  0.0 55.4 jit_solution(3841834746131234597)
XLA Ops:
  0.0 0.0 copy-start.1
  0.0 1.0 %constant_dynamic-update-slice_fusion.1 = bf16[2,2,256,256]{3,2,1,0:T(8,128)(2,1)S(1)} fusion(bf16[1,2,256,256]{3,2,1,0:T(8,128)(2,1)} %param.3), kind=kLoop, calls=%fused_computation.1 | loop fusion | bytes 524288
  1.0 0.0 copy-done.1
  1.0 0.0 copy-start
  1.1 1.6 %collective-permute-start = (bf16[2,2,256,256]{3,2,1,0:T(8,128)(2,1)S(1)}, bf16[2,2,256,256]{3,2,1,0:T(8,128)(2,1)S(1)}, u32[]{:S(2)}, u32[]{:S(2)}) collective-permute-start(bf16[2,2,256,256]{3,2,1,0:T(8,128)(2,1)S(1)} %constant_dynamic-update-slice_fusion.held), channel_id=1, source_target_pairs={{0,2},{1,3},{2,0},{3,1},{4,6},{5,7},{6,4},{7,5},{8,10},{9,11},{10,... | collective-permute-start | bytes 1572872 | tf_op jit(solution)/shard_map/ppermute | solution.py:197
  2.7 0.0 copy-done
  2.7 0.1 shard_map.37.packed
  2.7 1.3 %collective-permute-start.1 = (bf16[3,2,256,256]{3,2,1,0:T(8,128)(2,1)S(1)}, bf16[3,2,256,256]{3,2,1,0:T(8,128)(2,1)S(1)}, u32[]{:S(2)}, u32[]{:S(2)}) collective-permute-start(bf16[3,2,256,256]{3,2,1,0:T(8,128)(2,1)S(1)} %shard_map.37.packed), channel_id=1, source_target_pairs={{1,0},{2,3},{5,4},{6,7},{9,8},{10,11},{13,12},{14,15},{17,16},{18,... | collective-permute-start | bytes 2359304 | tf_op jit(solution)/shard_map/ppermute | solution.py:197
  4.0 3.2 %collective-permute-start.3 = (bf16[3,2,256,256]{3,2,1,0:T(8,128)(2,1)S(1)}, bf16[3,2,256,256]{3,2,1,0:T(8,128)(2,1)S(1)}, u32[]{:S(2)}, u32[]{:S(2)}) collective-permute-start(bf16[3,2,256,256]{3,2,1,0:T(8,128)(2,1)S(1)} %shard_map.37.packed), channel_id=1, source_target_pairs={{3,6},{4,1},{7,10},{8,5},{11,14},{12,9},{19,22},{20,17},{23,26},{2... | collective-permute-start | bytes 2359304 | tf_op jit(solution)/shard_map/ppermute | solution.py:197
  7.2 7.6 %collective-permute-done.crossed = bf16[2,2,256,256]{3,2,1,0:T(8,128)(2,1)S(1)} collective-permute-done((bf16[2,2,256,256]{3,2,1,0:T(8,128)(2,1)S(1)}, bf16[2,2,256,256]{3,2,1,0:T(8,128)(2,1)S(1)}, u32[]{:S(2)}, u32[]{:S(2)}) %collective-permute-start) | collective-permute-done | bytes 524320 | tf_op jit(solution)/shard_map/ppermute | solution.py:197
  14.8 1.3 %collective-permute-start.2 = (bf16[2,2,256,256]{3,2,1,0:T(8,128)(2,1)S(1)}, bf16[2,2,256,256]{3,2,1,0:T(8,128)(2,1)S(1)}, u32[]{:S(2)}, u32[]{:S(2)}) collective-permute-start(bf16[2,2,256,256]{3,2,1,0:T(8,128)(2,1)S(1)} %collective-permute-done.crossed), channel_id=1, source_target_pairs={{0,1},{3,2},{4,5},{7,6},{8,9},{11,10},{12,13},{15,14},{16,17},{19,... | collective-permute-start | bytes 1572872 | tf_op jit(solution)/shard_map/ppermute | solution.py:197
  16.1 0.0 collective-permute-done.1.core
  16.1 0.3 shard_map.40
  16.4 1.6 %collective-permute-start.8 = (bf16[2,256,256]{2,1,0:T(8,128)(2,1)S(1)}, bf16[2,256,256]{2,1,0:T(8,128)(2,1)S(1)}, u32[]{:S(2)}, u32[]{:S(2)}) collective-permute-start(bf16[2,256,256]{2,1,0:T(8,128)(2,1)S(1)} %shard_map.40), channel_id=1, source_target_pairs={{0,2},{1,3},{2,0},{3,1},{4,6},{5,7},{6,4},{7,5},{8,10},{9,11},{10,... | collective-permute-start | bytes 786440 | tf_op jit(solution)/shard_map/ppermute | solution.py:197
  18.0 0.0 collective-permute-done.3.level
  18.0 0.0 collective-permute-done.2.onward
  18.0 1.9 %shard_map.38 = (bf16[2,2,256,256]{3,2,1,0:T(8,128)(2,1)S(1)}, bf16[2,256,256]{2,1,0:T(8,128)(2,1)S(1)}) custom-call(bf16[2,2,256,256]{3,2,1,0:T(8,128)(2,1)S(1)} %constant_dynamic-update-slice_fusion.held, bf16[2,2,256,256]{3,2,1,0:T(8,128)(2,1)S(1)} %collective-permute-done.crossed, bf16[3,2,256,256]{3,2,1,0:T(8,128)(2,1)S(1)} %collective-permute-done.1.core, ...), custom_call_target="tpu_custom_call" | custom-call | flops 1 | bytes 1 | tf_op jit(solution)/shard_map/pallas_call | solution.py:178
  19.9 2.8 %collective-permute-start.5 = (bf16[2,2,256,256]{3,2,1,0:T(8,128)(2,1)S(1)}, bf16[2,2,256,256]{3,2,1,0:T(8,128)(2,1)S(1)}, u32[]{:S(2)}, u32[]{:S(2)}) collective-permute-start(bf16[2,2,256,256]{3,2,1,0:T(8,128)(2,1)S(1)} %get-tuple-element.16.held), channel_id=1, source_target_pairs={{1,4},{3,6},{4,1},{5,8},{6,3},{7,10},{8,5},{9,12},{10,7},{11,14},{... | collective-permute-start | bytes 1572872 | tf_op jit(solution)/shard_map/ppermute | solution.py:197
  22.8 0.8 %collective-permute-start.4 = (bf16[2,2,256,256]{3,2,1,0:T(8,128)(2,1)S(1)}, bf16[2,2,256,256]{3,2,1,0:T(8,128)(2,1)S(1)}, u32[]{:S(2)}, u32[]{:S(2)}) collective-permute-start(bf16[2,2,256,256]{3,2,1,0:T(8,128)(2,1)S(1)} %get-tuple-element.16.held), channel_id=1, source_target_pairs={{0,1},{1,0},{2,3},{3,2},{4,5},{5,4},{6,7},{7,6},{8,9},{9,8},{10,11... | collective-permute-start | bytes 1572872 | tf_op jit(solution)/shard_map/ppermute | solution.py:197
  23.6 2.0 %collective-permute-done.8.crossed_rhs = bf16[2,256,256]{2,1,0:T(8,128)(2,1)S(1)} collective-permute-done((bf16[2,256,256]{2,1,0:T(8,128)(2,1)S(1)}, bf16[2,256,256]{2,1,0:T(8,128)(2,1)S(1)}, u32[]{:S(2)}, u32[]{:S(2)}) %collective-permute-start.8) | collective-permute-done | bytes 262176 | tf_op jit(solution)/shard_map/ppermute | solution.py:197
  25.6 0.9 %shard_map.41.rhs = bf16[2,256,256]{2,1,0:T(8,128)(2,1)S(1)} custom-call(bf16[2,2,256,256]{3,2,1,0:T(8,128)(2,1)S(1)} %collective-permute-done.crossed, bf16[2,256,256]{2,1,0:T(8,128)(2,1)S(1)} %get-tuple-element.20.spread, bf16[2,256,256]{2,1,0:T(8,128)(2,1)S(1)} %bitcast.2, bf16[2,256,256]{2,1,0:T(8,128)(2,1)S(1)} %collective-permute-done.8.crossed_rhs, ...), custom_call_target="tpu_custom_call" | custom-call | flops 99999997952 | bytes 1 | tf_op jit(solution)/shard_map/pallas_call | solution.py:178
  26.5 2.0 %collective-permute-start.10 = (bf16[2,256,256]{2,1,0:T(8,128)(2,1)S(1)}, bf16[2,256,256]{2,1,0:T(8,128)(2,1)S(1)}, u32[]{:S(2)}, u32[]{:S(2)}) collective-permute-start(bf16[2,256,256]{2,1,0:T(8,128)(2,1)S(1)} %shard_map.41.rhs), channel_id=1, source_target_pairs={{1,4},{3,6},{4,1},{5,8},{6,3},{7,10},{8,5},{9,12},{10,7},{11,14},{... | collective-permute-start | bytes 786440 | tf_op jit(solution)/shard_map/ppermute | solution.py:197
  28.5 1.7 %collective-permute-start.9 = (bf16[2,256,256]{2,1,0:T(8,128)(2,1)S(1)}, bf16[2,256,256]{2,1,0:T(8,128)(2,1)S(1)}, u32[]{:S(2)}, u32[]{:S(2)}) collective-permute-start(bf16[2,256,256]{2,1,0:T(8,128)(2,1)S(1)} %shard_map.41.rhs), channel_id=1, source_target_pairs={{0,1},{1,0},{2,3},{3,2},{4,5},{5,4},{6,7},{7,6},{8,9},{9,8},{10,11... | collective-permute-start | bytes 786440 | tf_op jit(solution)/shard_map/ppermute | solution.py:197
  30.2 0.2 collective-permute-done.5.level
  30.4 0.0 collective-permute-done.4.core
  30.4 1.9 %shard_map.39 = (bf16[2,256,256]{2,1,0:T(8,128)(2,1)S(1)}, bf16[2,256,256]{2,1,0:T(8,128)(2,1)S(1)}, bf16[2,256,256]{2,1,0:T(8,128)(2,1)S(1)}) custom-call(bf16[2,2,256,256]{3,2,1,0:T(8,128)(2,1)S(1)} %get-tuple-element.16.held, bf16[2,2,256,256]{3,2,1,0:T(8,128)(2,1)S(1)} %collective-permute-done.4.core, ...), custom_call_target="tpu_custom_call" | custom-call | flops 1 | bytes 1 | tf_op jit(solution)/shard_map/pallas_call | solution.py:178
  32.4 1.6 %collective-permute-start.6 = (bf16[2,256,256]{2,1,0:T(8,128)(2,1)S(1)}, bf16[2,256,256]{2,1,0:T(8,128)(2,1)S(1)}, u32[]{:S(2)}, u32[]{:S(2)}) collective-permute-start(bf16[2,256,256]{2,1,0:T(8,128)(2,1)S(1)} %get-tuple-element.17.pairing), channel_id=1, source_target_pairs={{0,4},{1,5},{2,6},{3,7},{4,0},{5,1},{6,2},{7,3},{8,12},{9,13},{10,... | collective-permute-start | bytes 786440 | tf_op jit(solution)/shard_map/ppermute | solution.py:197
  34.0 1.9 %collective-permute-start.7 = (bf16[2,256,256]{2,1,0:T(8,128)(2,1)S(1)}, bf16[2,256,256]{2,1,0:T(8,128)(2,1)S(1)}, u32[]{:S(2)}, u32[]{:S(2)}) collective-permute-start(bf16[2,256,256]{2,1,0:T(8,128)(2,1)S(1)} %get-tuple-element.18.joining), channel_id=1, source_target_pairs={{4,8},{5,9},{6,10},{7,11},{8,4},{9,5},{10,6},{11,7},{20,24},{21,25... | collective-permute-start | bytes 786440 | tf_op jit(solution)/shard_map/ppermute | solution.py:197
  35.9 0.0 collective-permute-done.10.level
  35.9 0.0 collective-permute-done.9.core
  36.0 0.9 %shard_map.42 = (bf16[2,256,128]{2,1,0:T(8,128)(2,1)S(1)}, bf16[2,256,128]{2,1,0:T(8,128)(2,1)S(1)}) custom-call(bf16[2,2,256,256]{3,2,1,0:T(8,128)(2,1)S(1)} %get-tuple-element.16.held, bf16[2,256,256]{2,1,0:T(8,128)(2,1)S(1)} %get-tuple-element.19.spread, bf16[2,256,256]{2,1,0:T(8,128)(2,1)S(1)} %shard_map.41.rhs, ...), custom_call_target="tpu_custom_call" | custom-call | flops 1 | bytes 1 | tf_op jit(solution)/shard_map/pallas_call | solution.py:178
  36.9 0.1 collective-permute-start.15
  36.9 3.9 %collective-permute-start.14 = (bf16[2,256,128]{2,1,0:T(8,128)(2,1)S(1)}, bf16[2,256,128]{2,1,0:T(8,128)(2,1)S(1)}, u32[]{:S(2)}, u32[]{:S(2)}) collective-permute-start(bf16[2,256,128]{2,1,0:T(8,128)(2,1)S(1)} %get-tuple-element.21.left), channel_id=1, source_target_pairs={{4,8},{5,9},{6,10},{7,11},{8,4},{9,5},{10,6},{11,7},{20,24},{21,25... | collective-permute-start | bytes 393224 | tf_op jit(solution)/shard_map/ppermute | solution.py:197
  40.9 0.1 collective-permute-start.12
  40.9 0.5 collective-permute-done.6.paired
  41.4 2.3 %collective-permute-start.11 = (bf16[2,256,128]{2,1,0:T(8,128)(2,1)S(1)}, bf16[2,256,128]{2,1,0:T(8,128)(2,1)S(1)}, u32[]{:S(2)}, u32[]{:S(2)}) collective-permute-start(bf16[2,256,128]{2,1,0:T(8,128)(2,1)S(1)} %get-tuple-element.22.right), channel_id=1, source_target_pairs={{4,8},{5,9},{6,10},{7,11},{8,4},{9,5},{10,6},{11,7},{20,24},{21,25... | collective-permute-start | bytes 393224 | tf_op jit(solution)/shard_map/ppermute | solution.py:197
  43.8 1.4 %collective-permute-done.7.joined = bf16[2,256,256]{2,1,0:T(8,128)(2,1)S(1)} collective-permute-done((bf16[2,256,256]{2,1,0:T(8,128)(2,1)S(1)}, bf16[2,256,256]{2,1,0:T(8,128)(2,1)S(1)}, u32[]{:S(2)}, u32[]{:S(2)}) %collective-permute-start.7) | collective-permute-done | bytes 262176 | tf_op jit(solution)/shard_map/ppermute | solution.py:197
  45.1 2.1 %shard_map.43 = (bf16[2,256,256]{2,1,0:T(8,128)(2,1)S(1)}, bf16[2,256,256]{2,1,0:T(8,128)(2,1)S(1)}, f32[2,256,128]{2,1,0:T(8,128)S(1)}, f32[2,256,128]{2,1,0:T(8,128)S(1)}) custom-call(bf16[2,256,256]{2,1,0:T(8,128)(2,1)S(1)} %get-tuple-element.17.pairing, bf16[2,256,256]{2,1,0:T(8,128)(2,1)S(1)} %get-tuple-element.18.joining, ...), custom_call_target="tpu_custom_call" | custom-call | flops 1 | bytes 1 | tf_op jit(solution)/shard_map/pallas_call | solution.py:178
  47.2 0.0 collective-permute-done.15.paired
  47.2 0.0 collective-permute-done.14.joined
  47.2 0.4 shard_map.45
  47.7 0.0 collective-permute-start.16
  47.7 0.0 collective-permute-done.12.paired
  47.7 1.7 %collective-permute-done.11.joined = bf16[2,256,128]{2,1,0:T(8,128)(2,1)S(1)} collective-permute-done((bf16[2,256,128]{2,1,0:T(8,128)(2,1)S(1)}, bf16[2,256,128]{2,1,0:T(8,128)(2,1)S(1)}, u32[]{:S(2)}, u32[]{:S(2)}) %collective-permute-start.11) | collective-permute-done | bytes 131104 | tf_op jit(solution)/shard_map/ppermute | solution.py:197
  49.3 0.4 shard_map.44
  49.8 0.0 collective-permute-start.13
  49.8 2.8 %collective-permute-done.16.part = bf16[2,256,128]{2,1,0:T(8,128)(2,1)S(1)} collective-permute-done((bf16[2,256,128]{2,1,0:T(8,128)(2,1)S(1)}, bf16[2,256,128]{2,1,0:T(8,128)(2,1)S(1)}, u32[]{:S(2)}, u32[]{:S(2)}) %collective-permute-start.16) | collective-permute-done | bytes 131104 | tf_op jit(solution)/shard_map/ppermute | solution.py:197
  52.6 0.7 %shard_map.46.refs_0_ = bf16[1,2,256,256]{3,2,1,0:T(8,128)(2,1)} custom-call(bf16[2,256,128]{2,1,0:T(8,128)(2,1)S(1)} %collective-permute-done.16.part), custom_call_target="tpu_custom_call" | custom-call | tf_op jit(solution)/shard_map/pallas_call | solution.py:264
  53.3 1.5 %collective-permute-done.13.part = bf16[2,256,128]{2,1,0:T(8,128)(2,1)S(1)} collective-permute-done((bf16[2,256,128]{2,1,0:T(8,128)(2,1)S(1)}, bf16[2,256,128]{2,1,0:T(8,128)(2,1)S(1)}, u32[]{:S(2)}, u32[]{:S(2)}) %collective-permute-start.13) | collective-permute-done | bytes 131104 | tf_op jit(solution)/shard_map/ppermute | solution.py:197
  54.8 0.7 %shard_map.47 = bf16[1,2,256,256]{3,2,1,0:T(8,128)(2,1)} custom-call(bf16[2,256,128]{2,1,0:T(8,128)(2,1)S(1)} %collective-permute-done.13.part, bf16[1,2,256,256]{3,2,1,0:T(8,128)(2,1)} %shard_map.46.refs_0_), custom_call_target="tpu_custom_call", output_to_operand_aliasing={{}: (1, {})} | custom-call | tf_op jit(solution)/shard_map/pallas_call | solution.py:264
  (1 shorter events, 0.0 us)
Async XLA Ops:
  0.0 1.0 %copy-start.1 = (bf16[1,2,256,256]{3,2,1,0:T(8,128)(2,1)S(1)}, bf16[1,2,256,256]{3,2,1,0:T(8,128)(2,1)}, u32[]{:S(2)}) copy-start(bf16[1,2,256,256]{3,2,1,0:T(8,128)(2,1)} %param.4) | copy-start | bytes 786436
  1.0 1.6 %copy-start = (bf16[1,2,256,256]{3,2,1,0:T(8,128)(2,1)S(1)}, bf16[1,2,256,256]{3,2,1,0:T(8,128)(2,1)}, u32[]{:S(2)}) copy-start(bf16[1,2,256,256]{3,2,1,0:T(8,128)(2,1)} %param.5) | copy-start | bytes 786436
  1.1 13.7 %collective-permute-start = (bf16[2,2,256,256]{3,2,1,0:T(8,128)(2,1)S(1)}, bf16[2,2,256,256]{3,2,1,0:T(8,128)(2,1)S(1)}, u32[]{:S(2)}, u32[]{:S(2)}) collective-permute-start(bf16[2,2,256,256]{3,2,1,0:T(8,128)(2,1)S(1)} %constant_dynamic-update-slice_fusion.held), channel_id=1, source_target_pairs={{0,2},{1,3},{2,0},{3,1},{4,6},{5,7},{6,4},{7,5},{8,10},{9,11},{10,... | collective-permute-start | bytes 1572872 | tf_op jit(solution)/shard_map/ppermute | solution.py:197
  2.7 13.4 %collective-permute-start.1 = (bf16[3,2,256,256]{3,2,1,0:T(8,128)(2,1)S(1)}, bf16[3,2,256,256]{3,2,1,0:T(8,128)(2,1)S(1)}, u32[]{:S(2)}, u32[]{:S(2)}) collective-permute-start(bf16[3,2,256,256]{3,2,1,0:T(8,128)(2,1)S(1)} %shard_map.37.packed), channel_id=1, source_target_pairs={{1,0},{2,3},{5,4},{6,7},{9,8},{10,11},{13,12},{14,15},{17,16},{18,... | collective-permute-start | bytes 2359304 | tf_op jit(solution)/shard_map/ppermute | solution.py:197
  4.0 14.0 %collective-permute-start.3 = (bf16[3,2,256,256]{3,2,1,0:T(8,128)(2,1)S(1)}, bf16[3,2,256,256]{3,2,1,0:T(8,128)(2,1)S(1)}, u32[]{:S(2)}, u32[]{:S(2)}) collective-permute-start(bf16[3,2,256,256]{3,2,1,0:T(8,128)(2,1)S(1)} %shard_map.37.packed), channel_id=1, source_target_pairs={{3,6},{4,1},{7,10},{8,5},{11,14},{12,9},{19,22},{20,17},{23,26},{2... | collective-permute-start | bytes 2359304 | tf_op jit(solution)/shard_map/ppermute | solution.py:197
  14.8 3.2 %collective-permute-start.2 = (bf16[2,2,256,256]{3,2,1,0:T(8,128)(2,1)S(1)}, bf16[2,2,256,256]{3,2,1,0:T(8,128)(2,1)S(1)}, u32[]{:S(2)}, u32[]{:S(2)}) collective-permute-start(bf16[2,2,256,256]{3,2,1,0:T(8,128)(2,1)S(1)} %collective-permute-done.crossed), channel_id=1, source_target_pairs={{0,1},{3,2},{4,5},{7,6},{8,9},{11,10},{12,13},{15,14},{16,17},{19,... | collective-permute-start | bytes 1572872 | tf_op jit(solution)/shard_map/ppermute | solution.py:197
  16.4 9.2 %collective-permute-start.8 = (bf16[2,256,256]{2,1,0:T(8,128)(2,1)S(1)}, bf16[2,256,256]{2,1,0:T(8,128)(2,1)S(1)}, u32[]{:S(2)}, u32[]{:S(2)}) collective-permute-start(bf16[2,256,256]{2,1,0:T(8,128)(2,1)S(1)} %shard_map.40), channel_id=1, source_target_pairs={{0,2},{1,3},{2,0},{3,1},{4,6},{5,7},{6,4},{7,5},{8,10},{9,11},{10,... | collective-permute-start | bytes 786440 | tf_op jit(solution)/shard_map/ppermute | solution.py:197
  19.9 10.5 %collective-permute-start.5 = (bf16[2,2,256,256]{3,2,1,0:T(8,128)(2,1)S(1)}, bf16[2,2,256,256]{3,2,1,0:T(8,128)(2,1)S(1)}, u32[]{:S(2)}, u32[]{:S(2)}) collective-permute-start(bf16[2,2,256,256]{3,2,1,0:T(8,128)(2,1)S(1)} %get-tuple-element.16.held), channel_id=1, source_target_pairs={{1,4},{3,6},{4,1},{5,8},{6,3},{7,10},{8,5},{9,12},{10,7},{11,14},{... | collective-permute-start | bytes 1572872 | tf_op jit(solution)/shard_map/ppermute | solution.py:197
  22.8 7.7 %collective-permute-start.4 = (bf16[2,2,256,256]{3,2,1,0:T(8,128)(2,1)S(1)}, bf16[2,2,256,256]{3,2,1,0:T(8,128)(2,1)S(1)}, u32[]{:S(2)}, u32[]{:S(2)}) collective-permute-start(bf16[2,2,256,256]{3,2,1,0:T(8,128)(2,1)S(1)} %get-tuple-element.16.held), channel_id=1, source_target_pairs={{0,1},{1,0},{2,3},{3,2},{4,5},{5,4},{6,7},{7,6},{8,9},{9,8},{10,11... | collective-permute-start | bytes 1572872 | tf_op jit(solution)/shard_map/ppermute | solution.py:197
  26.5 9.4 %collective-permute-start.10 = (bf16[2,256,256]{2,1,0:T(8,128)(2,1)S(1)}, bf16[2,256,256]{2,1,0:T(8,128)(2,1)S(1)}, u32[]{:S(2)}, u32[]{:S(2)}) collective-permute-start(bf16[2,256,256]{2,1,0:T(8,128)(2,1)S(1)} %shard_map.41.rhs), channel_id=1, source_target_pairs={{1,4},{3,6},{4,1},{5,8},{6,3},{7,10},{8,5},{9,12},{10,7},{11,14},{... | collective-permute-start | bytes 786440 | tf_op jit(solution)/shard_map/ppermute | solution.py:197
  28.5 7.4 %collective-permute-start.9 = (bf16[2,256,256]{2,1,0:T(8,128)(2,1)S(1)}, bf16[2,256,256]{2,1,0:T(8,128)(2,1)S(1)}, u32[]{:S(2)}, u32[]{:S(2)}) collective-permute-start(bf16[2,256,256]{2,1,0:T(8,128)(2,1)S(1)} %shard_map.41.rhs), channel_id=1, source_target_pairs={{0,1},{1,0},{2,3},{3,2},{4,5},{5,4},{6,7},{7,6},{8,9},{9,8},{10,11... | collective-permute-start | bytes 786440 | tf_op jit(solution)/shard_map/ppermute | solution.py:197
  32.4 9.0 %collective-permute-start.6 = (bf16[2,256,256]{2,1,0:T(8,128)(2,1)S(1)}, bf16[2,256,256]{2,1,0:T(8,128)(2,1)S(1)}, u32[]{:S(2)}, u32[]{:S(2)}) collective-permute-start(bf16[2,256,256]{2,1,0:T(8,128)(2,1)S(1)} %get-tuple-element.17.pairing), channel_id=1, source_target_pairs={{0,4},{1,5},{2,6},{3,7},{4,0},{5,1},{6,2},{7,3},{8,12},{9,13},{10,... | collective-permute-start | bytes 786440 | tf_op jit(solution)/shard_map/ppermute | solution.py:197
  34.0 11.1 %collective-permute-start.7 = (bf16[2,256,256]{2,1,0:T(8,128)(2,1)S(1)}, bf16[2,256,256]{2,1,0:T(8,128)(2,1)S(1)}, u32[]{:S(2)}, u32[]{:S(2)}) collective-permute-start(bf16[2,256,256]{2,1,0:T(8,128)(2,1)S(1)} %get-tuple-element.18.joining), channel_id=1, source_target_pairs={{4,8},{5,9},{6,10},{7,11},{8,4},{9,5},{10,6},{11,7},{20,24},{21,25... | collective-permute-start | bytes 786440 | tf_op jit(solution)/shard_map/ppermute | solution.py:197
  36.9 10.3 %collective-permute-start.15 = (bf16[2,256,128]{2,1,0:T(8,128)(2,1)S(1)}, bf16[2,256,128]{2,1,0:T(8,128)(2,1)S(1)}, u32[]{:S(2)}, u32[]{:S(2)}) collective-permute-start(bf16[2,256,128]{2,1,0:T(8,128)(2,1)S(1)} %get-tuple-element.21.left), channel_id=1, source_target_pairs={{0,4},{1,5},{2,6},{3,7},{4,0},{5,1},{6,2},{7,3},{8,12},{9,13},{10,... | collective-permute-start | bytes 393224 | tf_op jit(solution)/shard_map/ppermute | solution.py:197
  36.9 10.3 %collective-permute-start.14 = (bf16[2,256,128]{2,1,0:T(8,128)(2,1)S(1)}, bf16[2,256,128]{2,1,0:T(8,128)(2,1)S(1)}, u32[]{:S(2)}, u32[]{:S(2)}) collective-permute-start(bf16[2,256,128]{2,1,0:T(8,128)(2,1)S(1)} %get-tuple-element.21.left), channel_id=1, source_target_pairs={{4,8},{5,9},{6,10},{7,11},{8,4},{9,5},{10,6},{11,7},{20,24},{21,25... | collective-permute-start | bytes 393224 | tf_op jit(solution)/shard_map/ppermute | solution.py:197
  40.9 6.8 %collective-permute-start.12 = (bf16[2,256,128]{2,1,0:T(8,128)(2,1)S(1)}, bf16[2,256,128]{2,1,0:T(8,128)(2,1)S(1)}, u32[]{:S(2)}, u32[]{:S(2)}) collective-permute-start(bf16[2,256,128]{2,1,0:T(8,128)(2,1)S(1)} %get-tuple-element.22.right), channel_id=1, source_target_pairs={{0,4},{1,5},{2,6},{3,7},{4,0},{5,1},{6,2},{7,3},{8,12},{9,13},{10,... | collective-permute-start | bytes 393224 | tf_op jit(solution)/shard_map/ppermute | solution.py:197
  41.4 7.9 %collective-permute-start.11 = (bf16[2,256,128]{2,1,0:T(8,128)(2,1)S(1)}, bf16[2,256,128]{2,1,0:T(8,128)(2,1)S(1)}, u32[]{:S(2)}, u32[]{:S(2)}) collective-permute-start(bf16[2,256,128]{2,1,0:T(8,128)(2,1)S(1)} %get-tuple-element.22.right), channel_id=1, source_target_pairs={{4,8},{5,9},{6,10},{7,11},{8,4},{9,5},{10,6},{11,7},{20,24},{21,25... | collective-permute-start | bytes 393224 | tf_op jit(solution)/shard_map/ppermute | solution.py:197
  47.7 5.0 %collective-permute-start.16 = (bf16[2,256,128]{2,1,0:T(8,128)(2,1)S(1)}, bf16[2,256,128]{2,1,0:T(8,128)(2,1)S(1)}, u32[]{:S(2)}, u32[]{:S(2)}) collective-permute-start(bf16[2,256,128]{2,1,0:T(8,128)(2,1)S(1)} %shard_map.45), channel_id=1, source_target_pairs={{0,1},{1,3},{2,0},{3,2},{4,5},{5,7},{6,4},{7,6},{8,9},{9,11},{10,8... | collective-permute-start | bytes 393224 | tf_op jit(solution)/shard_map/ppermute | solution.py:197
  49.8 5.0 %collective-permute-start.13 = (bf16[2,256,128]{2,1,0:T(8,128)(2,1)S(1)}, bf16[2,256,128]{2,1,0:T(8,128)(2,1)S(1)}, u32[]{:S(2)}, u32[]{:S(2)}) collective-permute-start(bf16[2,256,128]{2,1,0:T(8,128)(2,1)S(1)} %shard_map.44), channel_id=1, source_target_pairs={{0,1},{1,3},{2,0},{3,2},{4,5},{5,7},{6,4},{7,6},{8,9},{9,11},{10,8... | collective-permute-start | bytes 393224 | tf_op jit(solution)/shard_map/ppermute | solution.py:197
